TPU v7x, 32 devices: a whole 2x2x4 slice. The times are simulated.
32 devices in a mesh: dp: 8 (over z, x), tensor: 4 (over y, core).
Axes of the slice: x: 2, y: 2, z: 4, core: 2. Of those that a mesh axis runs over, the one named last changes fastest.
Arguments:
- block_input: bfloat16 [64, 512, 768], P('dp', 'tensor'), may hold values from -6 to 6
- cotangent: bfloat16 [64, 512, 768], P('dp', 'tensor'), may hold values from -6 to 6
- segment_ids: int32 [64, 512], P('dp'), may hold values from 0 to 7, as said below
- rel_bucket: int32 [1023], replicated, may hold values from 0 to 31, as said below
- expert_route: int32 [64, 512], P('dp', 'tensor'), may hold values from 0 to 7
- expert_slot: int32 [64, 512], P('dp', 'tensor'), may hold values from -1 to 239, as said below
- attn_gain: bfloat16 [768], replicated, may hold values from 0.099609375 to 1.8984375
- moe_gain: bfloat16 [768], replicated, may hold values from 0.099609375 to 1.8984375
- router_weight: bfloat16 [768, 8], replicated, may hold values from -0.109375 to 0.109375
- rel_table: bfloat16 [32, 12], replicated, may hold values from -4 to 4
- w_query: bfloat16 [768, 768], P('dp', 'tensor'), may hold values from -0.02734375 to 0.02734375
- w_key: bfloat16 [768, 768], P('dp', 'tensor'), may hold values from -0.21875 to 0.21875
- w_value: bfloat16 [768, 768], P('dp', 'tensor'), may hold values from -0.21875 to 0.21875
- w_out: bfloat16 [768, 768], P('tensor', 'dp'), may hold values from -0.625 to 0.625
- expert_in: bfloat16 [8, 768, 3072], P('dp', None, 'tensor'), may hold values from -0.21875 to 0.21875
- expert_out: bfloat16 [8, 3072, 768], P('dp', 'tensor'), may hold values from -1.75 to 1.75
Outputs:
- block_output: bfloat16 [64, 512, 768], P('dp', 'tensor')
- input_grad: float32 [64, 512, 768], P('dp', 'tensor')
- attn_gain_grad: float32 [768], replicated
- moe_gain_grad: float32 [768], replicated
- router_grad: float32 [768, 8], replicated
- rel_table_grad: float32 [32, 12], replicated
- w_query_grad: float32 [768, 768], P('dp', 'tensor')
- w_key_grad: float32 [768, 768], P('dp', 'tensor')
- w_value_grad: float32 [768, 768], P('dp', 'tensor')
- w_out_grad: float32 [768, 768], P('tensor', 'dp')
- expert_in_grad: float32 [8, 768, 3072], P('dp', None, 'tensor')
- expert_out_grad: float32 [8, 3072, 768], P('dp', 'tensor')
Inputs may be any that keep to these rules, and one draw needn't show every extreme that they name: `segment_ids`: segment numbers start at 0 in each sequence and never fall along it; in every group of 8 sequences of one index of dp one sequence is a single segment. `rel_bucket`: entry j - i + 511 holds the bucket of key j for query i; keys at or before the query use the lower half of the 32 buckets, keys after it the upper half, and buckets never fall as the distance grows. `expert_slot`: within the 1024 tokens of one device (its sequences in order, positions in order within each), a token's slot is the number of earlier tokens of that device routed to the same expert, or -1 once that number reaches 240; in every draw one expert receives 240 tokens from every device.
All inputs are finite; a program needn't handle non-finite values.
Results may differ from a plain program's by a relative error of at most 0.018.
Values may be sent and summed in bfloat16 or wider, within the bound.
No kernel may reach another device: no remote copies, remote signals or barrier semaphores. Data moves between devices by JAX's collectives and lax.ppermute only.
A program may use at most 256 MiB of HBM per device.

v0:
```python
import jax
import jax.numpy as jnp
from jax import lax
from jax.sharding import PartitionSpec as P

EPSILON = 1e-06
MASKED_SCORE = -1e30


def rms_inverse(values):
    return lax.rsqrt(jnp.mean(values * values, axis=-1, keepdims=True) + EPSILON)


def attn_norm(tokens_in, gain):
    return tokens_in * rms_inverse(tokens_in) * gain


def diagonal_spread(line, seq_len):
    heads_count = line.shape[0]
    padded = jnp.pad(line, ((0, 0), (0, 1)))
    tiled = jnp.tile(padded, (1, seq_len))
    window = tiled[:, seq_len - 1 : seq_len - 1 + seq_len * (2 * seq_len - 1)]
    return window.reshape(heads_count, seq_len, 2 * seq_len - 1)[:, :, :seq_len]


def diagonal_sums(square):
    heads_count, seq_len = (square.shape[0], square.shape[1])
    flipped = square[:, ::-1, :]
    padded = jnp.pad(flipped, ((0, 0), (0, 0), (0, seq_len)))
    flat = padded.reshape(heads_count, 2 * seq_len * seq_len)[:, : seq_len * (2 * seq_len - 1)]
    return jnp.sum(flat.reshape(heads_count, seq_len, 2 * seq_len - 1), axis=1)


def scored(queries, key_rows, seg_row, position_bias):
    logits = jnp.einsum("ihc,jhc->hij", queries, key_rows, preferred_element_type=jnp.float32)
    same_doc = seg_row[:, None] == seg_row[None, :]
    return jnp.where(same_doc[None], logits + position_bias, MASKED_SCORE)


def attend_one(packed, position_bias):
    queries, key_rows, value_rows, seg_row = packed
    logits = scored(queries, key_rows, seg_row, position_bias)
    peak_value = jnp.max(logits, axis=-1, keepdims=True)
    expo = jnp.exp(logits - peak_value)
    denominator = jnp.sum(expo, axis=-1, keepdims=True)
    attention_probabilities = (expo / denominator).astype(jnp.bfloat16)
    attended = jnp.einsum(
        "hij,jhc->ihc", attention_probabilities, value_rows, preferred_element_type=jnp.float32
    )
    return (attended.astype(jnp.bfloat16), (peak_value + jnp.log(denominator))[..., 0])


def attend_back(packed, position_bias, bucket_lines):
    queries, key_rows, value_rows, seg_row, log_total, attended_grad = packed
    logits = scored(queries, key_rows, seg_row, position_bias)
    attention_probabilities = jnp.exp(logits - log_total[..., None])
    value_grad = jnp.einsum(
        "hij,ihc->jhc",
        attention_probabilities.astype(jnp.bfloat16),
        attended_grad,
        preferred_element_type=jnp.float32,
    )
    prob_grad = jnp.einsum(
        "ihc,jhc->hij", attended_grad, value_rows, preferred_element_type=jnp.float32
    )
    inner_sum = jnp.sum(attention_probabilities * prob_grad, axis=-1, keepdims=True)
    score_grad = (attention_probabilities * (prob_grad - inner_sum)).astype(jnp.bfloat16)
    query_grad = jnp.einsum(
        "hij,jhc->ihc", score_grad, key_rows, preferred_element_type=jnp.float32
    )
    key_grad = jnp.einsum("hij,ihc->jhc", score_grad, queries, preferred_element_type=jnp.float32)
    offset_sums = diagonal_sums(score_grad.astype(jnp.float32))
    table_grad = jnp.einsum(
        "hk,kb->bh",
        offset_sums,
        bucket_lines,
        precision=lax.Precision.HIGHEST,
        preferred_element_type=jnp.float32,
    )
    seq_len = queries.shape[0]
    stacked = jnp.concatenate(
        [
            query_grad.reshape(seq_len, -1),
            key_grad.reshape(seq_len, -1),
            value_grad.reshape(seq_len, -1),
        ],
        axis=1,
    )
    return (stacked.astype(jnp.bfloat16), table_grad)


def to_experts(buffer):
    return lax.all_to_all(buffer, "dp", split_axis=0, concat_axis=0, tiled=True)


def from_experts(buffer):
    return lax.all_to_all(buffer, "dp", split_axis=0, concat_axis=0, tiled=True)


def group_rows(buffer):
    return lax.all_gather(buffer, "tensor", axis=1, tiled=True)


def group_sums(terms):
    return lax.psum_scatter(terms, "tensor", scatter_dimension=1, tiled=True)


def local(
    block_input,
    cotangent,
    segment_ids,
    rel_bucket,
    expert_route,
    expert_slot,
    attn_gain,
    moe_gain,
    router_weight,
    rel_table,
    w_query,
    w_key,
    w_value,
    w_out,
    expert_in,
    expert_out,
):
    group_seqs, part_len, model_width = block_input.shape
    tensor_size = lax.axis_size("tensor")
    dp_size = lax.axis_size("dp")
    full_len = part_len * tensor_size
    head_cols = w_query.shape[1]
    heads_here = rel_table.shape[1] // tensor_size
    head_size = head_cols // heads_here
    relative_bucket_count = rel_table.shape[0]
    experts_here = expert_in.shape[0]
    experts_all = router_weight.shape[1]
    tok_rows = group_seqs * part_len
    capacity = tok_rows * 15 // (8 * experts_all)
    buffer_size = experts_all * capacity
    query_full, key_full, value_full, complete_output_rows = (
        lax.all_gather(w_query, "dp", axis=0, tiled=True),
        lax.all_gather(w_key, "dp", axis=0, tiled=True),
        lax.all_gather(w_value, "dp", axis=0, tiled=True),
        lax.all_gather(w_out, "dp", axis=1, tiled=True),
    )
    combined_weight_matrix = jnp.concatenate([query_full, key_full, value_full], axis=1)
    flat_input = block_input.astype(jnp.float32)
    attn_gain_f = attn_gain.astype(jnp.float32)
    normed_local = attn_norm(flat_input, attn_gain_f).astype(jnp.bfloat16)
    complete_normalized_rows = lax.all_gather(normed_local, "tensor", axis=1, tiled=True)
    projected = jnp.einsum(
        "unt,tk->unk",
        complete_normalized_rows,
        combined_weight_matrix,
        preferred_element_type=jnp.float32,
    ).astype(jnp.bfloat16)
    query_heads = projected[:, :, :head_cols].reshape(group_seqs, full_len, heads_here, head_size)
    key_heads = projected[:, :, head_cols : 2 * head_cols].reshape(
        group_seqs, full_len, heads_here, head_size
    )
    value_heads = projected[:, :, 2 * head_cols :].reshape(
        group_seqs, full_len, heads_here, head_size
    )
    bucket_lines = (rel_bucket[:, None] == jnp.arange(relative_bucket_count)[None, :]).astype(
        jnp.float32
    )
    head_start = lax.axis_index("tensor") * heads_here
    table_local = lax.dynamic_slice_in_dim(rel_table, head_start, heads_here, 1).astype(jnp.float32)
    bias_line = jnp.einsum(
        "kb,bh->hk",
        bucket_lines,
        table_local,
        precision=lax.Precision.HIGHEST,
        preferred_element_type=jnp.float32,
    )
    position_bias = diagonal_spread(bias_line, full_len)

    def forward_one(packed):
        return attend_one(packed, position_bias)

    attended, log_totals = lax.map(forward_one, (query_heads, key_heads, value_heads, segment_ids))
    attended_token_rows = attended.reshape(group_seqs, full_len, head_cols)
    partial_out = jnp.einsum(
        "inr,rp->inp", attended_token_rows, complete_output_rows, preferred_element_type=jnp.float32
    )
    attn_branch = lax.psum_scatter(partial_out, "tensor", scatter_dimension=1, tiled=True)
    residual = flat_input + attn_branch
    hidden_rows = residual.reshape(tok_rows, model_width)
    route_rows = expert_route.reshape(tok_rows)
    slot_rows = expert_slot.reshape(tok_rows)
    kept_rows = slot_rows >= 0
    slot_place = jnp.where(kept_rows, route_rows * capacity + slot_rows, buffer_size)
    slot_table = (slot_place[:, None] == jnp.arange(buffer_size)[None, :]).astype(jnp.bfloat16)
    route_onehot = (route_rows[:, None] == jnp.arange(experts_all)[None, :]).astype(jnp.float32)

    def place_rows(rows):
        placed = jnp.einsum("tb,td->bd", slot_table, rows, preferred_element_type=jnp.float32)
        return placed.astype(jnp.bfloat16).reshape(experts_all, capacity, model_width)

    def take_rows(buffer):
        return jnp.dot(
            slot_table, buffer.reshape(buffer_size, model_width), preferred_element_type=jnp.float32
        )

    def moe_front(hidden_in, gain, router_full):
        normed = hidden_in * rms_inverse(hidden_in) * gain
        logits = jnp.dot(
            normed, router_full, precision=lax.Precision.HIGHEST, preferred_element_type=jnp.float32
        )
        router_probs = jax.nn.softmax(logits, axis=-1)
        return (normed, jnp.sum(router_probs * route_onehot, axis=-1))

    (normed_moe, gate_value), front_back = jax.vjp(
        moe_front, hidden_rows, moe_gain.astype(jnp.float32), router_weight.astype(jnp.float32)
    )

    def expert_major(buffer):
        shaped = buffer.reshape(dp_size, experts_here, capacity, model_width)
        return shaped.transpose(1, 0, 2, 3).reshape(experts_here, dp_size * capacity, model_width)

    def source_major(buffer):
        shaped = buffer.reshape(experts_here, dp_size, capacity, model_width)
        return shaped.transpose(1, 0, 2, 3).reshape(dp_size * experts_here, capacity, model_width)

    dispatch = place_rows(normed_moe.astype(jnp.bfloat16))
    arrived = expert_major(to_experts(dispatch))
    expert_inputs = group_rows(arrived)
    w_first, w_second = (expert_in, expert_out)
    pre_act = jnp.einsum("erd,edf->erf", expert_inputs, w_first, preferred_element_type=jnp.float32)
    hidden = jax.nn.gelu(pre_act).astype(jnp.bfloat16)
    expert_terms = jnp.einsum("erf,efd->erd", hidden, w_second, preferred_element_type=jnp.float32)
    expert_sum = group_sums(expert_terms)
    returned = from_experts(source_major(expert_sum.astype(jnp.bfloat16)))
    fetched = take_rows(returned)
    output_rows = hidden_rows + gate_value[:, None] * fetched
    block_output = output_rows.astype(jnp.bfloat16).reshape(group_seqs, part_len, model_width)
    out_grad = cotangent.astype(jnp.float32).reshape(tok_rows, model_width)
    gate_grad = jnp.sum(out_grad * fetched, axis=-1)
    fetched_grad = (gate_value[:, None] * out_grad).astype(jnp.bfloat16)
    returned_grad = place_rows(fetched_grad)
    sum_grad = expert_major(to_experts(returned_grad))
    sum_grad = group_rows(sum_grad)
    hidden_grad = jnp.einsum("erd,efd->erf", sum_grad, w_second, preferred_element_type=jnp.float32)
    second_grad = jnp.einsum("erf,erd->efd", hidden, sum_grad, preferred_element_type=jnp.float32)
    gelu_grad = jax.vjp(jax.nn.gelu, pre_act)[1](hidden_grad)[0]
    pre_grad = gelu_grad.astype(jnp.bfloat16)
    first_grad = jnp.einsum(
        "erd,erf->edf", expert_inputs, pre_grad, preferred_element_type=jnp.float32
    )
    input_terms = jnp.einsum("erf,edf->erd", pre_grad, w_first, preferred_element_type=jnp.float32)
    input_sum = group_sums(input_terms)
    dispatch_grad = from_experts(source_major(input_sum.astype(jnp.bfloat16)))
    normed_grad = take_rows(dispatch_grad)
    hidden_back, moe_gain_part, router_part = front_back((normed_grad, gate_grad))
    residual_grad = out_grad + hidden_back
    branch_grad = residual_grad.reshape(group_seqs, part_len, model_width).astype(jnp.bfloat16)
    complete_branch_output = lax.all_gather(branch_grad, "tensor", axis=1, tiled=True)
    out_weight_grad = jnp.einsum(
        "qza,qzw->aw",
        attended_token_rows,
        complete_branch_output,
        preferred_element_type=jnp.float32,
    )
    attended_grad = jnp.einsum(
        "zgq,wq->zgw",
        complete_branch_output,
        complete_output_rows,
        preferred_element_type=jnp.float32,
    ).astype(jnp.bfloat16)
    attended_grad = attended_grad.reshape(group_seqs, full_len, heads_here, head_size)

    def backward_one(packed):
        return attend_back(packed, position_bias, bucket_lines)

    combined_gradients, table_parts = lax.map(
        backward_one, (query_heads, key_heads, value_heads, segment_ids, log_totals, attended_grad)
    )
    joined_weight_grad = jnp.einsum(
        "tmf,tmw->fw",
        complete_normalized_rows,
        combined_gradients,
        preferred_element_type=jnp.float32,
    )
    normed_term = jnp.einsum(
        "iyp,mp->iym",
        combined_gradients,
        combined_weight_matrix,
        preferred_element_type=jnp.float32,
    )
    normed_back = lax.psum_scatter(
        normed_term.astype(jnp.bfloat16), "tensor", scatter_dimension=1, tiled=True
    ).astype(jnp.float32)
    input_back, attn_gain_part = jax.vjp(attn_norm, flat_input, attn_gain_f)[1](normed_back)
    input_grad = residual_grad.reshape(group_seqs, part_len, model_width) + input_back
    query_grad, key_grad, value_grad, out_grad_w = (
        lax.psum_scatter(joined_weight_grad[:, :head_cols], "dp", scatter_dimension=0, tiled=True),
        lax.psum_scatter(
            joined_weight_grad[:, head_cols : 2 * head_cols], "dp", scatter_dimension=0, tiled=True
        ),
        lax.psum_scatter(
            joined_weight_grad[:, 2 * head_cols :], "dp", scatter_dimension=0, tiled=True
        ),
        lax.psum_scatter(out_weight_grad, "dp", scatter_dimension=1, tiled=True),
    )
    table_empty = jnp.zeros((relative_bucket_count, heads_here * tensor_size), jnp.float32)
    table_full = lax.dynamic_update_slice_in_dim(
        table_empty, jnp.sum(table_parts, axis=0), head_start, 1
    )
    attn_gain_grad, moe_gain_grad, router_grad, table_grad = lax.psum(
        (attn_gain_part, moe_gain_part, router_part, table_full), ("dp", "tensor")
    )
    return (
        block_output,
        input_grad,
        attn_gain_grad,
        moe_gain_grad,
        router_grad,
        table_grad,
        query_grad,
        key_grad,
        value_grad,
        out_grad_w,
        first_grad,
        second_grad,
    )


def solution(mesh):
    in_specs = (
        P("dp", "tensor", None),
        P("dp", "tensor", None),
        P("dp", None),
        P(),
        P("dp", "tensor"),
        P("dp", "tensor"),
        P(),
        P(),
        P(),
        P(),
        P("dp", "tensor"),
        P("dp", "tensor"),
        P("dp", "tensor"),
        P("tensor", "dp"),
        P("dp", None, "tensor"),
        P("dp", "tensor", None),
    )
    out_specs = (
        P("dp", "tensor", None),
        P("dp", "tensor", None),
        P(),
        P(),
        P(),
        P(),
        P("dp", "tensor"),
        P("dp", "tensor"),
        P("dp", "tensor"),
        P("tensor", "dp"),
        P("dp", None, "tensor"),
        P("dp", "tensor", None),
    )
    return jax.shard_map(local, mesh=mesh, in_specs=in_specs, out_specs=out_specs, check_vma=False)
```

profile of v0, /device:TPU:0, one launch (start us, length us, event | category | flops | bytes accessed | tf_op | source)
XLA Modules:
  0.0 2145.2 jit_solution(12115809669340409489)
XLA Ops:
  14.1 32.7 %all_gather.25 = bf16[768,192]{1,0:T(8,128)(2,1)S(1)} all-gather(bf16[96,192]{1,0:T(8,128)(2,1)S(1)} %copy-done.43), channel_id=1, replica_groups=mesh['dp'=8,'tensor'=4] {'dp'}, dimensions={0}, use_global_device_ids=true | all-gather | bytes 331776 | tf_op jit(solution)/shard_map/all_gather | solution.py:140
  47.0 31.0 %all_gather.26 = bf16[768,192]{1,0:T(8,128)(2,1)S(1)} all-gather(bf16[96,192]{1,0:T(8,128)(2,1)S(1)} %copy-done.44), channel_id=1, replica_groups=mesh['dp'=8,'tensor'=4] {'dp'}, dimensions={0}, use_global_device_ids=true | all-gather | bytes 331776 | tf_op jit(solution)/shard_map/all_gather | solution.py:141
  78.9 30.9 %all_gather.27 = bf16[768,192]{1,0:T(8,128)(2,1)S(1)} all-gather(bf16[96,192]{1,0:T(8,128)(2,1)S(1)} %copy-done.45), channel_id=1, replica_groups=mesh['dp'=8,'tensor'=4] {'dp'}, dimensions={0}, use_global_device_ids=true | all-gather | bytes 331776 | tf_op jit(solution)/shard_map/all_gather | solution.py:142
  128.7 13.2 reshape.378
  149.5 31.0 %all_gather.28 = bf16[192,768]{0,1:T(8,128)(2,1)S(1)} all-gather(bf16[192,96]{0,1:T(8,128)(2,1)S(1)} %copy.60), channel_id=1, replica_groups=mesh['dp'=8,'tensor'=4] {'dp'}, dimensions={1}, use_global_device_ids=true | all-gather | bytes 331776 | tf_op jit(solution)/shard_map/all_gather | solution.py:143
  180.5 7.9 convolution_convert_fusion.3
  190.4 56.5 %while.27 = (s32[]{:T(128)}, bf16[8,512,3,64]{1,3,2,0:T(8,128)(2,1)}, f32[8,3,512]{2,1,0:T(4,128)}, bf16[8,512,3,64]{1,3,2,0:T(8,128)(2,1)}, s32[8,512]{1,0:T(8,...) while((s32[]{:T(128)}, ...), condition=%wide.region_4.5_spmd, body=%wide.region_1.4_spmd.sunk | while | flops 207976960 | bytes 13953633 | solution.py:180
  246.9 8.4 fusion.97
  256.0 99.8 %reduce-scatter.17.cloned.1.call-done = f32[8,128,768]{2,1,0:T(8,128)} async-done(((f32[8,512,768]{2,1,0:T(8,128)}), f32[8,128,768]{2,1,0:T(8,128)}) %reduce-scatter.17.cloned.1.call-update) | async-done | bytes 3145744 | tf_op jit(solution)/shard_map/reduce_scatter | solution.py:185
  364.6 72.7 %all_to_all.20 = bf16[8,240,768]{2,1,0:T(8,128)(2,1)} all-to-all(bf16[8,240,768]{2,1,0:T(8,128)(2,1)S(1)} %bitcast.259), channel_id=1, replica_groups=mesh['dp'=8,'tensor'=4] {'dp'}, dimensions={0} | all-to-all | bytes 5898240 | tf_op jit(solution)/shard_map/all_to_all | solution.py:93
  437.4 75.2 %all-gather.7.cloned.1.call-done = bf16[1,7680,768]{2,1,0:T(8,128)(2,1)} async-done(((bf16[1,1920,768]{2,1,0:T(8,128)(2,1)}), bf16[1,7680,768]{2,1,0:T(8,128)(2,1)}) %all-gather.7.cloned.1.call-update) | async-done | bytes 11796496 | tf_op jit(solution)/shard_map/all_gather | solution.py:101
  512.6 17.5 fusion.56
  530.0 22.9 %convolution_bitcast_fusion.2 = f32[1,7680,768]{2,1,0:T(8,128)} fusion(bf16[1,768,768]{2,1,0:T(8,128)(2,1)S(1)} %copy-done, f32[7680,768]{1,0:T(8,128)} %fusion.56), kind=kOutput, calls=%fused_computation.69 | convolution fusion | flops 9112780800 | bytes 48365568 | tf_op jit(solution)/shard_map/erf,efd->erd/dot_general | solution.py:230
  552.9 170.3 %reduce-scatter.19.cloned.1.call-done = f32[1,1920,768]{2,1,0:T(8,128)} async-done(((f32[1,7680,768]{2,1,0:T(8,128)}), f32[1,1920,768]{2,1,0:T(8,128)}) %reduce-scatter.19.cloned.1.call-update) | async-done | bytes 5898256 | tf_op jit(solution)/shard_map/reduce_scatter | solution.py:105
  737.2 62.8 %all-to-all-done.1 = bf16[8,240,768]{2,1,0:T(8,128)(2,1)} async-done(((bf16[8,240,768]{2,1,0:T(8,128)(2,1)}), bf16[8,240,768]{2,1,0:T(8,128)(2,1)}, u32[]{:S(2)}, u32[]{:S(2)}) %all-to-all-start.1) | async-done | bytes 2949152 | tf_op jit(solution)/shard_map/all_to_all | solution.py:97
  811.5 70.8 %all_to_all.21 = bf16[8,240,768]{2,1,0:T(8,128)(2,1)} all-to-all(bf16[8,240,768]{2,1,0:T(8,128)(2,1)S(1)} %bitcast.260), channel_id=1, replica_groups=mesh['dp'=8,'tensor'=4] {'dp'}, dimensions={0} | all-to-all | bytes 5898240 | tf_op jit(solution)/shard_map/all_to_all | solution.py:93
  882.8 74.8 %all-gather.9.cloned.1.call-done = bf16[1,7680,768]{2,1,0:T(8,128)(2,1)} async-done(((bf16[1,1920,768]{2,1,0:T(8,128)(2,1)}), bf16[1,7680,768]{2,1,0:T(8,128)(2,1)}) %all-gather.9.cloned.1.call-update) | async-done | bytes 11796496 | tf_op jit(solution)/shard_map/all_gather | solution.py:101
  957.6 28.3 %fusion.49 = bf16[7680,768]{1,0:T(8,128)(2,1)} fusion(f32[7680,768]{1,0:T(8,128)} %fusion.56, bf16[1,7680,768]{2,1,0:T(8,128)(2,1)} %all-gather.9.cloned.1.call-done, bf16[1,768,768]{2,1,0:T(8,128)(2,1)S(1)} %copy-done), kind=kOutput, calls=%fused_computation.66 | convolution fusion | flops 9177661440 | bytes 48365568 | tf_op jit(solution)/shard_map/erd,efd->erf/dot_general | solution.py:242
  985.9 17.5 convolution_bitcast_fusion.1
  1003.4 170.3 %reduce-scatter.21.cloned.1.call-done = f32[1,1920,768]{2,1,0:T(8,128)} async-done(((f32[1,7680,768]{2,1,0:T(8,128)}), f32[1,1920,768]{2,1,0:T(8,128)}) %reduce-scatter.21.cloned.1.call-update) | async-done | bytes 5898256 | tf_op jit(solution)/shard_map/reduce_scatter | solution.py:105
  1184.1 66.3 %all-to-all-done.3 = bf16[8,240,768]{2,1,0:T(8,128)(2,1)} async-done(((bf16[8,240,768]{2,1,0:T(8,128)(2,1)}), bf16[8,240,768]{2,1,0:T(8,128)(2,1)}, u32[]{:S(2)}, u32[]{:S(2)}) %all-to-all-start.3) | async-done | bytes 2949152 | tf_op jit(solution)/shard_map/all_to_all | solution.py:97
  1264.3 44.6 %all-gather.11.cloned.1.call-done = bf16[8,512,768]{2,1,0:T(8,128)(2,1)} async-done(((bf16[8,128,768]{2,1,0:T(8,128)(2,1)}), bf16[8,512,768]{2,1,0:T(8,128)(2,1)}) %all-gather.11.cloned.1.call-update) | async-done | bytes 6291472 | tf_op jit(solution)/shard_map/all_gather | solution.py:256
  1320.8 552.2 %while.28 = (s32[]{:T(128)}, bf16[8,512,576]{1,2,0:T(8,128)(2,1)}, f32[8,32,3]{1,2,0:T(4,128)S(1)}, bf16[8,512,3,64]{1,3,2,0:T(8,128)(2,1)}, s32[8,512]{1,0:T(8,...) while((s32[]{:T(128)}, bf16[8,512,576]{1,2,0:T(8,128)(2,1)}, ...), condition=%wide.region_18.19_spmd.clone, body=%wide.region_15.18_spmd.clone.sunk | while | flops 515531584 | bytes 157856080 | solution.py:274
  1329.6 17.6 rev.8
  1356.2 7.1 copy.89
  1367.5 13.2 reshape.413
  1398.6 17.6 rev.8
  1436.4 13.2 reshape.413
  1467.5 17.6 rev.8
  1505.4 13.2 reshape.413
  1536.5 17.6 rev.8
  1574.3 13.2 reshape.413
  1605.4 17.6 rev.8
  1643.3 13.2 reshape.413
  1674.4 17.6 rev.8
  1712.2 13.2 reshape.413
  1743.3 17.6 rev.8
  1781.1 13.2 reshape.413
  1812.2 17.6 rev.8
  1850.1 13.2 reshape.413
  1873.0 9.4 convolution_convert_fusion.2
  1882.5 8.5 convolution_bitcast_fusion.3
  1897.8 20.5 fusion.82
  1919.5 15.6 fusion.85
  1944.0 40.8 %all-reduce.2 = (f32[768]{0:T(1024)}, f32[768]{0:T(1024)}, f32[768,8]{0,1:T(8,128)}, f32[32,12]{0,1:T(8,128)}) all-reduce(f32[768]{0:T(1024)S(1)} %get-tuple-element.298, f32[768]{0:T(1024)S(1)} %copy-done.55, f32[768,8]{0,1:T(8,128)S(1)} %fusion.114, ...), channel_id=1, replica_groups=mesh['dp'=8,'tensor'=4] {'dp','tensor'}, use_global_device_ids=true, to_apply=%region_22.23 | all-reduce | flops 8064 | bytes 64512 | tf_op jit(solution)/shard_map/psum | solution.py:308
  1989.7 17.5 reduce-scatter.25.cloned.1.call-done
  2007.3 65.7 %reduce-scatter.27.cloned.1.call-done = f32[96,192]{1,0:T(8,128)} async-done(((f32[768,192]{1,0:T(8,128)}), f32[96,192]{1,0:T(8,128)}) %reduce-scatter.27.cloned.1.call-update) | async-done | bytes 73744
  2073.0 65.2 %reduce-scatter.29.cloned.1.call-done = f32[96,192]{1,0:T(8,128)} async-done(((f32[768,192]{1,0:T(8,128)}), f32[96,192]{1,0:T(8,128)}) %reduce-scatter.29.cloned.1.call-update) | async-done | bytes 73744
  (480 shorter events, 482.5 us)
Async XLA Ops:
  7.2 522.9 %copy-start = (bf16[1,768,768]{2,1,0:T(8,128)(2,1)S(1)}, bf16[1,768,768]{2,1,0:T(8,128)(2,1)}, u32[]{:S(2)}) copy-start(bf16[1,768,768]{2,1,0:T(8,128)(2,1)} %param.35) | copy-start | bytes 3538948
  7.2 173.3 %all-gather.5.cloned.1.call-start = ((), (), s32[]{:S(2)}) async-start(), calls=%async_computation.12 | async-start | bytes 7864320 | tf_op jit(solution)/shard_map/all_gather | solution.py:149
  9.1 37.9 %copy-start.44 = (bf16[96,192]{1,0:T(8,128)(2,1)S(1)}, bf16[96,192]{1,0:T(8,128)(2,1)}, u32[]{:S(2)}) copy-start(bf16[96,192]{1,0:T(8,128)(2,1)} %param.31) | copy-start | bytes 110596
  11.0 67.9 %copy-start.45 = (bf16[96,192]{1,0:T(8,128)(2,1)S(1)}, bf16[96,192]{1,0:T(8,128)(2,1)}, u32[]{:S(2)}) copy-start(bf16[96,192]{1,0:T(8,128)(2,1)} %param.32) | copy-start | bytes 110596
  14.0 96.8 %copy-start.60 = (s32[1023]{0:T(1024)S(1)}, s32[1023]{0:T(1024)}, u32[]{:S(2)}) copy-start(s32[1023]{0:T(1024)} %param.23) | copy-start | bytes 12280
  14.0 341.8 %reduce-scatter.17.cloned.1.call-start = ((), (), s32[]{:S(2)}) async-start(), calls=%async_computation.13 | async-start | bytes 15728640 | tf_op jit(solution)/shard_map/reduce_scatter | solution.py:185
  47.0 133.5 %copy-start.22 = (bf16[768,192]{0,1:T(8,128)(2,1)}, bf16[768,192]{0,1:T(8,128)(2,1)S(1)}, u32[]{:S(2)}) copy-start(bf16[768,192]{0,1:T(8,128)(2,1)S(1)} %copy.56) | copy-start | bytes 884740
  145.8 34.7 %copy-start.24 = (bf16[768,192]{0,1:T(8,128)(2,1)S(1)}, bf16[768,192]{0,1:T(8,128)(2,1)}, u32[]{:S(2)}) copy-start(bf16[768,192]{0,1:T(8,128)(2,1)} %copy.57) | copy-start | bytes 884740
  145.8 34.7 %copy-start.26 = (bf16[768,192]{0,1:T(8,128)(2,1)S(1)}, bf16[768,192]{0,1:T(8,128)(2,1)}, u32[]{:S(2)}) copy-start(bf16[768,192]{0,1:T(8,128)(2,1)} %copy.58) | copy-start | bytes 884740
  180.5 66.4 %copy-start.16 = (bf16[192,768]{0,1:T(8,128)(2,1)}, bf16[192,768]{0,1:T(8,128)(2,1)S(1)}, u32[]{:S(2)}) copy-start(bf16[192,768]{0,1:T(8,128)(2,1)S(1)} %all_gather.28) | copy-start | bytes 884740
  255.3 100.5 %copy-start.9 = (bf16[8,128,768]{2,1,0:T(8,128)(2,1)S(1)}, bf16[8,128,768]{2,1,0:T(8,128)(2,1)}, u32[]{:S(2)}) copy-start(bf16[8,128,768]{2,1,0:T(8,128)(2,1)} %param.20) | copy-start | bytes 4718596
  255.3 257.3 %all-gather.7.cloned.1.call-start = ((), (), s32[]{:S(2)}) async-start(), calls=%async_computation.14 | async-start | bytes 14745600 | tf_op jit(solution)/shard_map/all_gather | solution.py:101
  256.0 102.2 %copy-start.36 = (f32[768]{0:T(1024)}, f32[768]{0:T(1024)S(1)}, u32[]{:S(2)}) copy-start(f32[768]{0:T(1024)S(1)} %convert_element_type.112) | copy-start | bytes 9220
  364.6 148.0 %copy-start.58 = (bf16[1,768,768]{2,1,0:T(8,128)(2,1)S(1)}, bf16[1,768,768]{2,1,0:T(8,128)(2,1)}, u32[]{:S(2)}) copy-start(bf16[1,768,768]{2,1,0:T(8,128)(2,1)} %param.34) | copy-start | bytes 3538948
  437.3 286.0 %reduce-scatter.19.cloned.1.call-start = ((), (), s32[]{:S(2)}) async-start(), calls=%async_computation.15 | async-start | bytes 29491200 | tf_op jit(solution)/shard_map/reduce_scatter | solution.py:105
  727.8 72.3 %copy-start.19 = (bf16[8,128,768]{2,1,0:T(8,128)(2,1)S(1)}, bf16[8,128,768]{2,1,0:T(8,128)(2,1)}, u32[]{:S(2)}) copy-start(bf16[8,128,768]{2,1,0:T(8,128)(2,1)} %param.21) | copy-start | bytes 4718596
  727.8 72.2 %all-to-all-start.1 = ((bf16[8,240,768]{2,1,0:T(8,128)(2,1)}), bf16[8,240,768]{2,1,0:T(8,128)(2,1)}, u32[]{:S(2)}, u32[]{:S(2)}) async-start(bf16[8,240,768]{2,1,0:T(8,128)(2,1)} %bitcast.253), calls=%async_computation.3 | async-start | bytes 5898240 | tf_op jit(solution)/shard_map/all_to_all | solution.py:97
  733.5 224.2 %all-gather.9.cloned.1.call-start = ((), (), s32[]{:S(2)}) async-start(), calls=%async_computation.16 | async-start | bytes 14745600 | tf_op jit(solution)/shard_map/all_gather | solution.py:101
  737.1 518.9 %copy-start.20 = (f32[1024,8]{0,1:T(8,128)}, f32[1024,8]{0,1:T(8,128)S(1)}, u32[]{:S(2)}) copy-start(f32[1024,8]{0,1:T(8,128)S(1)} %get-tuple-element.359) | copy-start | bytes 98308
  737.2 518.9 %copy-start.28 = (f32[1024]{0:T(1024)}, f32[1024]{0:T(1024)S(1)}, u32[]{:S(2)}) copy-start(f32[1024]{0:T(1024)S(1)} %get-tuple-element.358) | copy-start | bytes 12292
  737.2 518.9 %copy-start.30 = (f32[1024]{0:T(1024)}, f32[1024]{0:T(1024)S(1)}, u32[]{:S(2)}) copy-start(f32[1024]{0:T(1024)S(1)} %fusion.104) | copy-start | bytes 12292
  807.2 448.9 %copy-start.51 = (f32[1024]{0:T(1024)}, f32[1024]{0:T(1024)S(1)}, u32[]{:S(2)}) copy-start(f32[1024]{0:T(1024)S(1)} %get-tuple-element.360) | copy-start | bytes 12292
  882.3 291.4 %reduce-scatter.21.cloned.1.call-start = ((), (), s32[]{:S(2)}) async-start(), calls=%async_computation.17 | async-start | bytes 29491200 | tf_op jit(solution)/shard_map/reduce_scatter | solution.py:105
  957.6 28.3 %copy-start.59 = (bf16[1,768,768]{2,1,0:T(8,128)(2,1)S(1)}, bf16[1,768,768]{2,1,0:T(8,128)(2,1)}, u32[]{:S(2)}) copy-start(bf16[1,768,768]{2,1,0:T(8,128)(2,1)} %param.34) | copy-start | bytes 3538948
  1178.3 72.1 %all-to-all-start.3 = ((bf16[8,240,768]{2,1,0:T(8,128)(2,1)}), bf16[8,240,768]{2,1,0:T(8,128)(2,1)}, u32[]{:S(2)}, u32[]{:S(2)}) async-start(bf16[8,240,768]{2,1,0:T(8,128)(2,1)} %bitcast.256), calls=%async_computation.6 | async-start | bytes 5898240 | tf_op jit(solution)/shard_map/all_to_all | solution.py:97
  1183.8 125.1 %all-gather.11.cloned.1.call-start = ((), (), s32[]{:S(2)}) async-start(), calls=%async_computation.18 | async-start | bytes 7864320 | tf_op jit(solution)/shard_map/all_gather | solution.py:256
  1184.1 72.0 %copy-start.49 = (f32[1024]{0:T(1024)}, f32[1024]{0:T(1024)S(1)}, u32[]{:S(2)}) copy-start(f32[1024]{0:T(1024)S(1)} %neg.6) | copy-start | bytes 12292
  1264.2 671.0 %reduce-scatter.31.cloned.1.call-start = ((), (), s32[]{:S(2)}) async-start(), calls=%async_computation.23 | async-start | bytes 884736
  1264.3 51.4 %copy-start.17 = (bf16[192,768]{0,1:T(8,128)(2,1)S(1)}, bf16[192,768]{0,1:T(8,128)(2,1)}, u32[]{:S(2)}) copy-start(bf16[192,768]{0,1:T(8,128)(2,1)} %copy-done.16) | copy-start | bytes 884740
  1315.7 625.3 %reduce-scatter.23.cloned.1.call-start = ((), (), s32[]{:S(2)}) async-start(), calls=%async_computation.19 | async-start | bytes 7864320 | tf_op jit(solution)/shard_map/reduce_scatter | solution.py:289
  1315.7 557.2 %copy-start.27 = (bf16[768,192]{0,1:T(8,128)(2,1)S(1)}, bf16[768,192]{0,1:T(8,128)(2,1)}, u32[]{:S(2)}) copy-start(bf16[768,192]{0,1:T(8,128)(2,1)} %copy.58) | copy-start | bytes 884740
  1320.8 552.2 %copy-start.23 = (bf16[768,192]{0,1:T(8,128)(2,1)S(1)}, bf16[768,192]{0,1:T(8,128)(2,1)}, u32[]{:S(2)}) copy-start(bf16[768,192]{0,1:T(8,128)(2,1)} %copy-done.22) | copy-start | bytes 884740
  1320.8 552.2 %copy-start.25 = (bf16[768,192]{0,1:T(8,128)(2,1)S(1)}, bf16[768,192]{0,1:T(8,128)(2,1)}, u32[]{:S(2)}) copy-start(bf16[768,192]{0,1:T(8,128)(2,1)} %copy.57) | copy-start | bytes 884740
  1329.6 21.1 copy-start.4
  1398.6 21.1 copy-start.4
  1467.5 21.1 copy-start.4
  1536.5 21.1 copy-start.4
  1605.4 21.1 copy-start.4
  1743.3 21.1 copy-start.4
  1812.2 21.1 copy-start.4
  1882.4 124.9 %reduce-scatter.25.cloned.1.call-start = ((), (), s32[]{:S(2)}) async-start(), calls=%async_computation.20 | async-start | bytes 884736
  1892.4 180.6 %reduce-scatter.27.cloned.1.call-start = ((), (), s32[]{:S(2)}) async-start(), calls=%async_computation.21 | async-start | bytes 884736
  1897.7 240.4 %reduce-scatter.29.cloned.1.call-start = ((), (), s32[]{:S(2)}) async-start(), calls=%async_computation.22 | async-start | bytes 884736
  1919.5 21.5 %copy-start.10 = (bf16[8,128,768]{2,1,0:T(8,128)(2,1)S(1)}, bf16[8,128,768]{2,1,0:T(8,128)(2,1)}, u32[]{:S(2)}) copy-start(bf16[8,128,768]{2,1,0:T(8,128)(2,1)} %param.20) | copy-start | bytes 4718596
  1919.5 21.5 %copy-start.33 = (f32[8,128]{1,0:T(8,128)S(1)}, f32[8,128]{1,0:T(8,128)}, u32[]{:S(2)}) copy-start(f32[8,128]{1,0:T(8,128)} %copy-done.32) | copy-start | bytes 12292
  1919.5 21.5 %copy-start.35 = (f32[768]{0:T(1024)S(1)}, f32[768]{0:T(1024)}, u32[]{:S(2)}) copy-start(f32[768]{0:T(1024)} %copy-done.34) | copy-start | bytes 9220
  1935.1 49.6 %copy-start.54 = (f32[8,128]{1,0:T(8,128)S(1)}, f32[8,128]{1,0:T(8,128)}, u32[]{:S(2)}) copy-start(f32[8,128]{1,0:T(8,128)} %copy-done.53) | copy-start | bytes 12292
  1984.7 153.4 %copy-start.1 = (bf16[1,768,768]{2,1,0:T(8,128)(2,1)S(1)}, bf16[1,768,768]{2,1,0:T(8,128)(2,1)}, u32[]{:S(2)}) copy-start(bf16[1,768,768]{2,1,0:T(8,128)(2,1)} %param.35) | copy-start | bytes 3538948
  (77 other events, 278.9 us)
Sparse Core Ops, SparseCore 0:
  14.1 49.0 all-gather.4
  255.4 100.3 reduce-scatter.16
  437.4 75.0 all-gather.6
  553.1 170.1 reduce-scatter.18
  882.4 75.1 all-gather.8
  1003.5 170.1 reduce-scatter.20
  1264.4 44.5 all-gather.10
  1315.8 62.5 reduce-scatter.30
  1882.5 58.3 reduce-scatter.22
  1944.7 62.5 reduce-scatter.24
  2011.5 61.4 reduce-scatter.26
  2076.7 61.3 reduce-scatter.28
where the time goes:
time: 2150 us
  waiting for transfers between devices  917 us (43%)
  local copies, waits for them, and re-layouts  491 us (23%)
  matrix products  317 us (15%)
  blocking collectives  310 us (14%)
  other arithmetic  81 us (4%)
    reduce_scatter x2, waiting for transfers between devices, group_sums(): return lax.psum_scatter(terms, 'tensor', scatter_dimension=1, tiled=True)  341 us
    all_gather x2, waiting for transfers between devices, group_rows(): return lax.all_gather(buffer, 'tensor', axis=1, tiled=True)  150 us
    unnamed x16, waiting for transfers between devices  149 us
    all_to_all x2, blocking collectives, to_experts(): return lax.all_to_all(buffer, 'dp', split_axis=0, concat_axis=0, tiled=True)  143 us
    while x136, local copies, waits for them, and re-layouts  142 us
    rev x8, local copies, waits for them, and re-layouts, diagonal_sums(): flipped = square[:, ::-1, :]  141 us
    all_to_all x2, waiting for transfers between devices, from_experts(): return lax.all_to_all(buffer, 'dp', split_axis=0, concat_axis=0, tiled=True)  129 us
    reshape x8, local copies, waits for them, and re-layouts, diagonal_sums(): return jnp.sum(flat.reshape(heads_count, seq_len, 2 * seq_len - 1), axis=1)  106 us
  transfers between devices with their start and end apart: 14, of which 12 were waited for; matrix products, arithmetic and copies ran while one was open for 31% of the time, Pallas kernels for 0%

commit v1 on v0

v1 whole, which is shorter than its diff:
```python
import functools

import jax
import jax.numpy as jnp
from jax import lax
from jax.experimental import pallas as pl
from jax.experimental.pallas import tpu as pltpu
from jax.sharding import PartitionSpec as P

EPSILON = 1e-06
MASKED_SCORE = -1e30
BF = jnp.bfloat16
F32 = jnp.float32
TILE = 128
NT = (((1,), (1,)), ((), ()))
TN = (((0,), (0,)), ((), ()))


def rms_inverse(values):
    return lax.rsqrt(jnp.mean(values * values, axis=-1, keepdims=True) + EPSILON)


def attn_norm(tokens_in, gain):
    return tokens_in * rms_inverse(tokens_in) * gain


def matmul(left, right, dims=None):
    if dims is None:
        dims = (((1,), (0,)), ((), ()))
    return lax.dot_general(left, right, dims, preferred_element_type=F32)


def head_only(rows, head, head_size):
    lane = lax.broadcasted_iota(jnp.int32, rows.shape, 1)
    inside = (lane >= head * head_size) & (lane < (head + 1) * head_size)
    return jnp.where(inside, rows, jnp.zeros_like(rows))


def attend_kernel(heads, head_size, n1_ref, w_ref, segc_ref, segr_ref, line_ref,
                  out_ref, qkv_ref, o_ref, p_ref, bias_ref, acc_ref):
    group, seq = pl.program_id(0), pl.program_id(1)
    width = heads * head_size
    model = n1_ref.shape[-1]
    length = segr_ref.shape[-1]
    tiles = length // TILE

    @pl.when(seq == 0)
    def _():
        for head in range(heads):
            for d in range(2 * tiles - 1):
                line = jnp.broadcast_to(line_ref[0, head, d : d + 1, :], (TILE, 2 * TILE))
                bias_ref[head, d] = pltpu.roll(line, 0, 1, stride=1, stride_axis=0)[:, TILE:]

    rows = n1_ref[:, 0].reshape(length, model)
    qkv = matmul(rows, w_ref[0, :, : 3 * width]).astype(BF)
    qkv_ref[0, 0] = qkv
    queries, keys, values = qkv[:, :width], qkv[:, width : 2 * width], qkv[:, 2 * width :]
    seg_row = segr_ref[0]
    attended = jnp.zeros((length, width), F32)
    for head in range(heads):
        scores = matmul(head_only(queries, head, head_size), keys, NT)
        for t in range(tiles):
            span = slice(t * TILE, (t + 1) * TILE)
            bias = jnp.concatenate(
                [bias_ref[head, c - t + tiles - 1] for c in range(tiles)], axis=1
            )
            same_doc = segc_ref[0, span] == seg_row
            part = jnp.where(same_doc, scores[span] + bias, MASKED_SCORE)
            peak = jnp.max(part, axis=1, keepdims=True)
            expo = jnp.exp(part - peak)
            total = jnp.sum(expo, axis=1, keepdims=True)
            p_ref[0, 0, head, span] = (expo * (1.0 / total)).astype(BF)
        attended += matmul(p_ref[0, 0, head], head_only(values, head, head_size))
    attended = attended.astype(BF)
    o_ref[0, 0] = attended
    branch = matmul(attended, w_ref[0, :, 3 * width :], NT)

    @pl.when(group == 0)
    def _():
        acc_ref[seq] = branch

    @pl.when(group > 0)
    def _():
        acc_ref[seq] += branch

    @pl.when(group == pl.num_programs(0) - 1)
    def _():
        out_ref[:, seq] = acc_ref[seq].astype(BF).reshape(tiles, TILE, model)


def attend_back_kernel(heads, head_size, n1_ref, db_ref, w_ref, qkv_ref, o_ref, p_ref,
                       out_ref, dw_ref, line_ref, gain_ref, acc_ref, dw_acc, sums_ref):
    group, seq = pl.program_id(0), pl.program_id(1)
    width = heads * head_size
    model = n1_ref.shape[-1]
    length = qkv_ref.shape[2]
    tiles = length // TILE
    rows = n1_ref[:, 0].reshape(length, model)
    branch_grad = db_ref[:, 0].reshape(length, model)
    attended_grad = matmul(branch_grad, w_ref[0, :, 3 * width :]).astype(BF)
    qkv = qkv_ref[0, 0]
    queries, keys, values = qkv[:, :width], qkv[:, width : 2 * width], qkv[:, 2 * width :]
    attended = o_ref[0, 0]
    queries_t = queries.T
    grad_t = attended_grad.T
    inner_all = attended_grad.astype(F32) * attended.astype(F32)

    @pl.when(seq == 0)
    def _():
        sums_ref[...] = jnp.zeros_like(sums_ref)

    query_grad = jnp.zeros((length, width), F32)
    key_grads, value_grads = [], []
    for head in range(heads):
        cut = slice(head * head_size, (head + 1) * head_size)
        inner = jnp.sum(head_only(inner_all, head, head_size), axis=1, keepdims=True)
        prob_grad = matmul(head_only(attended_grad, head, head_size), values, NT)
        probs = p_ref[0, 0, head]
        parts = []
        for t in range(tiles):
            span = slice(t * TILE, (t + 1) * TILE)
            part = probs[span].astype(F32) * (prob_grad[span] - inner[span])
            for c in range(tiles):
                sums_ref[head, c - t + tiles - 1] += part[:, c * TILE : (c + 1) * TILE]
            parts.append(part.astype(BF))
        score_grad = jnp.concatenate(parts, axis=0)
        query_grad += matmul(score_grad, head_only(keys, head, head_size))
        key_grads.append(matmul(queries_t[cut], score_grad))
        value_grads.append(matmul(grad_t[cut], probs))
    key_grad = jnp.concatenate(key_grads, axis=0).T
    value_grad = jnp.concatenate(value_grads, axis=0).T
    joined = jnp.concatenate(
        [query_grad.astype(BF), key_grad.astype(BF), value_grad.astype(BF)], axis=1
    )
    normed_grad = matmul(joined, w_ref[0, :, : 3 * width], NT)
    proj_grad = matmul(rows, joined, TN)
    out_grad = matmul(branch_grad, attended, TN)

    @pl.when(seq == 0)
    def _():
        dw_acc[:, : 3 * width] = proj_grad
        dw_acc[:, 3 * width :] = out_grad

    @pl.when(seq > 0)
    def _():
        dw_acc[:, : 3 * width] += proj_grad
        dw_acc[:, 3 * width :] += out_grad

    @pl.when(group == 0)
    def _():
        acc_ref[seq] = normed_grad

    @pl.when(group > 0)
    def _():
        acc_ref[seq] += normed_grad

    @pl.when(seq == pl.num_programs(1) - 1)
    def _():
        dw_ref[0] = dw_acc[...].astype(BF)
        row = lax.broadcasted_iota(jnp.int32, (TILE, TILE), 0)
        lane = lax.broadcasted_iota(jnp.int32, (TILE, TILE), 1)
        flip = (row + lane == TILE - 1).astype(F32)
        for head in range(heads):
            for d in range(2 * tiles - 1):
                turned = lax.dot_general(
                    flip, sums_ref[head, d], (((1,), (0,)), ((), ())),
                    precision=lax.Precision.HIGHEST, preferred_element_type=F32,
                )
                wide = jnp.concatenate([turned, jnp.zeros_like(turned)], axis=1)
                skewed = pltpu.roll(wide, 1, 1, stride=1, stride_axis=0)
                line_ref[0, head, d : d + 1, :] = jnp.sum(skewed, axis=0, keepdims=True)
            line_ref[0, head, 2 * tiles - 1 :, :] = jnp.zeros((1, 2 * TILE), F32)

    @pl.when((group == 0) & (seq == 0))
    def _():
        gain_ref[...] = jnp.zeros_like(gain_ref)

    @pl.when(group == pl.num_programs(0) - 1)
    def _():
        total = acc_ref[seq]
        out_ref[:, seq] = total.astype(BF).reshape(tiles, TILE, model)
        gain_ref[...] += jnp.sum(total * rows.astype(F32), axis=0, keepdims=True)


def expert_kernel(u_ref, c_ref, wi_ref, wo_ref, du_ref, dg_ref, r_ref, da_ref, acc_ref, dg_acc):
    chunk = pl.program_id(1)
    first, second = wi_ref[0], wo_ref[0]
    pre_act = matmul(u_ref[...], first)
    hidden_grad = matmul(c_ref[...], second, NT)
    root = 0.7978845608028654
    square = pre_act * pre_act
    bend = jnp.tanh(root * pre_act * (1.0 + 0.044715 * square))
    half = 0.5 * (1.0 + bend)
    hidden = (pre_act * half).astype(BF)
    slope = half + 0.5 * root * pre_act * (1.0 - bend * bend) * (1.0 + 3 * 0.044715 * square)
    pre_grad = (hidden_grad * slope).astype(BF)
    r_ref[0] = hidden
    da_ref[0] = pre_grad
    gate_part = jnp.sum(hidden.astype(F32) * hidden_grad, axis=1, keepdims=True)
    input_part = matmul(pre_grad, first, NT)

    @pl.when(chunk == 0)
    def _():
        acc_ref[...] = input_part
        dg_acc[...] = gate_part

    @pl.when(chunk > 0)
    def _():
        acc_ref[...] += input_part
        dg_acc[...] += gate_part

    @pl.when(chunk == pl.num_programs(1) - 1)
    def _():
        du_ref[...] = acc_ref[...].astype(BF)
        dg_ref[...] = dg_acc[...]


def attend(n1_seqs, weights, seg_here, lines, heads, head_size):
    groups, seqs, part, model = n1_seqs.shape
    length = seg_here.shape[1]
    width = heads * head_size
    tiles = length // TILE
    flops = 2 * groups * seqs * length * (4 * width * model + 2 * heads * length * head_size)
    return pl.pallas_call(
        functools.partial(attend_kernel, heads, head_size),
        grid=(groups, seqs),
        in_specs=[
            pl.BlockSpec((groups, 1, part, model), lambda g, s: (0, s, 0, 0)),
            pl.BlockSpec((1, model, 4 * width), lambda g, s: (g, 0, 0)),
            pl.BlockSpec((1, length, 1), lambda g, s: (s, 0, 0)),
            pl.BlockSpec((1, 1, length), lambda g, s: (s, 0, 0)),
            pl.BlockSpec((1, heads, 2 * tiles, 2 * TILE), lambda g, s: (g, 0, 0, 0)),
        ],
        out_specs=[
            pl.BlockSpec((groups, seqs, part, model), lambda g, s: (0, 0, 0, 0)),
            pl.BlockSpec((1, 1, length, 3 * width), lambda g, s: (g, s, 0, 0)),
            pl.BlockSpec((1, 1, length, width), lambda g, s: (g, s, 0, 0)),
            pl.BlockSpec((1, 1, heads, length, length), lambda g, s: (g, s, 0, 0, 0)),
        ],
        out_shape=[
            jax.ShapeDtypeStruct((groups, seqs, part, model), BF),
            jax.ShapeDtypeStruct((groups, seqs, length, 3 * width), BF),
            jax.ShapeDtypeStruct((groups, seqs, length, width), BF),
            jax.ShapeDtypeStruct((groups, seqs, heads, length, length), BF),
        ],
        scratch_shapes=[
            pltpu.VMEM((heads, 2 * tiles - 1, TILE, TILE), F32),
            pltpu.VMEM((seqs, length, model), F32),
        ],
        compiler_params=pltpu.CompilerParams(vmem_limit_bytes=48 << 20),
        cost_estimate=pl.CostEstimate(
            flops=6 * flops, bytes_accessed=24 << 20, transcendentals=groups * seqs * heads * length**2
        ),
        name="attend",
    )(n1_seqs, weights, seg_here[:, :, None], seg_here[:, None, :], lines)


def attend_back(n1_seqs, db_seqs, weights, qkv, attended, probs, heads, head_size):
    groups, seqs, part, model = n1_seqs.shape
    length = qkv.shape[2]
    width = heads * head_size
    tiles = length // TILE
    flops = 2 * groups * seqs * length * (8 * width * model + 4 * heads * length * head_size)
    return pl.pallas_call(
        functools.partial(attend_back_kernel, heads, head_size),
        grid=(groups, seqs),
        in_specs=[
            pl.BlockSpec((groups, 1, part, model), lambda g, s: (0, s, 0, 0)),
            pl.BlockSpec((groups, 1, part, model), lambda g, s: (0, s, 0, 0)),
            pl.BlockSpec((1, model, 4 * width), lambda g, s: (g, 0, 0)),
            pl.BlockSpec((1, 1, length, 3 * width), lambda g, s: (g, s, 0, 0)),
            pl.BlockSpec((1, 1, length, width), lambda g, s: (g, s, 0, 0)),
            pl.BlockSpec((1, 1, heads, length, length), lambda g, s: (g, s, 0, 0, 0)),
        ],
        out_specs=[
            pl.BlockSpec((groups, seqs, part, model), lambda g, s: (0, 0, 0, 0)),
            pl.BlockSpec((1, model, 4 * width), lambda g, s: (g, 0, 0)),
            pl.BlockSpec((1, heads, 2 * tiles, 2 * TILE), lambda g, s: (g, 0, 0, 0)),
            pl.BlockSpec((1, model), lambda g, s: (0, 0)),
        ],
        out_shape=[
            jax.ShapeDtypeStruct((groups, seqs, part, model), BF),
            jax.ShapeDtypeStruct((groups, model, 4 * width), BF),
            jax.ShapeDtypeStruct((groups, heads, 2 * tiles, 2 * TILE), F32),
            jax.ShapeDtypeStruct((1, model), F32),
        ],
        scratch_shapes=[
            pltpu.VMEM((seqs, length, model), F32),
            pltpu.VMEM((model, 4 * width), F32),
            pltpu.VMEM((heads, 2 * tiles - 1, TILE, TILE), F32),
        ],
        compiler_params=pltpu.CompilerParams(vmem_limit_bytes=56 << 20),
        cost_estimate=pl.CostEstimate(
            flops=6 * flops, bytes_accessed=32 << 20, transcendentals=0
        ),
        name="attend_back",
    )(n1_seqs, db_seqs, weights, qkv, attended, probs)


def run_experts(inputs, grads, first, second):
    rows, model = inputs.shape
    chunks, _, units = first.shape
    block = rows // 4
    flops = 2 * 3 * rows * model * units * chunks
    return pl.pallas_call(
        expert_kernel,
        grid=(rows // block, chunks),
        in_specs=[
            pl.BlockSpec((block, model), lambda b, k: (b, 0)),
            pl.BlockSpec((block, model), lambda b, k: (b, 0)),
            pl.BlockSpec((1, model, units), lambda b, k: (k, 0, 0)),
            pl.BlockSpec((1, units, model), lambda b, k: (k, 0, 0)),
        ],
        out_specs=[
            pl.BlockSpec((block, model), lambda b, k: (b, 0)),
            pl.BlockSpec((block, 1), lambda b, k: (b, 0)),
            pl.BlockSpec((1, block, units), lambda b, k: (k, b, 0)),
            pl.BlockSpec((1, block, units), lambda b, k: (k, b, 0)),
        ],
        out_shape=[
            jax.ShapeDtypeStruct((rows, model), BF),
            jax.ShapeDtypeStruct((rows, 1), F32),
            jax.ShapeDtypeStruct((chunks, rows, units), BF),
            jax.ShapeDtypeStruct((chunks, rows, units), BF),
        ],
        scratch_shapes=[pltpu.VMEM((block, model), F32), pltpu.VMEM((block, 1), F32)],
        compiler_params=pltpu.CompilerParams(vmem_limit_bytes=48 << 20),
        cost_estimate=pl.CostEstimate(
            flops=flops, bytes_accessed=60 << 20, transcendentals=rows * units * chunks
        ),
        name="experts",
    )(inputs, grads, first, second)


def swap_tensor(block, bit):
    size = lax.axis_size("tensor")
    return lax.ppermute(block, "tensor", [(i, i ^ bit) for i in range(size)])


def gather_tensor(block):
    pair = jnp.stack([block, swap_tensor(block, 2)])
    return jnp.concatenate([pair, swap_tensor(pair, 1)], axis=0)


def scatter_tensor(stack):
    near = swap_tensor(stack[2:], 1)
    kept = stack[0].astype(F32) + near[0].astype(F32)
    passed = (stack[1].astype(F32) + near[1].astype(F32)).astype(stack.dtype)
    return kept + swap_tensor(passed, 2).astype(F32)


def swap_dp(buffer):
    return lax.all_to_all(buffer, "dp", split_axis=0, concat_axis=0, tiled=True)


def swap_seqs(buffer):
    return lax.all_to_all(buffer, "tensor", split_axis=0, concat_axis=0, tiled=True)


def local(
    block_input,
    cotangent,
    segment_ids,
    rel_bucket,
    expert_route,
    expert_slot,
    attn_gain,
    moe_gain,
    router_weight,
    rel_table,
    w_query,
    w_key,
    w_value,
    w_out,
    expert_in,
    expert_out,
):
    group_seqs, part_len, model_width = block_input.shape
    tensor_size = lax.axis_size("tensor")
    dp_size = lax.axis_size("dp")
    full_len = part_len * tensor_size
    seqs_here = group_seqs // tensor_size
    head_cols = w_query.shape[1]
    weight_rows = w_query.shape[0]
    heads_all = rel_table.shape[1]
    heads_here = heads_all // tensor_size
    head_size = head_cols // heads_here
    bucket_count = rel_table.shape[0]
    experts_all = router_weight.shape[1]
    tok_rows = group_seqs * part_len
    capacity = tok_rows * 15 // (8 * experts_all)
    buffer_size = experts_all * capacity
    tiles = full_len // TILE
    me = lax.axis_index("tensor")
    visits = jnp.array([0, 2, 1, 3])
    order = me ^ visits

    packed = jnp.concatenate([w_query, w_key, w_value, w_out.T], axis=1)
    spread = jnp.broadcast_to(packed[None], (dp_size,) + packed.shape)
    owned = swap_dp(spread).reshape(model_width, 4 * head_cols)
    weights = gather_tensor(owned)

    flat_input = block_input.astype(F32)
    attn_gain_f = attn_gain.astype(F32)
    normed_local = attn_norm(flat_input, attn_gain_f).astype(BF)

    def by_seqs(rows):
        return swap_seqs(rows.reshape(tensor_size, seqs_here, part_len, model_width))

    n1_seqs = by_seqs(normed_local)
    seg_here = lax.dynamic_slice_in_dim(segment_ids, me * seqs_here, seqs_here, 0)
    bucket_onehot = (rel_bucket[:, None] == jnp.arange(bucket_count)[None, :]).astype(F32)
    bias_line = jnp.einsum(
        "kb,bh->hk", bucket_onehot, rel_table.astype(F32), precision=lax.Precision.HIGHEST
    )
    bias_line = jnp.pad(bias_line, ((0, 0), (1, 0))).reshape(heads_all, 2 * tiles, TILE)
    windows = jnp.concatenate([bias_line, jnp.roll(bias_line, -1, axis=1)], axis=2)
    windows = windows.reshape(tensor_size, heads_here, 2 * tiles, 2 * TILE)
    windows = jnp.take(windows, order, axis=0)

    route_rows = expert_route.reshape(tok_rows)
    slot_rows = expert_slot.reshape(tok_rows)
    slot_place = jnp.where(slot_rows >= 0, route_rows * capacity + slot_rows, buffer_size)
    slot_table = (slot_place[:, None] == jnp.arange(buffer_size)[None, :]).astype(BF)
    route_onehot = (route_rows[:, None] == jnp.arange(experts_all)[None, :]).astype(F32)

    def place_rows(rows):
        placed = jnp.einsum("tb,td->bd", slot_table, rows, preferred_element_type=F32)
        return placed.astype(BF).reshape(experts_all, capacity, model_width)

    def take_rows(buffer):
        return jnp.dot(
            slot_table, buffer.reshape(buffer_size, model_width), preferred_element_type=F32
        )

    cotangent_rows = cotangent.reshape(tok_rows, model_width)
    cotangent_arrived = swap_dp(place_rows(cotangent_rows)).reshape(buffer_size, model_width)
    first = gather_tensor(expert_in.reshape(model_width, -1))
    second = gather_tensor(expert_out.reshape(-1, model_width))

    branch, qkv, attended, probs = attend(
        n1_seqs, weights, seg_here, windows, heads_here, head_size
    )
    attn_branch = swap_seqs(branch).reshape(tok_rows, model_width).astype(F32)
    hidden_rows = flat_input.reshape(tok_rows, model_width) + attn_branch

    moe_gain_f = moe_gain.astype(F32)
    router_f = router_weight.astype(F32)
    rms = rms_inverse(hidden_rows)
    scaled = hidden_rows * rms
    normed_moe = scaled * moe_gain_f
    logits = jnp.dot(
        normed_moe, router_f, precision=lax.Precision.HIGHEST, preferred_element_type=F32
    )
    router_probs = jax.nn.softmax(logits, axis=-1)
    gate_value = jnp.sum(router_probs * route_onehot, axis=-1)

    arrived = swap_dp(place_rows(normed_moe.astype(BF))).reshape(buffer_size, model_width)
    slot_gate = jnp.sum(
        jnp.where(slot_place[:, None] == jnp.arange(buffer_size)[None, :], gate_value[:, None], 0.0),
        axis=0,
    )
    gate_arrived = swap_dp(slot_gate.reshape(experts_all, capacity)).reshape(buffer_size, 1)

    input_rows, gate_rows, hidden, pre_grad = run_experts(
        arrived, cotangent_arrived, first, second
    )
    input_back = swap_dp(input_rows.reshape(experts_all, capacity, model_width))
    gate_back = swap_dp(gate_rows.reshape(experts_all, capacity)).reshape(buffer_size)
    out_rows = jnp.einsum("krf,kfd->rd", hidden, second, preferred_element_type=F32).astype(BF)
    gated_c = (gate_arrived * cotangent_arrived.astype(F32)).astype(BF)
    gated_u = (gate_arrived * arrived.astype(F32)).astype(BF)
    second_terms = jnp.einsum("krf,rd->kfd", hidden, gated_c, preferred_element_type=F32).astype(BF)
    first_terms = jnp.einsum("rd,krf->kdf", gated_u, pre_grad, preferred_element_type=F32).astype(BF)
    second_grad = scatter_tensor(second_terms).reshape(expert_out.shape)
    first_grad = scatter_tensor(first_terms).reshape(expert_in.shape)

    out_grad = cotangent_rows.astype(F32)
    gate_grad = jnp.sum(
        jnp.where(slot_place[:, None] == jnp.arange(buffer_size)[None, :], gate_back[None, :], 0.0),
        axis=1,
    )
    logit_grad = (gate_grad * gate_value)[:, None] * (route_onehot - router_probs)
    router_part = lax.dot_general(
        normed_moe, logit_grad, TN, precision=lax.Precision.HIGHEST, preferred_element_type=F32
    )
    normed_grad = gate_value[:, None] * take_rows(input_back) + lax.dot_general(
        logit_grad, router_f, NT, precision=lax.Precision.HIGHEST, preferred_element_type=F32
    )
    moe_gain_part = jnp.sum(normed_grad * scaled, axis=0)
    gained = normed_grad * moe_gain_f
    residual_grad = (
        out_grad + rms * gained - scaled * rms * jnp.mean(gained * scaled, axis=-1, keepdims=True)
    )
    db_seqs = by_seqs(residual_grad.astype(BF))
    normed_back, weight_terms, line_sums, gain_sums = attend_back(
        n1_seqs, db_seqs, weights, qkv, attended, probs, heads_here, head_size
    )
    returned = swap_dp(out_rows.reshape(experts_all, capacity, model_width))
    block_output = (hidden_rows + gate_value[:, None] * take_rows(returned)).astype(BF)
    block_output = block_output.reshape(group_seqs, part_len, model_width)

    normed_back = swap_seqs(normed_back).reshape(group_seqs, part_len, model_width).astype(F32)
    gained_in = normed_back * attn_gain_f
    rms_in = rms_inverse(flat_input)
    scaled_in = flat_input * rms_in
    input_grad = (
        residual_grad.reshape(group_seqs, part_len, model_width)
        + rms_in * gained_in
        - scaled_in * rms_in * jnp.mean(gained_in * scaled_in, axis=-1, keepdims=True)
    )

    owner_terms = scatter_tensor(weight_terms).astype(BF)
    owner_terms = swap_dp(owner_terms.reshape(dp_size, weight_rows, 4 * head_cols))
    owner_grad = jnp.sum(owner_terms.astype(F32), axis=0)

    low, high = line_sums[..., :TILE], line_sums[..., TILE:]
    offset_sums = low + jnp.roll(high, 1, axis=2)
    offset_sums = offset_sums.reshape(heads_all, 2 * full_len)[:, 1:]
    table_part = jnp.einsum(
        "hk,kb->bh", offset_sums, bucket_onehot, precision=lax.Precision.HIGHEST
    ).reshape(bucket_count, tensor_size, heads_here)
    table_part = jnp.take(table_part, visits[me ^ jnp.arange(tensor_size)], axis=1).reshape(bucket_count, heads_all)
    attn_gain_grad, moe_gain_grad, router_grad, table_grad = lax.psum(
        (gain_sums[0] / attn_gain_f, moe_gain_part, router_part, table_part), ("dp", "tensor")
    )
    return (
        block_output,
        input_grad,
        attn_gain_grad,
        moe_gain_grad,
        router_grad,
        table_grad,
        owner_grad[:, :head_cols],
        owner_grad[:, head_cols : 2 * head_cols],
        owner_grad[:, 2 * head_cols : 3 * head_cols],
        owner_grad[:, 3 * head_cols :].T,
        first_grad,
        second_grad,
    )


def solution(mesh):
    in_specs = (
        P("dp", "tensor", None),
        P("dp", "tensor", None),
        P("dp", None),
        P(),
        P("dp", "tensor"),
        P("dp", "tensor"),
        P(),
        P(),
        P(),
        P(),
        P("dp", "tensor"),
        P("dp", "tensor"),
        P("dp", "tensor"),
        P("tensor", "dp"),
        P("dp", None, "tensor"),
        P("dp", "tensor", None),
    )
    out_specs = (
        P("dp", "tensor", None),
        P("dp", "tensor", None),
        P(),
        P(),
        P(),
        P(),
        P("dp", "tensor"),
        P("dp", "tensor"),
        P("dp", "tensor"),
        P("tensor", "dp"),
        P("dp", None, "tensor"),
        P("dp", "tensor", None),
    )
    return jax.shard_map(local, mesh=mesh, in_specs=in_specs, out_specs=out_specs, check_vma=False)
```

time: 2150 us -> 695 us (0.32)
  waiting for transfers between devices: 917 us -> 270 us
  local copies, waits for them, and re-layouts: 491 us -> 27 us
  matrix products: 317 us -> 78.8 us
  blocking collectives: 310 us -> 87.8 us
  Pallas kernels: 0 us -> 125 us
  starting transfers between devices: 12.4 us -> 50.2 us
  other arithmetic: 81 us -> 45.5 us
    reduce_scatter x4 -> x0, waiting for transfers between devices: 444 us -> none  [the longest x2 341 us: group_sums(): return lax.psum_scatter(terms, 'tensor', scatter_dimension=1, tiled=True)]
    dot_general x82 -> x10, matrix products: 304 us -> 64.1 us  [the longest x1 14.3 us: local(): jnp.einsum('krf,rd->kfd', hidden, gated_c, preferred_element_type=F32)]
    all_gather x4 -> x0, waiting for transfers between devices: 195 us -> none  [the longest x2 150 us: group_rows(): return lax.all_gather(buffer, 'tensor', axis=1, tiled=True)]
    unnamed x16 -> x0, waiting for transfers between devices: 149 us -> none
    while x137 -> x0, local copies, waits for them, and re-layouts: 146 us -> none
    rev x8 -> x0, local copies, waits for them, and re-layouts: 141 us -> none  [diagonal_sums(): flipped = square[:, ::-1, :]]
    ppermute x0 -> x12, waiting for transfers between devices: none -> 127 us  [swap_tensor(): return lax.ppermute(block, 'tensor', [(i, i ^ bit) for i in range(size)])]
    all_gather x4 -> x0, blocking collectives: 126 us -> none  [the longest x1 32.7 us: local(): lax.all_gather(w_query, 'dp', axis=0, tiled=True)]
  transfers between devices with their start and end apart: 14 -> 22, of which waited for: 12 -> 16; matrix products, arithmetic and copies ran while one was open for 31% -> 19% of each run, Pallas kernels for 0% -> 7%
where the time goes in v1:
time: 695 us; the launch traced here: 686 us
  waiting for transfers between devices  270 us (39%)
  Pallas kernels  125 us (18%)
  blocking collectives  87.8 us (13%)
  matrix products  78.8 us (11%)
  starting transfers between devices  50.2 us (7%)
  other arithmetic  45.5 us (7%)
  local copies, waits for them, and re-layouts  27 us (4%)
    ppermute x12, waiting for transfers between devices, swap_tensor(): return lax.ppermute(block, 'tensor', [(i, i ^ bit) for i in range(size)])  127 us
    all_to_all x6, waiting for transfers between devices, swap_dp(): return lax.all_to_all(buffer, 'dp', split_axis=0, concat_axis=0, tiled=True)  100 us
    pallas_call x1, Pallas kernels, attend_back(): pl.pallas_call(functools.partial(attend_back_kernel, heads, head_size), g...  48.5 us
    all_to_all x2, blocking collectives, swap_dp(): return lax.all_to_all(buffer, 'dp', split_axis=0, concat_axis=0, tiled=True)  44.9 us
    all_to_all x4, waiting for transfers between devices, swap_seqs(): lax.all_to_all(buffer, 'tensor', split_axis=0, concat_axis=0, tiled=True)  43.5 us
    psum x1, blocking collectives, local(): lax.psum((gain_sums[0] / attn_gain_f, moe_gain_part, router_part, table_p...  42.9 us
    pallas_call x1, Pallas kernels, run_experts(): pl.pallas_call(expert_kernel, grid=(rows // block, chunks), in_specs=[pl....  42.7 us
    pallas_call x1, Pallas kernels, attend(): pl.pallas_call(functools.partial(attend_kernel, heads, head_size), grid=(...  33.9 us
  transfers between devices with their start and end apart: 22, of which 16 were waited for; matrix products, arithmetic and copies ran while one was open for 19% of the time, Pallas kernels for 7%

profile of v1, /device:TPU:0, one launch (start us, length us, event | category | flops | bytes accessed | tf_op | source)
XLA Modules:
  0.0 686.4 jit_solution(12756583295903690298)
XLA Ops:
  4.5 36.0 %all_to_all.69 = bf16[8,96,768]{2,1,0:T(8,128)(2,1)S(1)} all-to-all(bf16[8,96,768]{2,1,0:T(8,128)(2,1)S(1)} %broadcast_in_dim.57), channel_id=1, replica_groups=mesh['dp'=8,'tensor'=4] {'dp'}, dimensions={0} | all-to-all | bytes 2359296 | tf_op jit(solution)/shard_map/all_to_all | solution.py:353
  42.0 24.6 %collective-permute-done = bf16[768,768]{1,0:T(8,128)(2,1)S(1)} collective-permute-done((bf16[768,768]{1,0:T(8,128)(2,1)S(1)}, bf16[768,768]{1,0:T(8,128)(2,1)S(1)}, u32[]{:S(2)}, u32[]{:S(2)}) %collective-permute-start) | collective-permute-done | bytes 1179680 | tf_op jit(solution)/shard_map/ppermute | solution.py:337
  70.4 3.7 all-to-all-start
  75.6 3.8 pad_maximum_fusion.w_ref
  79.4 14.7 %all-to-all-done.n1_ref = bf16[4,2,128,768]{3,2,1,0:T(8,128)(2,1)S(1)} async-done(((bf16[4,2,128,768]{3,2,1,0:T(8,128)(2,1)}), bf16[4,2,128,768]{3,2,1,0:T(8,128)(2,1)S(1)}, u32[]{:S(2)}, u32[]{:S(2)}) %all-to-all-start) | async-done | bytes 1572896 | tf_op jit(solution)/shard_map/all_to_all | solution.py:357
  94.1 33.9 %attend.1 = (bf16[4,2,128,768]{3,2,1,0:T(8,128)(2,1)}, bf16[4,2,512,576]{3,2,1,0:T(8,128)(2,1)}, bf16[4,2,512,192]{3,2,1,0:T(8,128)(2,1)S(1)}, bf16[4,2,3,512,512]{4,3,2,1,0:T(8,128)(2,1)}) custom-call(bf16[4,2,128,768]{3,2,1,0:T(8,128)(2,1)S(1)} %all-to-all-done.n1_ref, bf16[4,768,768]{2,1,0:T(8,128)(2,1)} %pad_maximum_fusion.w_ref, ...), custom_call_target="tpu_custom_call" | custom-call | flops 38654705664 | bytes 25165824 | tf_op jit(solution)/shard_map/attend/pallas_call | solution.py:224
  129.4 3.7 all-to-all-start.2
  133.1 5.8 fusion.9
  138.9 14.2 %all-to-all-done.2 = bf16[4,2,128,768]{3,2,1,0:T(8,128)(2,1)S(1)} async-done(((bf16[4,2,128,768]{3,2,1,0:T(8,128)(2,1)}), bf16[4,2,128,768]{3,2,1,0:T(8,128)(2,1)S(1)}, u32[]{:S(2)}, u32[]{:S(2)}) %all-to-all-start.2) | async-done | bytes 1572896 | tf_op jit(solution)/shard_map/all_to_all | solution.py:357
  153.2 5.1 all-to-all-start.4
  160.9 6.0 fusion.8
  166.9 57.7 %all-to-all-done.4 = bf16[8,240,768]{2,1,0:T(8,128)(2,1)} async-done(((bf16[8,240,768]{2,1,0:T(8,128)(2,1)}), bf16[8,240,768]{2,1,0:T(8,128)(2,1)}, u32[]{:S(2)}, u32[]{:S(2)}) %all-to-all-start.4) | async-done | bytes 2949152 | tf_op jit(solution)/shard_map/all_to_all | solution.py:353
  224.6 4.6 all-to-all-start.3
  231.3 26.9 %collective-permute-done.2 = bf16[768,768]{1,0:T(8,128)(2,1)S(1)} collective-permute-done((bf16[768,768]{1,0:T(8,128)(2,1)S(1)}, bf16[768,768]{1,0:T(8,128)(2,1)S(1)}, u32[]{:S(2)}, u32[]{:S(2)}) %collective-permute-start.2) | collective-permute-done | bytes 1179680 | tf_op jit(solution)/shard_map/ppermute | solution.py:337
  258.5 22.8 %collective-permute-done.4 = bf16[768,768]{1,0:T(8,128)(2,1)S(1)} collective-permute-done((bf16[768,768]{1,0:T(8,128)(2,1)}, bf16[768,768]{1,0:T(8,128)(2,1)S(1)}, u32[]{:S(2)}, u32[]{:S(2)}) %collective-permute-start.4) | collective-permute-done | bytes 1179680 | tf_op jit(solution)/shard_map/ppermute | solution.py:337
  290.9 4.3 all-to-all-done.3
  295.1 42.7 %experts.1 = (bf16[1920,768]{1,0:T(8,128)(2,1)}, f32[1920,1]{1,0:T(8,128)S(1)}, bf16[4,1920,768]{2,1,0:T(8,128)(2,1)}, bf16[4,1920,768]{2,1,0:T(8,128)(2,1)}) custom-call(bf16[1920,768]{1,0:T(8,128)(2,1)} %bitcast.15.u_ref, bf16[1920,768]{1,0:T(8,128)(2,1)} %bitcast.18.c_ref, bf16[4,768,768]{2,1,0:T(8,128)(2,1)} %pad_maximum_fusion.1.wi_ref, ...), custom_call_target="tpu_custom_call" | custom-call | flops 27179089920 | bytes 62914560 | tf_op jit(solution)/shard_map/experts/pallas_call | solution.py:305
  338.9 3.9 all-to-all-start.7
  342.8 6.4 all-to-all-done.7
  351.7 8.9 %all_to_all.70 = f32[8,1,240]{2,1,0:T(1,128)S(1)} all-to-all(f32[8,1,240]{2,1,0:T(1,128)S(1)} %all_to_all.54), channel_id=1, replica_groups=mesh['dp'=8,'tensor'=4] {'dp'}, dimensions={0} | all-to-all | bytes 15360 | tf_op jit(solution)/shard_map/all_to_all | solution.py:353
  360.6 4.6 all-to-all-start.6
  365.2 14.3 %bitcast_convert_fusion = bf16[1920,768]{1,0:T(8,128)(2,1)} fusion(bf16[4,1920,768]{2,1,0:T(8,128)(2,1)} %get-tuple-element.25, bf16[2,768,768]{2,1,0:T(8,128)(2,1)} %copy-done.20, bf16[1,768,768]{2,1,0:T(8,128)(2,1)} %bitcast.147, bf16[1,768,768]{2,1,0:T(8,128)(2,1)S(1)} %copy-done.15), kind=kOutput, calls=%fused_computation.10 | convolution fusion | flops 9065889792 | bytes 19464192 | tf_op jit(solution)/shard_map/krf,kfd->rd/dot_general | solution.py:470
  379.4 3.1 fusion.54
  382.6 14.3 %convert_bitcast_fusion = bf16[4,768,768]{1,2,0:T(8,128)(2,1)S(1)} fusion(bf16[4,1920,768]{2,1,0:T(8,128)(2,1)} %get-tuple-element.35, bf16[1920,768]{1,0:T(8,128)(2,1)} %bitcast.15.u_ref, f32[1920]{0:T(1024)S(1)} %mul.199), kind=kOutput, calls=%fused_computation.16 | convolution fusion | flops 9066479616 | bytes 19471872 | tf_op jit(solution)/shard_map/rd,krf->kdf/dot_general | solution.py:474
  400.6 29.0 %all-to-all-done.6 = bf16[8,240,768]{2,1,0:T(8,128)(2,1)} async-done(((bf16[8,240,768]{2,1,0:T(8,128)(2,1)}), bf16[8,240,768]{2,1,0:T(8,128)(2,1)}, u32[]{:S(2)}, u32[]{:S(2)}) %all-to-all-start.6) | async-done | bytes 2949152 | tf_op jit(solution)/shard_map/all_to_all | solution.py:353
  429.5 7.5 %multiply_reduce_fusion = (f32[768]{0:T(1024)S(1)}, f32[1024]{0:T(1024)S(1)}, f32[1024,768]{1,0:T(8,128)S(1)}) fusion(f32[1024]{0:T(1024)S(1)} %rsqrt_bitcast_fusion, bf16[4,2,128,768]{3,2,1,0:T(8,128)(2,1)S(1)} %copy-done.11, bf16[8,128,768]{2,1,0:T(8,128)(2,1)S(1)} %copy-done.7, f32[768]{0:T(1024)S(1)} %convert_element_type.169, f32[1024,768]{1,0:T(8,128)} %fusion.54, ...), kind=kOutput, calls=%fused_computation.33 | convolution fusion | flops 3030513920 | bytes 12408832 | tf_op jit(solution)/shard_map/dot_general | solution.py:432
  437.1 3.0 fusion.64
  440.1 3.6 all-to-all-start.8
  443.7 14.3 %fusion.25 = bf16[4,768,768]{2,1,0:T(8,128)(2,1)S(1)} fusion(bf16[4,1920,768]{2,1,0:T(8,128)(2,1)} %get-tuple-element.25, bf16[1920,768]{1,0:T(8,128)(2,1)} %bitcast.18.c_ref, f32[1920]{0:T(1024)S(1)} %mul.199), kind=kOutput, calls=%fused_computation.46 | convolution fusion | flops 9066479616 | bytes 19471872 | tf_op jit(solution)/shard_map/krf,rd->kfd/dot_general | solution.py:473
  464.9 4.6 all-to-all-start.5
  469.5 48.5 %attend_back.1 = (bf16[4,2,128,768]{3,2,1,0:T(8,128)(2,1)}, bf16[4,768,768]{2,1,0:T(8,128)(2,1)}, f32[4,3,8,256]{3,2,1,0:T(8,128)}, f32[1,768]{1,0:T(1,128)}) custom-call(bf16[4,2,128,768]{3,2,1,0:T(8,128)(2,1)} %copy-done.2, bf16[4,2,128,768]{3,2,1,0:T(8,128)(2,1)} %copy-done.23, bf16[4,768,768]{2,1,0:T(8,128)(2,1)} %pad_maximum_fusion.w_ref, ...), custom_call_target="tpu_custom_call" | custom-call | flops 77309411328 | bytes 33554432 | tf_op jit(solution)/shard_map/attend_back/pallas_call | solution.py:264
  518.1 3.2 slice.89
  522.0 2.9 fusion.46
  525.3 2.9 fusion.47
  529.9 2.9 fusion.45
  536.1 3.6 all-to-all-start.9
  539.7 3.9 fusion.30
  543.5 10.4 %collective-permute-done.9 = bf16[768,768]{0,1:T(8,128)(2,1)} collective-permute-done((bf16[768,768]{0,1:T(8,128)(2,1)}, bf16[768,768]{0,1:T(8,128)(2,1)}, u32[]{:S(2)}, u32[]{:S(2)}) %collective-permute-start.9) | collective-permute-done | bytes 1179680 | tf_op jit(solution)/shard_map/ppermute | solution.py:337
  554.0 3.8 fusion.35
  557.7 3.0 copy.69
  560.8 18.5 %collective-permute-done.11 = bf16[768,768]{1,0:T(8,128)(2,1)} collective-permute-done((bf16[768,768]{1,0:T(8,128)(2,1)}, bf16[768,768]{1,0:T(8,128)(2,1)}, u32[]{:S(2)}, u32[]{:S(2)}) %collective-permute-start.11) | collective-permute-done | bytes 1179680 | tf_op jit(solution)/shard_map/ppermute | solution.py:337
  579.3 3.8 fusion.34
  583.0 21.5 %collective-permute-done.7 = bf16[768,768]{1,0:T(8,128)(2,1)} collective-permute-done((bf16[768,768]{1,0:T(8,128)(2,1)}, bf16[768,768]{1,0:T(8,128)(2,1)}, u32[]{:S(2)}, u32[]{:S(2)}) %collective-permute-start.7) | collective-permute-done | bytes 1179680 | tf_op jit(solution)/shard_map/ppermute | solution.py:337
  604.5 3.4 fusion.36
  608.0 12.9 %all-to-all-done.9 = bf16[4,2,128,768]{3,2,1,0:T(8,128)(2,1)S(1)} async-done(((bf16[4,2,128,768]{3,2,1,0:T(8,128)(2,1)}), bf16[4,2,128,768]{3,2,1,0:T(8,128)(2,1)S(1)}, u32[]{:S(2)}, u32[]{:S(2)}) %all-to-all-start.9) | async-done | bytes 1572896 | tf_op jit(solution)/shard_map/all_to_all | solution.py:357
  620.9 6.2 all-to-all-start.10
  627.2 7.3 %add_convert_fusion = bf16[1024,768]{1,0:T(8,128)(2,1)} fusion(f32[1024,768]{1,0:T(8,128)} %copy-done.8, bf16[1920,768]{1,0:T(8,128)(2,1)} %bitcast.25, s32[1024]{0:T(1024)S(1)} %fusion.59, f32[1024]{0:T(1024)S(1)} %select_reduce_fusion.2), kind=kOutput, calls=%fused_computation.37 | convolution fusion | flops 3024224256 | bytes 7675904 | tf_op jit(solution)/shard_map/dot_general | solution.py:432
  635.7 42.9 %all-reduce.1 = (f32[768]{0:T(1024)}, f32[768]{0:T(1024)}, f32[768,8]{0,1:T(8,128)}, f32[32,12]{0,1:T(8,128)}) all-reduce(f32[768]{0:T(1024)S(1)} %convert_divide_fusion, f32[768]{0:T(1024)S(1)} %get-tuple-element.84, f32[768,8]{0,1:T(8,128)S(1)} %fusion.30, ...), channel_id=1, replica_groups=mesh['dp'=8,'tensor'=4] {'dp','tensor'}, use_global_device_ids=true, to_apply=%region_8.9 | all-reduce | flops 8064 | bytes 64512 | tf_op jit(solution)/shard_map/psum | solution.py:524
  (176 shorter events, 55.2 us)
Async XLA Ops:
  0.6 74.0 %copy-start = (s32[8,512]{1,0:T(8,128)S(1)}, s32[8,512]{1,0:T(8,128)}, u32[]{:S(2)}) copy-start(s32[8,512]{1,0:T(8,128)} %param.19) | copy-start | bytes 49156
  40.5 27.9 %copy-start.31 = (bf16[768]{0:T(1024)(128)(2,1)S(1)}, bf16[768]{0:T(1024)(128)(2,1)}, u32[]{:S(2)}) copy-start(bf16[768]{0:T(1024)(128)(2,1)} %param.23) | copy-start | bytes 4612
  40.5 27.9 %copy-start.6 = (bf16[8,128,768]{2,1,0:T(8,128)(2,1)S(1)}, bf16[8,128,768]{2,1,0:T(8,128)(2,1)}, u32[]{:S(2)}) copy-start(bf16[8,128,768]{2,1,0:T(8,128)(2,1)} %param.17) | copy-start | bytes 4718596
  40.5 26.1 %collective-permute-start = (bf16[768,768]{1,0:T(8,128)(2,1)S(1)}, bf16[768,768]{1,0:T(8,128)(2,1)S(1)}, u32[]{:S(2)}, u32[]{:S(2)}) collective-permute-start(bf16[768,768]{1,0:T(8,128)(2,1)S(1)} %bitcast.138), channel_id=1, source_target_pairs={{0,2},{1,3},{2,0},{3,1},{4,6},{5,7},{6,4},{7,5},{8,10},{9,11},{10,... | collective-permute-start | bytes 3538952 | tf_op jit(solution)/shard_map/ppermute | solution.py:337
  68.3 7.3 %collective-permute-start.1 = (bf16[2,768,768]{2,1,0:T(8,128)(2,1)}, bf16[2,768,768]{2,1,0:T(8,128)(2,1)}, u32[]{:S(2)}, u32[]{:S(2)}) collective-permute-start(bf16[2,768,768]{2,1,0:T(8,128)(2,1)} %pad_maximum_fusion.3), channel_id=1, source_target_pairs={{0,1},{1,0},{2,3},{3,2},{4,5},{5,4},{6,7},{7,6},{8,9},{9,8},{10,11... | collective-permute-start | bytes 7077896 | tf_op jit(solution)/shard_map/ppermute | solution.py:337
  68.8 5.3 copy-start.36
  68.8 5.3 copy-start.37
  70.4 4.5 copy-start.4
  70.4 23.8 %all-to-all-start = ((bf16[4,2,128,768]{3,2,1,0:T(8,128)(2,1)}), bf16[4,2,128,768]{3,2,1,0:T(8,128)(2,1)S(1)}, u32[]{:S(2)}, u32[]{:S(2)}) async-start(bf16[4,2,128,768]{3,2,1,0:T(8,128)(2,1)} %bitcast.141), calls=%async_computation | async-start | bytes 3145728 | tf_op jit(solution)/shard_map/all_to_all | solution.py:357
  94.1 33.9 %copy-start.2 = (bf16[4,2,128,768]{3,2,1,0:T(8,128)(2,1)}, bf16[4,2,128,768]{3,2,1,0:T(8,128)(2,1)S(1)}, u32[]{:S(2)}) copy-start(bf16[4,2,128,768]{3,2,1,0:T(8,128)(2,1)S(1)} %all-to-all-done.n1_ref) | copy-start | bytes 4718596
  129.4 3.7 copy-start.21
  129.4 23.7 %all-to-all-start.2 = ((bf16[4,2,128,768]{3,2,1,0:T(8,128)(2,1)}), bf16[4,2,128,768]{3,2,1,0:T(8,128)(2,1)S(1)}, u32[]{:S(2)}, u32[]{:S(2)}) async-start(bf16[4,2,128,768]{3,2,1,0:T(8,128)(2,1)} %get-tuple-element.24), calls=%async_computation.2 | async-start | bytes 3145728 | tf_op jit(solution)/shard_map/all_to_all | solution.py:357
  153.2 5.8 copy-start.10
  153.2 5.1 copy-start.35
  153.2 5.2 copy-start.7
  153.2 71.5 %all-to-all-start.4 = ((bf16[8,240,768]{2,1,0:T(8,128)(2,1)}), bf16[8,240,768]{2,1,0:T(8,128)(2,1)}, u32[]{:S(2)}, u32[]{:S(2)}) async-start(bf16[8,240,768]{2,1,0:T(8,128)(2,1)} %bitcast.155), calls=%async_computation.4 | async-start | bytes 5898240 | tf_op jit(solution)/shard_map/all_to_all | solution.py:353
  224.6 4.6 copy-start.13
  224.6 70.5 %all-to-all-start.3 = ((bf16[8,240,768]{2,1,0:T(8,128)(2,1)}), bf16[8,240,768]{2,1,0:T(8,128)(2,1)}, u32[]{:S(2)}, u32[]{:S(2)}) async-start(bf16[8,240,768]{2,1,0:T(8,128)(2,1)} %bitcast.154), calls=%async_computation.3 | async-start | bytes 5898240 | tf_op jit(solution)/shard_map/all_to_all | solution.py:353
  229.2 52.1 %copy-start.14 = (bf16[1,768,768]{2,1,0:T(8,128)(2,1)S(1)}, bf16[1,768,768]{2,1,0:T(8,128)(2,1)}, u32[]{:S(2)}) copy-start(bf16[1,768,768]{2,1,0:T(8,128)(2,1)} %param.32) | copy-start | bytes 3538948
  229.2 29.0 %collective-permute-start.2 = (bf16[768,768]{1,0:T(8,128)(2,1)S(1)}, bf16[768,768]{1,0:T(8,128)(2,1)S(1)}, u32[]{:S(2)}, u32[]{:S(2)}) collective-permute-start(bf16[768,768]{1,0:T(8,128)(2,1)S(1)} %bitcast.143), channel_id=1, source_target_pairs={{0,2},{1,3},{2,0},{3,1},{4,6},{5,7},{6,4},{7,5},{8,10},{9,11},{10,... | collective-permute-start | bytes 3538952 | tf_op jit(solution)/shard_map/ppermute | solution.py:337
  229.9 51.4 %collective-permute-start.4 = (bf16[768,768]{1,0:T(8,128)(2,1)}, bf16[768,768]{1,0:T(8,128)(2,1)S(1)}, u32[]{:S(2)}, u32[]{:S(2)}) collective-permute-start(bf16[768,768]{1,0:T(8,128)(2,1)} %bitcast.144), channel_id=1, source_target_pairs={{0,2},{1,3},{2,0},{3,1},{4,6},{5,7},{6,4},{7,5},{8,10},{9,11},{10,... | collective-permute-start | bytes 3538952 | tf_op jit(solution)/shard_map/ppermute | solution.py:337
  258.4 23.2 %collective-permute-start.3 = (bf16[2,768,768]{2,1,0:T(8,128)(2,1)S(1)}, bf16[2,768,768]{2,1,0:T(8,128)(2,1)S(1)}, u32[]{:S(2)}, u32[]{:S(2)}) collective-permute-start(bf16[2,768,768]{2,1,0:T(8,128)(2,1)S(1)} %pad_maximum_fusion.4), channel_id=1, source_target_pairs={{0,1},{1,0},{2,3},{3,2},{4,5},{5,4},{6,7},{7,6},{8,9},{9,8},{10,11... | collective-permute-start | bytes 7077896 | tf_op jit(solution)/shard_map/ppermute | solution.py:337
  281.3 4.8 copy-start.16
  281.5 4.6 collective-permute-start.5
  284.1 4.9 copy-start.9
  284.1 4.9 copy-start.30
  338.9 10.3 %all-to-all-start.7 = ((f32[8,1,240]{2,1,0:T(1,128)}), f32[8,1,240]{2,1,0:T(1,128)S(1)}, u32[]{:S(2)}, u32[]{:S(2)}) async-start(f32[8,1,240]{2,1,0:T(1,128)} %all_to_all.56), calls=%async_computation.7 | async-start | bytes 16384 | tf_op jit(solution)/shard_map/all_to_all | solution.py:353
  360.5 4.6 copy-start.15
  360.6 69.0 %all-to-all-start.6 = ((bf16[8,240,768]{2,1,0:T(8,128)(2,1)}), bf16[8,240,768]{2,1,0:T(8,128)(2,1)}, u32[]{:S(2)}, u32[]{:S(2)}) async-start(bf16[8,240,768]{2,1,0:T(8,128)(2,1)} %bitcast.27), calls=%async_computation.6 | async-start | bytes 5898240 | tf_op jit(solution)/shard_map/all_to_all | solution.py:353
  399.0 30.5 %copy-start.11 = (bf16[4,2,128,768]{3,2,1,0:T(8,128)(2,1)S(1)}, bf16[4,2,128,768]{3,2,1,0:T(8,128)(2,1)}, u32[]{:S(2)}) copy-start(bf16[4,2,128,768]{3,2,1,0:T(8,128)(2,1)} %copy-done.10) | copy-start | bytes 4718596
  400.6 121.4 %collective-permute-start.8 = (bf16[2,768,768]{1,2,0:T(8,128)(2,1)}, bf16[2,768,768]{1,2,0:T(8,128)(2,1)}, u32[]{:S(2)}, u32[]{:S(2)}) collective-permute-start(bf16[2,768,768]{1,2,0:T(8,128)(2,1)} %slice.123), channel_id=1, source_target_pairs={{0,1},{1,0},{2,3},{3,2},{4,5},{5,4},{6,7},{7,6},{8,9},{9,8},{10,11... | collective-permute-start | bytes 7077896 | tf_op jit(solution)/shard_map/ppermute | solution.py:337
  429.5 7.6 %copy-start.22 = (bf16[8,128,768]{2,1,0:T(8,128)(2,1)S(1)}, bf16[8,128,768]{2,1,0:T(8,128)(2,1)}, u32[]{:S(2)}) copy-start(bf16[8,128,768]{2,1,0:T(8,128)(2,1)} %param.18) | copy-start | bytes 4718596
  440.1 23.6 %all-to-all-start.8 = ((bf16[4,2,128,768]{3,2,1,0:T(8,128)(2,1)}), bf16[4,2,128,768]{3,2,1,0:T(8,128)(2,1)S(1)}, u32[]{:S(2)}, u32[]{:S(2)}) async-start(bf16[4,2,128,768]{3,2,1,0:T(8,128)(2,1)} %bitcast.142), calls=%async_computation.8 | async-start | bytes 3145728 | tf_op jit(solution)/shard_map/all_to_all | solution.py:357
  461.7 63.6 %collective-permute-start.10 = (bf16[2,768,768]{2,1,0:T(8,128)(2,1)}, bf16[2,768,768]{2,1,0:T(8,128)(2,1)}, u32[]{:S(2)}, u32[]{:S(2)}) collective-permute-start(bf16[2,768,768]{2,1,0:T(8,128)(2,1)} %slice.128), channel_id=1, source_target_pairs={{0,1},{1,0},{2,3},{3,2},{4,5},{5,4},{6,7},{7,6},{8,9},{9,8},{10,11... | collective-permute-start | bytes 7077896 | tf_op jit(solution)/shard_map/ppermute | solution.py:337
  464.9 71.2 %all-to-all-start.5 = ((bf16[8,240,768]{2,1,0:T(8,128)(2,1)}), bf16[8,240,768]{2,1,0:T(8,128)(2,1)}, u32[]{:S(2)}, u32[]{:S(2)}) async-start(bf16[8,240,768]{2,1,0:T(8,128)(2,1)} %bitcast.153), calls=%async_computation.5 | async-start | bytes 5898240 | tf_op jit(solution)/shard_map/all_to_all | solution.py:353
  521.3 8.6 %collective-permute-start.6 = (bf16[2,768,768]{2,1,0:T(8,128)(2,1)}, bf16[2,768,768]{2,1,0:T(8,128)(2,1)}, u32[]{:S(2)}, u32[]{:S(2)}) collective-permute-start(bf16[2,768,768]{2,1,0:T(8,128)(2,1)} %slice.89), channel_id=1, source_target_pairs={{0,1},{1,0},{2,3},{3,2},{4,5},{5,4},{6,7},{7,6},{8,9},{9,8},{10,11... | collective-permute-start | bytes 7077896 | tf_op jit(solution)/shard_map/ppermute | solution.py:337
  524.9 29.1 %collective-permute-start.9 = (bf16[768,768]{0,1:T(8,128)(2,1)}, bf16[768,768]{0,1:T(8,128)(2,1)}, u32[]{:S(2)}, u32[]{:S(2)}) collective-permute-start(bf16[768,768]{0,1:T(8,128)(2,1)} %fusion.46), channel_id=1, source_target_pairs={{0,2},{1,3},{2,0},{3,1},{4,6},{5,7},{6,4},{7,5},{8,10},{9,11},{10,... | collective-permute-start | bytes 3538952 | tf_op jit(solution)/shard_map/ppermute | solution.py:337
  528.3 51.0 %collective-permute-start.11 = (bf16[768,768]{1,0:T(8,128)(2,1)}, bf16[768,768]{1,0:T(8,128)(2,1)}, u32[]{:S(2)}, u32[]{:S(2)}) collective-permute-start(bf16[768,768]{1,0:T(8,128)(2,1)} %fusion.47), channel_id=1, source_target_pairs={{0,2},{1,3},{2,0},{3,1},{4,6},{5,7},{6,4},{7,5},{8,10},{9,11},{10,... | collective-permute-start | bytes 3538952 | tf_op jit(solution)/shard_map/ppermute | solution.py:337
  532.8 71.7 %collective-permute-start.7 = (bf16[768,768]{1,0:T(8,128)(2,1)}, bf16[768,768]{1,0:T(8,128)(2,1)}, u32[]{:S(2)}, u32[]{:S(2)}) collective-permute-start(bf16[768,768]{1,0:T(8,128)(2,1)} %fusion.45), channel_id=1, source_target_pairs={{0,2},{1,3},{2,0},{3,1},{4,6},{5,7},{6,4},{7,5},{8,10},{9,11},{10,... | collective-permute-start | bytes 3538952 | tf_op jit(solution)/shard_map/ppermute | solution.py:337
  536.1 84.8 %all-to-all-start.9 = ((bf16[4,2,128,768]{3,2,1,0:T(8,128)(2,1)}), bf16[4,2,128,768]{3,2,1,0:T(8,128)(2,1)S(1)}, u32[]{:S(2)}, u32[]{:S(2)}) async-start(bf16[4,2,128,768]{3,2,1,0:T(8,128)(2,1)} %get-tuple-element.31), calls=%async_computation.9 | async-start | bytes 3145728 | tf_op jit(solution)/shard_map/all_to_all | solution.py:357
  620.9 62.3 %all-to-all-start.10 = ((bf16[8,96,768]{2,1,0:T(8,128)(2,1)}), bf16[8,96,768]{2,1,0:T(8,128)(2,1)}, u32[]{:S(2)}, u32[]{:S(2)}) async-start(bf16[8,96,768]{2,1,0:T(8,128)(2,1)} %bitcast.152), calls=%async_computation.10 | async-start | bytes 2359296 | tf_op jit(solution)/shard_map/all_to_all | solution.py:353
  627.1 7.3 %copy-start.24 = (f32[4,3,8,256]{3,2,1,0:T(8,128)S(1)}, f32[4,3,8,256]{3,2,1,0:T(8,128)}, u32[]{:S(2)}) copy-start(f32[4,3,8,256]{3,2,1,0:T(8,128)} %get-tuple-element.33) | copy-start | bytes 294916
  627.1 7.4 %copy-start.34 = (f32[1,768]{1,0:T(1,128)S(1)}, f32[1,768]{1,0:T(1,128)}, u32[]{:S(2)}) copy-start(f32[1,768]{1,0:T(1,128)} %get-tuple-element.32) | copy-start | bytes 9220
  627.2 7.4 %copy-start.38 = (s32[1023]{0:T(1024)S(1)}, s32[1023]{0:T(1024)}, u32[]{:S(2)}) copy-start(s32[1023]{0:T(1024)} %param.20) | copy-start | bytes 12280
  627.2 8.4 %copy-start.32 = (bf16[768]{0:T(1024)(128)(2,1)S(1)}, bf16[768]{0:T(1024)(128)(2,1)}, u32[]{:S(2)}) copy-start(bf16[768]{0:T(1024)(128)(2,1)} %param.23) | copy-start | bytes 4612
  627.2 51.4 %copy-start.26 = (f32[768]{0:T(1024)S(1)}, f32[768]{0:T(1024)}, u32[]{:S(2)}) copy-start(f32[768]{0:T(1024)} %copy-done.25) | copy-start | bytes 9220
  627.2 51.4 %copy-start.28 = (f32[8,128]{1,0:T(8,128)S(1)}, f32[8,128]{1,0:T(8,128)}, u32[]{:S(2)}) copy-start(f32[8,128]{1,0:T(8,128)} %copy-done.27) | copy-start | bytes 12292
  680.5 5.7 copy-start.1
  (13 other events, 29.6 us)

commit v2 on v1

v2 whole, which is shorter than its diff:
```python
import functools

import jax
import jax.numpy as jnp
from jax import lax
from jax.experimental import pallas as pl
from jax.experimental.pallas import tpu as pltpu
from jax.sharding import PartitionSpec as P

EPSILON = 1e-06
MASKED_SCORE = -1e30
BF = jnp.bfloat16
F32 = jnp.float32
TILE = 128
NT = (((1,), (1,)), ((), ()))
TN = (((0,), (0,)), ((), ()))


def rms_inverse(values):
    return lax.rsqrt(jnp.mean(values * values, axis=-1, keepdims=True) + EPSILON)


def attn_norm(tokens_in, gain):
    return tokens_in * rms_inverse(tokens_in) * gain


def matmul(left, right, dims=None):
    if dims is None:
        dims = (((1,), (0,)), ((), ()))
    return lax.dot_general(left, right, dims, preferred_element_type=F32)


def head_only(rows, head, head_size):
    lane = lax.broadcasted_iota(jnp.int32, rows.shape, 1)
    inside = (lane >= head * head_size) & (lane < (head + 1) * head_size)
    return jnp.where(inside, rows, jnp.zeros_like(rows))


def attend_kernel(heads, head_size, has_base, last, *refs):
    me_ref, n1_ref, segc_ref, segr_ref, line_ref = refs[:5]
    w_refs, refs = refs[5:7], refs[7:]
    if has_base:
        base_ref, refs = refs[0], refs[1:]
    if last:
        out_refs, refs = refs[:4], refs[4:]
        refs, total_all = refs[:-1], refs[-1]
    else:
        out_ref, refs = refs[0], refs[1:]
    qkv_ref, o_ref, p_ref, bias_ref = refs
    seq = pl.program_id(0)
    width = heads * head_size
    model = n1_ref.shape[-1]
    length = segr_ref.shape[-1]
    tiles = length // TILE

    @pl.when(seq == 0)
    def _():
        for group in range(2):
            for head in range(heads):
                for d in range(2 * tiles - 1):
                    line = jnp.broadcast_to(line_ref[group, head, d : d + 1, :], (TILE, 2 * TILE))
                    tile = pltpu.roll(line, 0, 1, stride=1, stride_axis=0)[:, TILE:]
                    bias_ref[group, head, d] = tile

    rows = n1_ref[:, 0].reshape(length, model)
    seg_row = segr_ref[0]
    branch = None
    for group in range(2):
        qkv = matmul(rows, w_refs[group][:, : 3 * width]).astype(BF)
        qkv_ref[group, 0] = qkv
        queries, keys, values = qkv[:, :width], qkv[:, width : 2 * width], qkv[:, 2 * width :]
        attended = jnp.zeros((length, width), F32)
        for head in range(heads):
            scores = matmul(head_only(queries, head, head_size), keys, NT)
            for t in range(tiles):
                span = slice(t * TILE, (t + 1) * TILE)
                bias = jnp.concatenate(
                    [bias_ref[group, head, c - t + tiles - 1] for c in range(tiles)], axis=1
                )
                same_doc = segc_ref[0, span] == seg_row
                part = jnp.where(same_doc, scores[span] + bias, MASKED_SCORE)
                peak = jnp.max(part, axis=1, keepdims=True)
                expo = jnp.exp(part - peak)
                total = jnp.sum(expo, axis=1, keepdims=True)
                p_ref[group, 0, head, span] = (expo * (1.0 / total)).astype(BF)
            attended += matmul(p_ref[group, 0, head], head_only(values, head, head_size))
        attended = attended.astype(BF)
        o_ref[group, 0] = attended
        term = matmul(attended, w_refs[group][:, 3 * width :], NT)
        branch = term if branch is None else branch + term
    if has_base:
        branch = branch + base_ref[0]
    if last:
        total_all[...] = branch
        part_len = n1_ref.shape[2]
        for k in range(4):
            start = pl.multiple_of((me_ref[0] ^ k) * part_len, part_len)
            out_refs[k][0] = total_all[pl.ds(start, part_len)].astype(BF)
    else:
        out_ref[0] = branch


def attend_back_kernel(heads, head_size, has_base, last, *refs):
    me_ref, n1_ref, qkv_ref, o_ref, p_ref = refs[:5]
    w_refs, db_refs, refs = refs[5:7], refs[7:11], refs[11:]
    if has_base:
        base_ref, refs = refs[0], refs[1:]
    if last:
        out_refs, refs = refs[:4], refs[4:]
    else:
        out_ref, refs = refs[0], refs[1:]
    dw_refs, line_ref, refs = refs[:2], refs[2], refs[3:]
    if last:
        gain_ref, refs = refs[0], refs[1:]
    dw_acc, sums_ref, db_all, total_all = refs
    seq = pl.program_id(0)
    part_len = n1_ref.shape[2]

    def place_of(k):
        return pl.ds(pl.multiple_of((me_ref[0] ^ k) * part_len, part_len), part_len)

    for k in range(4):
        db_all[place_of(k)] = db_refs[k][0]
    width = heads * head_size
    model = n1_ref.shape[-1]
    length = qkv_ref.shape[2]
    tiles = length // TILE
    rows = n1_ref[:, 0].reshape(length, model)
    branch_grad = db_all[...]

    @pl.when(seq == 0)
    def _():
        sums_ref[...] = jnp.zeros_like(sums_ref)
        dw_acc[...] = jnp.zeros_like(dw_acc)
        if last:
            gain_ref[...] = jnp.zeros_like(gain_ref)

    total = None
    for group in range(2):
        w_ref = w_refs[group]
        attended_grad = matmul(branch_grad, w_ref[:, 3 * width :]).astype(BF)
        qkv = qkv_ref[group, 0]
        queries, keys, values = qkv[:, :width], qkv[:, width : 2 * width], qkv[:, 2 * width :]
        attended = o_ref[group, 0]
        queries_t = queries.T
        grad_t = attended_grad.T
        inner_all = attended_grad.astype(F32) * attended.astype(F32)
        query_grad = jnp.zeros((length, width), F32)
        key_grads, value_grads = [], []
        for head in range(heads):
            cut = slice(head * head_size, (head + 1) * head_size)
            inner = jnp.sum(head_only(inner_all, head, head_size), axis=1, keepdims=True)
            prob_grad = matmul(head_only(attended_grad, head, head_size), values, NT)
            probs = p_ref[group, 0, head]
            parts = []
            for t in range(tiles):
                span = slice(t * TILE, (t + 1) * TILE)
                part = probs[span].astype(F32) * (prob_grad[span] - inner[span])
                for c in range(tiles):
                    tile = part[:, c * TILE : (c + 1) * TILE]
                    sums_ref[group, head, c - t + tiles - 1] += tile
                parts.append(part.astype(BF))
            score_grad = jnp.concatenate(parts, axis=0)
            query_grad += matmul(score_grad, head_only(keys, head, head_size))
            key_grads.append(matmul(queries_t[cut], score_grad))
            value_grads.append(matmul(grad_t[cut], probs))
        key_grad = jnp.concatenate(key_grads, axis=0).T
        value_grad = jnp.concatenate(value_grads, axis=0).T
        joined = jnp.concatenate(
            [query_grad.astype(BF), key_grad.astype(BF), value_grad.astype(BF)], axis=1
        )
        term = matmul(joined, w_ref[:, : 3 * width], NT)
        total = term if total is None else total + term
        dw_acc[group, :, : 3 * width] += matmul(rows, joined, TN)
        dw_acc[group, :, 3 * width :] += matmul(branch_grad, attended, TN)
    if has_base:
        total = total + base_ref[0]
    if last:
        total_all[...] = total
        for k in range(4):
            out_refs[k][0] = total_all[place_of(k)].astype(BF)
        gain_ref[...] += jnp.sum(total * rows.astype(F32), axis=0, keepdims=True)
    else:
        out_ref[0] = total

    @pl.when(seq == pl.num_programs(0) - 1)
    def _():
        row = lax.broadcasted_iota(jnp.int32, (TILE, TILE), 0)
        lane = lax.broadcasted_iota(jnp.int32, (TILE, TILE), 1)
        flip = (row + lane == TILE - 1).astype(F32)
        for group in range(2):
            dw_refs[group][...] = dw_acc[group].astype(BF)
            for head in range(heads):
                for d in range(2 * tiles - 1):
                    turned = lax.dot_general(
                        flip, sums_ref[group, head, d], (((1,), (0,)), ((), ())),
                        precision=lax.Precision.HIGHEST, preferred_element_type=F32,
                    )
                    wide = jnp.concatenate([turned, jnp.zeros_like(turned)], axis=1)
                    skewed = pltpu.roll(wide, 1, 1, stride=1, stride_axis=0)
                    line_ref[group, head, d : d + 1, :] = jnp.sum(skewed, axis=0, keepdims=True)
                line_ref[group, head, 2 * tiles - 1 :, :] = jnp.zeros((1, 2 * TILE), F32)


def expert_kernel(slots, u_ref, hg_ref, wi_ref, *refs):
    du_ref, r_ref, da_ref, acc_ref, dg_acc = refs[-5:]
    chunk = pl.program_id(1)
    first = wi_ref[0]
    sources, padded, model = u_ref.shape
    pre_act = matmul(u_ref[...].reshape(sources * padded, model), first)
    hidden_grad = hg_ref[0, :, 0].reshape(sources * padded, -1).astype(F32)
    root = 0.7978845608028654
    square = pre_act * pre_act
    bend = jnp.tanh(root * pre_act * (1.0 + 0.044715 * square))
    half = 0.5 * (1.0 + bend)
    hidden = (pre_act * half).astype(BF)
    slope = half + 0.5 * root * pre_act * (1.0 - bend * bend) * (1.0 + 3 * 0.044715 * square)
    pre_grad = (hidden_grad * slope).astype(BF)
    r_ref[0, :, 0] = hidden.reshape(sources, padded, -1)
    da_ref[0, :, 0] = pre_grad.reshape(sources, padded, -1)
    gate_part = jnp.sum(hidden.astype(F32) * hidden_grad, axis=1, keepdims=True)
    input_part = matmul(pre_grad, first, NT)

    @pl.when(chunk == 0)
    def _():
        acc_ref[...] = input_part
        dg_acc[...] = gate_part

    @pl.when(chunk > 0)
    def _():
        acc_ref[...] += input_part
        dg_acc[...] += gate_part

    @pl.when(chunk == pl.num_programs(1) - 1)
    def _():
        gates = jnp.broadcast_to(dg_acc[...], (sources * padded, TILE)).T[0:1]
        place = lax.broadcasted_iota(jnp.int32, (padded, model), 0)
        for source in range(sources):
            span = slice(source * padded, (source + 1) * padded)
            gate = gates[:, span]
            high = gate.astype(BF).astype(F32)
            extra = jnp.concatenate(
                [high, gate - high, jnp.zeros((1, model - 2 * padded), F32)], axis=1
            )
            du_ref[source] = jnp.where(place == slots, extra, acc_ref[span]).astype(BF)


def attend(me, n1_seqs, weights, seg_here, lines, base, heads, head_size):
    groups, seqs, part, model = n1_seqs.shape
    length = seg_here.shape[1]
    width = heads * head_size
    tiles = length // TILE
    last = base is not None
    flops = 2 * 2 * seqs * length * (4 * width * model + 2 * heads * length * head_size)
    whole = pl.BlockSpec((model, 4 * width), lambda s: (0, 0))
    rows_spec = pl.BlockSpec((1, length, model), lambda s: (s, 0, 0))
    seqs_spec = pl.BlockSpec((groups, 1, part, model), lambda s: (0, s, 0, 0))
    block_spec = pl.BlockSpec((1, part, model), lambda s: (s, 0, 0))
    return pl.pallas_call(
        functools.partial(attend_kernel, heads, head_size, last, last),
        grid=(seqs,),
        in_specs=[
            pl.BlockSpec(memory_space=pltpu.SMEM),
            seqs_spec,
            pl.BlockSpec((1, length, 1), lambda s: (s, 0, 0)),
            pl.BlockSpec((1, 1, length), lambda s: (s, 0, 0)),
            pl.BlockSpec((2, heads, 2 * tiles, 2 * TILE), lambda s: (0, 0, 0, 0)),
            whole,
            whole,
        ]
        + [rows_spec] * last,
        out_specs=[block_spec] * 4 * last
        + [rows_spec] * (not last)
        + [
            pl.BlockSpec((2, 1, length, 3 * width), lambda s: (0, s, 0, 0)),
            pl.BlockSpec((2, 1, length, width), lambda s: (0, s, 0, 0)),
            pl.BlockSpec((2, 1, heads, length, length), lambda s: (0, s, 0, 0, 0)),
        ],
        out_shape=[jax.ShapeDtypeStruct((seqs, part, model), BF)] * 4 * last
        + [jax.ShapeDtypeStruct((seqs, length, model), F32)] * (not last)
        + [
            jax.ShapeDtypeStruct((2, seqs, length, 3 * width), BF),
            jax.ShapeDtypeStruct((2, seqs, length, width), BF),
            jax.ShapeDtypeStruct((2, seqs, heads, length, length), BF),
        ],
        scratch_shapes=[pltpu.VMEM((2, heads, 2 * tiles - 1, TILE, TILE), F32)]
        + [pltpu.VMEM((length, model), F32)] * last,
        compiler_params=pltpu.CompilerParams(vmem_limit_bytes=48 << 20),
        cost_estimate=pl.CostEstimate(
            flops=3 * flops, bytes_accessed=12 << 20, transcendentals=2 * seqs * heads * length**2
        ),
        name="attend",
    )(me.reshape(1), n1_seqs, seg_here[:, :, None], seg_here[:, None, :], lines, *weights, *([base] * last))


def attend_back(me, n1_seqs, db_blocks, kept, weights, base, heads, head_size):
    qkv, attended, probs = kept
    groups, seqs, part, model = n1_seqs.shape
    length = qkv.shape[2]
    width = heads * head_size
    tiles = length // TILE
    last = base is not None
    flops = 2 * 2 * seqs * length * (8 * width * model + 4 * heads * length * head_size)
    whole = pl.BlockSpec((model, 4 * width), lambda s: (0, 0))
    rows_spec = pl.BlockSpec((1, length, model), lambda s: (s, 0, 0))
    seqs_spec = pl.BlockSpec((groups, 1, part, model), lambda s: (0, s, 0, 0))
    block_spec = pl.BlockSpec((1, part, model), lambda s: (s, 0, 0))
    dw_shape = jax.ShapeDtypeStruct((model, 4 * width), BF)
    return pl.pallas_call(
        functools.partial(attend_back_kernel, heads, head_size, last, last),
        grid=(seqs,),
        in_specs=[
            pl.BlockSpec(memory_space=pltpu.SMEM),
            seqs_spec,
            pl.BlockSpec((2, 1, length, 3 * width), lambda s: (0, s, 0, 0)),
            pl.BlockSpec((2, 1, length, width), lambda s: (0, s, 0, 0)),
            pl.BlockSpec((2, 1, heads, length, length), lambda s: (0, s, 0, 0, 0)),
            whole,
            whole,
        ]
        + [block_spec] * 4
        + [rows_spec] * last,
        out_specs=[block_spec] * 4 * last
        + [rows_spec] * (not last)
        + [
            whole,
            whole,
            pl.BlockSpec((2, heads, 2 * tiles, 2 * TILE), lambda s: (0, 0, 0, 0)),
        ]
        + [pl.BlockSpec((1, model), lambda s: (0, 0))] * last,
        out_shape=[jax.ShapeDtypeStruct((seqs, part, model), BF)] * 4 * last
        + [jax.ShapeDtypeStruct((seqs, length, model), F32)] * (not last)
        + [
            dw_shape,
            dw_shape,
            jax.ShapeDtypeStruct((2, heads, 2 * tiles, 2 * TILE), F32),
        ]
        + [jax.ShapeDtypeStruct((1, model), F32)] * last,
        scratch_shapes=[
            pltpu.VMEM((2, model, 4 * width), F32),
            pltpu.VMEM((2, heads, 2 * tiles - 1, TILE, TILE), F32),
            pltpu.VMEM((length, model), BF),
            pltpu.VMEM((length, model), F32),
        ],
        compiler_params=pltpu.CompilerParams(vmem_limit_bytes=56 << 20),
        cost_estimate=pl.CostEstimate(
            flops=2 * flops, bytes_accessed=16 << 20, transcendentals=0
        ),
        name="attend_back",
    )(me.reshape(1), n1_seqs, qkv, attended, probs, *weights, *db_blocks, *([base] * last))


def hidden_grads_kernel(c_ref, wo_ref, hg_ref):
    experts, halves, padded, model = c_ref.shape
    units = wo_ref.shape[1]
    grads = matmul(c_ref[...].reshape(experts * halves * padded, model), wo_ref[0], NT)
    hg_ref[0] = grads.astype(BF).reshape(experts, halves, padded, units)


def hidden_grads(grads, second):
    experts, halves, padded, model = grads.shape
    chunks, units, _ = second.shape
    sources = experts // 2
    return pl.pallas_call(
        hidden_grads_kernel,
        grid=(chunks, experts // sources),
        in_specs=[
            pl.BlockSpec((sources, halves, padded, model), lambda k, b: (b, 0, 0, 0)),
            pl.BlockSpec((1, units, model), lambda k, b: (k, 0, 0)),
        ],
        out_specs=pl.BlockSpec((1, sources, halves, padded, units), lambda k, b: (k, b, 0, 0, 0)),
        out_shape=jax.ShapeDtypeStruct((chunks, experts, halves, padded, units), BF),
        compiler_params=pltpu.CompilerParams(vmem_limit_bytes=48 << 20),
        cost_estimate=pl.CostEstimate(
            flops=2 * experts * halves * padded * model * units * chunks,
            bytes_accessed=20 << 20,
            transcendentals=0,
        ),
        name="hidden_grads",
    )(grads, second)


def expert_grads_kernel(gate_ref, ua_ref, ub_ref, c_ref, r_ref, da_ref, wo_ref,
                        y_ref, di_ref, di_near, do_ref, do_near,
                        y_acc, u_t, c_t, di_acc, do_acc):
    chunk, step = pl.program_id(0), pl.program_id(1)
    experts, halves, padded, model = c_ref.shape
    sources = experts // 2
    rows = sources * halves * padded
    units = wo_ref.shape[1]

    @pl.when(chunk == 0)
    def _():
        start = step * sources
        gate = gate_ref[pl.ds(pl.multiple_of(step * rows, rows), rows)]
        ua, ub = ua_ref[pl.ds(start, sources)], ub_ref[pl.ds(start, sources)]
        inputs = jnp.concatenate([ua[:, None], ub[:, None]], axis=1).reshape(rows, model)
        u_t[step] = (inputs.astype(F32) * gate).astype(BF).T
        grads = c_ref[pl.ds(start, sources)].reshape(rows, model)
        c_t[step] = (grads.astype(F32) * gate).astype(BF).T

    hidden = r_ref[0].reshape(rows, units)
    out_part = matmul(hidden, wo_ref[0])
    second_part = matmul(c_t[step], hidden)
    first_part = matmul(u_t[step], da_ref[0].reshape(rows, units))

    @pl.when(chunk == 0)
    def _():
        y_acc[step] = out_part

    @pl.when(chunk > 0)
    def _():
        y_acc[step] += out_part

    @pl.when(step == 0)
    def _():
        di_acc[...] = first_part
        do_acc[...] = second_part

    @pl.when((step == 1) & (chunk < 2))
    def _():
        di_ref[0] = (di_acc[...] + first_part).astype(BF)
        do_ref[0] = (do_acc[...] + second_part).T.astype(BF)

    @pl.when((step == 1) & (chunk >= 2))
    def _():
        di_near[0] = (di_acc[...] + first_part).astype(BF)
        do_near[0] = (do_acc[...] + second_part).T.astype(BF)

    @pl.when(chunk == pl.num_programs(0) - 1)
    def _():
        values = y_acc[step].astype(BF).reshape(sources, halves * padded, model)
        y_ref[pl.ds(step * sources, sources)] = values


def expert_grads(gates, u_first, u_second, grads, hidden, pre_grad, second):
    experts, halves, padded, model = grads.shape
    chunks, units, _ = second.shape
    sources = experts // 2
    rows = sources * halves * padded

    def whole(array):
        zeros = (0,) * array.ndim
        return pl.BlockSpec(array.shape, lambda k, b: zeros, pipeline_mode=pl.Buffered(1))

    kept_spec = pl.BlockSpec((1, sources, halves, padded, units), lambda k, b: (k, b, 0, 0, 0))
    own = pl.BlockSpec((1, model, units), lambda k, b: (jnp.minimum(k, 1), 0, 0))
    near = pl.BlockSpec((1, model, units), lambda k, b: (jnp.maximum(k - 2, 0), 0, 0))
    return pl.pallas_call(
        expert_grads_kernel,
        grid=(chunks, 2),
        in_specs=[
            whole(gates),
            whole(u_first),
            whole(u_second),
            whole(grads),
            kept_spec,
            kept_spec,
            pl.BlockSpec((1, units, model), lambda k, b: (k, 0, 0)),
        ],
        out_specs=[
            pl.BlockSpec((experts, halves * padded, model), lambda k, b: (0, 0, 0)),
            own,
            near,
            own,
            near,
        ],
        out_shape=[jax.ShapeDtypeStruct((experts, halves * padded, model), BF)]
        + [jax.ShapeDtypeStruct((2, model, units), BF)] * 4,
        scratch_shapes=[
            pltpu.VMEM((2, rows, model), F32),
            pltpu.VMEM((2, model, rows), BF),
            pltpu.VMEM((2, model, rows), BF),
            pltpu.VMEM((model, units), F32),
            pltpu.VMEM((model, units), F32),
        ],
        compiler_params=pltpu.CompilerParams(vmem_limit_bytes=60 << 20),
        cost_estimate=pl.CostEstimate(
            flops=4 * rows * model * units * chunks, bytes_accessed=40 << 20, transcendentals=0
        ),
        name="expert_grads",
    )(gates, u_first, u_second, grads, hidden, pre_grad, second)


def run_experts(half, slots, inputs, hidden_grad, first, kept):
    experts, padded, model = inputs.shape
    chunks, _, units = first.shape
    rows = experts * padded
    blocks = 2
    block = rows // blocks
    sources = experts // blocks
    kept_spec = pl.BlockSpec(
        (1, sources, 1, padded, units), lambda b, k: (k, b, half, 0, 0)
    )
    kept_shape = jax.ShapeDtypeStruct((chunks, experts, 2, padded, units), BF)
    return pl.pallas_call(
        functools.partial(expert_kernel, slots),
        grid=(blocks, chunks),
        in_specs=[
            pl.BlockSpec((sources, padded, model), lambda b, k: (b, 0, 0)),
            kept_spec,
            pl.BlockSpec((1, model, units), lambda b, k: (k, 0, 0)),
        ]
        + [pl.BlockSpec(memory_space=pl.ANY)] * len(kept),
        out_specs=[
            pl.BlockSpec((sources, padded, model), lambda b, k: (b, 0, 0)),
            kept_spec,
            kept_spec,
        ],
        out_shape=[jax.ShapeDtypeStruct((experts, padded, model), BF), kept_shape, kept_shape],
        scratch_shapes=[pltpu.VMEM((block, model), F32), pltpu.VMEM((block, 1), F32)],
        input_output_aliases={3 + i: 1 + i for i in range(len(kept))},
        compiler_params=pltpu.CompilerParams(vmem_limit_bytes=48 << 20),
        cost_estimate=pl.CostEstimate(
            flops=4 * rows * model * units * chunks, bytes_accessed=20 << 20, transcendentals=0
        ),
        name="experts",
    )(inputs, hidden_grad, first, *kept)


def swap_tensor(block, bit):
    size = lax.axis_size("tensor")
    return lax.ppermute(block, "tensor", [(i, i ^ bit) for i in range(size)])


def swap_dp(buffer):
    return lax.all_to_all(buffer, "dp", split_axis=0, concat_axis=0, tiled=True)


def swap_seqs(buffer):
    return lax.all_to_all(buffer, "tensor", split_axis=0, concat_axis=0, tiled=True)


def tie(*values):
    return lax.optimization_barrier(values)


def gather_dp(block):
    size, index = lax.axis_size("dp"), lax.axis_index("dp")
    found = block[None]
    bit = size // 2
    while bit:
        other = lax.ppermute(found, "dp", [(i, i ^ bit) for i in range(size)])
        upper = (index & bit) > 0
        pair = [jnp.where(upper, other, found), jnp.where(upper, found, other)]
        found = jnp.stack(pair, axis=1).reshape((-1,) + block.shape)
        bit //= 2
    return found


def scatter_dp(blocks):
    return jnp.sum(swap_dp(blocks).astype(F32), axis=0)


def sum_all(values):
    for axis in ("tensor", "dp"):
        size = lax.axis_size(axis)
        bit = 1
        while bit < size:
            values = values + lax.ppermute(values, axis, [(i, i ^ bit) for i in range(size)])
            bit *= 2
    return values


def by_xor(stack, index):
    pairs = jnp.concatenate([stack[1:2], stack[:1], stack[3:], stack[2:3]], axis=0)
    stack = jnp.where((index & 1) > 0, pairs, stack)
    return jnp.where((index & 2) > 0, jnp.concatenate([stack[2:], stack[:2]], axis=0), stack)


def local(
    block_input,
    cotangent,
    segment_ids,
    rel_bucket,
    expert_route,
    expert_slot,
    attn_gain,
    moe_gain,
    router_weight,
    rel_table,
    w_query,
    w_key,
    w_value,
    w_out,
    expert_in,
    expert_out,
):
    group_seqs, part_len, model_width = block_input.shape
    tensor_size = lax.axis_size("tensor")
    dp_size = lax.axis_size("dp")
    full_len = part_len * tensor_size
    seqs_here = group_seqs // tensor_size
    head_cols = w_query.shape[1]
    weight_rows = w_query.shape[0]
    heads_all = rel_table.shape[1]
    heads_here = heads_all // tensor_size
    head_size = head_cols // heads_here
    bucket_count = rel_table.shape[0]
    experts_all = router_weight.shape[1]
    tok_rows = group_seqs * part_len
    capacity = tok_rows * 15 // (8 * experts_all)
    half = capacity // 2
    padded = (half // 16 + 1) * 16
    half_size = experts_all * padded
    tiles = full_len // TILE
    me = lax.axis_index("tensor")

    packed = jnp.concatenate([w_query, w_key, w_value, w_out.T], axis=1)
    own_first = expert_in.reshape(model_width, -1)
    own_second = expert_out.reshape(-1, model_width)
    packed, tokens_in = tie(packed, block_input)
    w_own = gather_dp(packed).reshape(model_width, 4 * head_cols)
    w_core = swap_tensor(w_own, 1)
    w_far = swap_tensor(w_own, 2)

    flat_input = tokens_in.astype(F32)
    attn_gain_f = attn_gain.astype(F32)
    normed_local = attn_norm(flat_input, attn_gain_f).astype(BF)

    def by_seqs(rows):
        return swap_seqs(rows.reshape(tensor_size, seqs_here, part_len, model_width))

    n1_seqs = by_seqs(normed_local)
    seg_here = lax.dynamic_slice_in_dim(segment_ids, me * seqs_here, seqs_here, 0)
    bucket_onehot = (rel_bucket[:, None] == jnp.arange(bucket_count)[None, :]).astype(F32)
    bias_line = jnp.einsum(
        "kb,bh->hk", bucket_onehot, rel_table.astype(F32), precision=lax.Precision.HIGHEST
    )
    bias_line = jnp.pad(bias_line, ((0, 0), (1, 0))).reshape(heads_all, 2 * tiles, TILE)
    windows = jnp.concatenate([bias_line, jnp.roll(bias_line, -1, axis=1)], axis=2)
    windows = windows.reshape(tensor_size, heads_here, 2 * tiles, 2 * TILE)
    windows = by_xor(windows, me)

    route_rows = expert_route.reshape(tok_rows)
    slot_rows = expert_slot.reshape(tok_rows)
    upper = slot_rows >= half
    slot_place = jnp.where(
        slot_rows >= 0,
        route_rows * 2 * padded + slot_rows + upper * (padded - half),
        2 * half_size,
    )
    slot_ids = jnp.arange(2 * half_size).reshape(experts_all, 2, padded)

    def table_of(ids):
        return (slot_place[:, None] == ids.reshape(1, -1)).astype(BF)

    slot_tables = [table_of(slot_ids[:, h]) for h in range(2)]
    slot_table = table_of(slot_ids)
    route_onehot = (route_rows[:, None] == jnp.arange(experts_all)[None, :]).astype(F32)

    def place_rows(rows, h):
        placed = lax.dot_general(slot_tables[h], rows, TN, preferred_element_type=F32)
        return placed.reshape(experts_all, padded, model_width)

    def take_rows(buffers):
        return sum(
            matmul(slot_tables[h], buffers[h].reshape(half_size, -1)) for h in range(2)
        )

    def with_extra(placed, numbers, h):
        high = numbers.astype(BF)
        low = (numbers - high.astype(F32)).astype(BF)
        parts = lax.dot_general(jnp.stack([high, low]), slot_tables[h], (((1,), (0,)), ((), ())),
                                preferred_element_type=F32)
        parts = parts.reshape(2, experts_all, padded).transpose(1, 0, 2)
        parts = parts.reshape(experts_all, 1, 2 * padded)
        parts = jnp.pad(parts, ((0, 0), (0, 0), (0, model_width - 2 * padded)))
        at_extra = jnp.arange(padded)[None, :, None] == half
        return jnp.where(at_extra, parts, placed).astype(BF)

    def extra_of(buffer):
        row = buffer[:, half].astype(F32)
        return row[:, :padded] + row[:, padded : 2 * padded]

    cotangent_rows = cotangent.reshape(tok_rows, model_width)
    c_placed = lax.dot_general(slot_table, cotangent_rows, TN, preferred_element_type=F32)
    c_placed = c_placed.astype(BF).reshape(experts_all, 2 * padded, model_width)
    c_placed, n1_seqs, w_own = tie(c_placed, n1_seqs, w_own)
    c_arrived = swap_dp(c_placed)

    def stack_tensor(own, far):
        return jnp.stack([own, far, swap_tensor(own, 1), swap_tensor(far, 1)])

    partial, *kept_near = attend(
        me, n1_seqs, (w_own, w_core), seg_here, windows[:2], None, heads_here, head_size
    )
    partial, w_far, own_second = tie(partial, w_far, own_second)
    w_both = swap_tensor(w_far, 1)
    far_second = swap_tensor(own_second, 2)
    *branch, qkv_far, o_far, p_far = attend(
        me, n1_seqs, (w_far, w_both), seg_here, windows[2:], partial, heads_here, head_size
    )
    kept_far = (qkv_far, o_far, p_far)
    *branch, far_second = tie(*branch, far_second)
    branch = branch[:1] + [swap_tensor(branch[k], k) for k in range(1, 4)]
    *branch, c_arrived, own_first = tie(*branch, c_arrived, own_first)
    far_first = swap_tensor(own_first, 2)
    attn_branch = by_xor(jnp.stack(branch), me).reshape(tok_rows, model_width).astype(F32)
    hidden_rows = flat_input.reshape(tok_rows, model_width) + attn_branch
    second = stack_tensor(own_second, far_second)

    moe_gain_f = moe_gain.astype(F32)
    router_f = router_weight.astype(F32)
    rms = rms_inverse(hidden_rows)
    scaled = hidden_rows * rms
    normed_moe = scaled * moe_gain_f
    logits = jnp.dot(
        normed_moe, router_f, precision=lax.Precision.HIGHEST, preferred_element_type=F32
    )
    router_probs = jax.nn.softmax(logits, axis=-1)
    gate_value = jnp.sum(router_probs * route_onehot, axis=-1)

    sent_rows = normed_moe.astype(BF)
    u_placed = [with_extra(place_rows(sent_rows, h), gate_value, h) for h in range(2)]
    u_first = swap_dp(u_placed[0])
    c_all = c_arrived.reshape(experts_all, 2, padded, model_width)
    c_all, second, far_first = tie(c_all, second, far_first)
    first = stack_tensor(own_first, far_first)
    hidden_grad = hidden_grads(c_all, second)
    u_first, u_next, hidden_grad = tie(u_first, u_placed[1], hidden_grad)
    u_second = swap_dp(u_next)
    back_first, *kept = run_experts(0, half, u_first, hidden_grad, first, ())
    back_second, hidden, pre_grad = run_experts(1, half, u_second, hidden_grad, first, kept)
    back_first, u_second = tie(back_first, u_second)
    back_first = swap_dp(back_first)
    back_first, back_second = tie(back_first, back_second)
    back_second = swap_dp(back_second)

    gates = jnp.stack([extra_of(u_first), extra_of(u_second)], axis=1)[..., None]
    out_rows, first_terms, first_near, second_terms, second_near = expert_grads(
        gates.reshape(2 * half_size, 1), u_first, u_second, c_all, hidden, pre_grad, second
    )

    def near_sum(own, near):
        return own.astype(F32) + swap_tensor(near, 1).astype(F32)

    def near_terms(stack, near):
        near = swap_tensor(near, 1)
        passed = (stack[1].astype(F32) + near[1].astype(F32)).astype(BF)
        return passed, stack[0], near[0]

    first_passed, *first_parts = near_terms(first_terms, first_near)
    second_passed, *second_parts = near_terms(second_terms, second_near)

    out_grad = cotangent_rows.astype(F32)
    back_second, out_rows = tie(back_second, out_rows)
    returned = swap_dp(out_rows)
    gate_back = [extra_of(back_first), extra_of(back_second)]
    gate_back = [
        jnp.stack([v.astype(BF), (v - v.astype(BF).astype(F32)).astype(BF)], axis=-1)
        for v in gate_back
    ]
    gate_grad = jnp.sum(take_rows(gate_back), axis=-1)
    logit_grad = (gate_grad * gate_value)[:, None] * (route_onehot - router_probs)
    normed_grad = gate_value[:, None] * take_rows([back_first, back_second]) + lax.dot_general(
        logit_grad, router_f, NT, precision=lax.Precision.HIGHEST, preferred_element_type=F32
    )
    gained = normed_grad * moe_gain_f
    residual_grad = (
        out_grad + rms * gained - scaled * rms * jnp.mean(gained * scaled, axis=-1, keepdims=True)
    )
    db_rows = residual_grad.astype(BF).reshape(tensor_size, seqs_here, part_len, model_width)
    db_blocks = [lax.dynamic_index_in_dim(db_rows, me ^ k, 0, keepdims=False) for k in range(4)]
    db_blocks = db_blocks[:1] + [swap_tensor(db_blocks[k], k) for k in range(1, 4)]
    *db_blocks, first_passed = tie(*db_blocks, first_passed)
    first_far = swap_tensor(first_passed, 2)

    router_part = lax.dot_general(
        normed_moe, logit_grad, TN, precision=lax.Precision.HIGHEST, preferred_element_type=F32
    )
    moe_gain_part = jnp.sum(normed_grad * scaled, axis=0)

    partial, dw_far, dw_both, lines_far = attend_back(
        me, n1_seqs, db_blocks, kept_far, (w_far, w_both), None, heads_here, head_size
    )
    dw_both, first_far = tie(dw_both, first_far)
    far_term = near_sum(dw_far, dw_both).astype(BF)
    partial, far_term = tie(partial, far_term)
    far_term = swap_tensor(far_term, 2)
    *normed_back, dw_own, dw_core, lines_near, gain_sums = attend_back(
        me, n1_seqs, db_blocks, kept_near, (w_own, w_core), partial, heads_here, head_size
    )
    dw_core, far_term, returned = tie(dw_core, far_term, returned)
    owner_terms = (near_sum(dw_own, dw_core) + far_term.astype(F32)).astype(BF)
    owner_terms, gain_sums, lines_near = tie(owner_terms, gain_sums, lines_near)
    owner_grad = scatter_dp(owner_terms.reshape(dp_size, weight_rows, 4 * head_cols))

    normed_back = normed_back[:1] + [swap_tensor(normed_back[k], k) for k in range(1, 4)]
    *normed_back, second_passed, first_far = tie(*normed_back, second_passed, first_far)
    second_far = swap_tensor(second_passed, 2)
    first_grad = sum(v.astype(F32) for v in (*first_parts, first_far)).reshape(expert_in.shape)
    second_grad = sum(v.astype(F32) for v in (*second_parts, second_far))
    second_grad = second_grad.reshape(expert_out.shape)
    normed_back = by_xor(jnp.stack(normed_back), me)
    normed_back = normed_back.reshape(group_seqs, part_len, model_width).astype(F32)
    gained_in = normed_back * attn_gain_f
    rms_in = rms_inverse(flat_input)
    scaled_in = flat_input * rms_in
    input_grad = (
        residual_grad.reshape(group_seqs, part_len, model_width)
        + rms_in * gained_in
        - scaled_in * rms_in * jnp.mean(gained_in * scaled_in, axis=-1, keepdims=True)
    )
    block_output = hidden_rows + gate_value[:, None] * matmul(
        slot_table, returned.reshape(2 * half_size, model_width)
    )
    block_output = block_output.astype(BF).reshape(group_seqs, part_len, model_width)

    line_sums = by_xor(jnp.concatenate([lines_near, lines_far], axis=0), me)
    low, high = line_sums[..., :TILE], line_sums[..., TILE:]
    offset_sums = low + jnp.roll(high, 1, axis=2)
    offset_sums = offset_sums.reshape(heads_all, 2 * full_len)[:, 1:]
    table_part = jnp.einsum(
        "hk,kb->bh", offset_sums, bucket_onehot, precision=lax.Precision.HIGHEST
    )
    small = [gain_sums[0] / attn_gain_f, moe_gain_part, router_part, table_part]
    sums = jnp.concatenate([v.reshape(-1) for v in small])
    size = sums.size
    sums = jnp.pad(sums, (0, -size % (8 * TILE))).reshape(-1, TILE)
    sums = sum_all(sums).reshape(-1)
    totals, start = [], 0
    for v in small:
        totals.append(sums[start : start + v.size].reshape(v.shape))
        start += v.size
    return (
        block_output,
        input_grad,
        *totals,
        owner_grad[:, :head_cols],
        owner_grad[:, head_cols : 2 * head_cols],
        owner_grad[:, 2 * head_cols : 3 * head_cols],
        owner_grad[:, 3 * head_cols :].T,
        first_grad,
        second_grad,
    )


def solution(mesh):
    in_specs = (
        P("dp", "tensor", None),
        P("dp", "tensor", None),
        P("dp", None),
        P(),
        P("dp", "tensor"),
        P("dp", "tensor"),
        P(),
        P(),
        P(),
        P(),
        P("dp", "tensor"),
        P("dp", "tensor"),
        P("dp", "tensor"),
        P("tensor", "dp"),
        P("dp", None, "tensor"),
        P("dp", "tensor", None),
    )
    out_specs = (
        P("dp", "tensor", None),
        P("dp", "tensor", None),
        P(),
        P(),
        P(),
        P(),
        P("dp", "tensor"),
        P("dp", "tensor"),
        P("dp", "tensor"),
        P("tensor", "dp"),
        P("dp", None, "tensor"),
        P("dp", "tensor", None),
    )
    return jax.shard_map(local, mesh=mesh, in_specs=in_specs, out_specs=out_specs, check_vma=False)
```

time: 695 us -> 519 us (0.75)
  waiting for transfers between devices: 270 us -> 129 us
  blocking collectives: 87.8 us -> 0 us
  Pallas kernels: 125 us -> 195 us
  matrix products: 78.8 us -> 41.8 us
  starting transfers between devices: 50.2 us -> 70.4 us
    all_to_all x6 -> x7, waiting for transfers between devices: 100 us -> 15 us  [swap_dp(): return lax.all_to_all(buffer, 'dp', split_axis=0, concat_axis=0, tiled=True)]
    pallas_call x3 -> x8, Pallas kernels: 125 us -> 195 us  [the longest x2 48.8 us: attend_back(): pl.pallas_call(functools.partial(attend_back_kernel, heads, head_size, la...]
    ppermute x12 -> x25, waiting for transfers between devices: 127 us -> 80.4 us  [swap_tensor(): return lax.ppermute(block, 'tensor', [(i, i ^ bit) for i in range(size)])]
    all_to_all x2 -> x0, blocking collectives: 44.9 us -> none  [swap_dp(): return lax.all_to_all(buffer, 'dp', split_axis=0, concat_axis=0, tiled=True)]
    psum x1 -> x0, blocking collectives: 42.9 us -> none  [local(): lax.psum((gain_sums[0] / attn_gain_f, moe_gain_part, router_part, table_p...]
    all_to_all x4 -> x1, waiting for transfers between devices: 43.5 us -> 1.46 us  [swap_seqs(): lax.all_to_all(buffer, 'tensor', split_axis=0, concat_axis=0, tiled=True)]
    dot_general x7 -> x10, matrix products: 69.4 us -> 30.4 us  [the longest x5 16.9 us: matmul(): return lax.dot_general(left, right, dims, preferred_element_type=F32)]
    ppermute x0 -> x8, waiting for transfers between devices: none -> 31.9 us  [the longest x5 18.5 us: sum_all(): lax.ppermute(values, axis, [(i, i ^ bit) for i in range(size)])]
  transfers between devices with their start and end apart: 22 -> 41, of which waited for: 16 -> 24; matrix products, arithmetic and copies ran while one was open for 19% -> 19% of each run, Pallas kernels for 7% -> 38%
where the time goes in v2:
time: 519 us; the launch traced here: 514 us
  Pallas kernels  195 us (38%)
  waiting for transfers between devices  129 us (25%)
  starting transfers between devices  70.4 us (14%)
  other arithmetic  50 us (10%)
  matrix products  41.8 us (8%)
  local copies, waits for them, and re-layouts  26 us (5%)
    ppermute x25, waiting for transfers between devices, swap_tensor(): return lax.ppermute(block, 'tensor', [(i, i ^ bit) for i in range(size)])  80.4 us
    pallas_call x2, Pallas kernels, attend_back(): pl.pallas_call(functools.partial(attend_back_kernel, heads, head_size, la...  48.8 us
    pallas_call x1, Pallas kernels, expert_grads(): pl.pallas_call(expert_grads_kernel, grid=(chunks, 2), in_specs=[whole(gat...  48.3 us
    pallas_call x2, Pallas kernels, run_experts(): pl.pallas_call(functools.partial(expert_kernel, slots), grid=(blocks, chu...  45.9 us
    all_to_all x7, starting transfers between devices, swap_dp(): return lax.all_to_all(buffer, 'dp', split_axis=0, concat_axis=0, tiled=True)  39.2 us
    pallas_call x2, Pallas kernels, attend(): pl.pallas_call(functools.partial(attend_kernel, heads, head_size, last, l...  36.7 us
    ppermute x5, waiting for transfers between devices, sum_all(): lax.ppermute(values, axis, [(i, i ^ bit) for i in range(size)])  18.5 us
    dot_general x5, matrix products, matmul(): return lax.dot_general(left, right, dims, preferred_element_type=F32)  16.9 us
  transfers between devices with their start and end apart: 41, of which 24 were waited for; matrix products, arithmetic and copies ran while one was open for 19% of the time, Pallas kernels for 38%

profile of v2, /device:TPU:0, one launch (start us, length us, event | category | flops | bytes accessed | tf_op | source)
XLA Modules:
  0.0 514.0 jit_solution(13390907067361198935)
XLA Ops:
  2.6 4.1 collective-permute-start
  9.3 4.5 collective-permute-done
  16.8 3.7 all-to-all-start
  25.4 5.9 %fusion.20 = bf16[2048,768]{1,0:T(8,128)(2,1)} fusion(bf16[1024,768]{1,0:T(8,128)(2,1)S(1)} %bitcast.266, s32[1024]{0:T(1024)S(1)} %fusion.95), kind=kOutput, calls=%fused_computation.23 | convolution fusion | flops 3224895488 | bytes 4722688 | tf_op jit(solution)/shard_map/dot_general | solution.py:677
  31.3 6.5 %collective-permute-done.2 = bf16[4,96,768]{2,1,0:T(8,128)(2,1)S(1)} collective-permute-done((bf16[4,96,768]{2,1,0:T(8,128)(2,1)S(1)}, bf16[4,96,768]{2,1,0:T(8,128)(2,1)S(1)}, u32[]{:S(2)}, u32[]{:S(2)}) %collective-permute-start.2) | collective-permute-done | bytes 589856 | tf_op jit(solution)/shard_map/ppermute | solution.py:543
  41.7 6.2 %all-to-all-start.1 = ((bf16[8,256,768]{2,1,0:T(8,128)(2,1)}), bf16[8,256,768]{2,1,0:T(8,128)(2,1)S(1)}, u32[]{:S(2)}, u32[]{:S(2)}) async-start(bf16[8,256,768]{2,1,0:T(8,128)(2,1)} %bitcast.263), calls=%async_computation.1 | async-start | bytes 6291456 | tf_op jit(solution)/shard_map/all_to_all | solution.py:527
  55.4 18.0 %attend.2 = (f32[2,512,768]{2,1,0:T(8,128)}, bf16[2,2,512,576]{3,2,1,0:T(8,128)(2,1)}, bf16[2,2,512,192]{3,2,1,0:T(8,128)(2,1)S(1)}, bf16[2,2,3,512,512]{4,3,2,1,0:T(8,128)(2,1)}) custom-call(s32[1]{0:T(128)} %bitcast.2.refs_0_, bf16[4,2,128,768]{3,2,1,0:T(8,128)(2,1)S(1)} %copy-done.7, s32[2,512,1]{2,1,0:T(8,128)S(1)} %copy-done.10, ...), custom_call_target="tpu_custom_call" | custom-call | flops 9663676416 | bytes 12582912 | tf_op jit(solution)/shard_map/attend/pallas_call | solution.py:259
  73.5 3.9 collective-permute-done.4.refs_5_
  80.5 18.6 %attend.3 = (bf16[2,128,768]{2,1,0:T(8,128)(2,1)S(1)}, bf16[2,128,768]{2,1,0:T(8,128)(2,1)S(1)}, bf16[2,128,768]{2,1,0:T(8,128)(2,1)S(1)}, bf16[2,128,768]{2,1,0...) custom-call(s32[1]{0:T(128)} %bitcast.2.refs_0_, ...), custom_call_target="tpu_custom_call" | custom-call | flops 9663676416 | bytes 12582912 | tf_op jit(solution)/shard_map/attend/pallas_call | solution.py:259
  100.1 6.0 %collective-permute-done.6 = bf16[768,768]{1,0:T(8,128)(2,1)} collective-permute-done((bf16[768,768]{1,0:T(8,128)(2,1)}, bf16[768,768]{1,0:T(8,128)(2,1)}, u32[]{:S(2)}, u32[]{:S(2)}) %collective-permute-start.6) | collective-permute-done | bytes 1179680 | tf_op jit(solution)/shard_map/ppermute | solution.py:523
  109.6 8.4 %collective-permute-done.8 = bf16[2,128,768]{2,1,0:T(8,128)(2,1)S(1)} collective-permute-done((bf16[2,128,768]{2,1,0:T(8,128)(2,1)S(1)}, bf16[2,128,768]{2,1,0:T(8,128)(2,1)S(1)}, u32[]{:S(2)}, u32[]{:S(2)}) %collective-permute-start.8) | collective-permute-done | bytes 393248 | tf_op jit(solution)/shard_map/ppermute | solution.py:523
  118.8 7.0 %collective-permute-done.9 = bf16[2,128,768]{2,1,0:T(8,128)(2,1)} collective-permute-done((bf16[2,128,768]{2,1,0:T(8,128)(2,1)S(1)}, bf16[2,128,768]{2,1,0:T(8,128)(2,1)}, u32[]{:S(2)}, u32[]{:S(2)}) %collective-permute-start.9) | collective-permute-done | bytes 393248 | tf_op jit(solution)/shard_map/ppermute | solution.py:523
  125.8 3.0 maximum_select_fusion
  137.1 3.0 select_convert_fusion.1
  140.2 6.0 %all-to-all-start.2 = ((bf16[8,128,768]{2,1,0:T(8,128)(2,1)}), bf16[8,128,768]{2,1,0:T(8,128)(2,1)S(1)}, u32[]{:S(2)}, u32[]{:S(2)}) async-start(bf16[8,128,768]{2,1,0:T(8,128)(2,1)} %select_convert_fusion.1), calls=%async_computation.2 | async-start | bytes 3145728 | tf_op jit(solution)/shard_map/all_to_all | solution.py:527
  147.7 4.0 pad_maximum_fusion.wo_ref
  152.6 3.0 select_convert_fusion
  155.6 18.5 %collective-permute-done.12 = bf16[768,768]{1,0:T(8,128)(2,1)S(1)} collective-permute-done((bf16[768,768]{1,0:T(8,128)(2,1)}, bf16[768,768]{1,0:T(8,128)(2,1)S(1)}, u32[]{:S(2)}, u32[]{:S(2)}) %collective-permute-start.12) | collective-permute-done | bytes 1179680 | tf_op jit(solution)/shard_map/ppermute | solution.py:523
  175.2 15.1 %hidden_grads.1.hg_ref = bf16[4,8,2,128,768]{4,3,2,1,0:T(8,128)(2,1)} custom-call(bf16[8,2,128,768]{3,2,1,0:T(8,128)(2,1)S(1)} %bitcast.253, bf16[4,768,768]{2,1,0:T(8,128)(2,1)} %pad_maximum_fusion.wo_ref), custom_call_target="tpu_custom_call" | custom-call | flops 9663676416 | bytes 20971520 | tf_op jit(solution)/shard_map/hidden_grads/pallas_call | solution.py:364
  190.3 6.2 %all-to-all-start.3 = ((bf16[8,128,768]{2,1,0:T(8,128)(2,1)}), bf16[8,128,768]{2,1,0:T(8,128)(2,1)S(1)}, u32[]{:S(2)}, u32[]{:S(2)}) async-start(bf16[8,128,768]{2,1,0:T(8,128)(2,1)} %select_convert_fusion), calls=%async_computation.3 | async-start | bytes 3145728 | tf_op jit(solution)/shard_map/all_to_all | solution.py:527
  201.4 3.6 pad_maximum_fusion.1.wi_ref
  205.0 22.8 %experts.2 = (bf16[8,128,768]{2,1,0:T(8,128)(2,1)S(1)}, bf16[4,8,2,128,768]{4,3,2,1,0:T(8,128)(2,1)}, bf16[4,8,2,128,768]{4,3,2,1,0:T(8,128)(2,1)}) custom-call(bf16[8,128,768]{2,1,0:T(8,128)(2,1)S(1)} %all-to-all-done.2.u_ref.ua_ref, bf16[4,8,2,128,768]{4,3,2,1,0:T(8,128)(2,1)} %hidden_grads.1.hg_ref, bf16[4,768,768]{2,1,0:T(8,128)(2,1)} %pad_maximum_fusion.1.wi_ref), custom_call_target="tpu_custom_call" | custom-call | flops 9663676416 | bytes 20971520 | tf_op jit(solution)/shard_map/experts/pallas_call | solution.py:496
  228.9 3.7 all-to-all-done.3.u_ref.ub_ref
  232.6 4.3 all-to-all-start.4
  238.9 23.1 %experts.3 = (bf16[8,128,768]{2,1,0:T(8,128)(2,1)}, bf16[4,8,2,128,768]{4,3,2,1,0:T(8,128)(2,1)}, bf16[4,8,2,128,768]{4,3,2,1,0:T(8,128)(2,1)}) custom-call(bf16[8,128,768]{2,1,0:T(8,128)(2,1)S(1)} %all-to-all-done.3.u_ref.ub_ref, bf16[4,8,2,128,768]{4,3,2,1,0:T(8,128)(2,1)} %hidden_grads.1.hg_ref, ...), custom_call_target="tpu_custom_call", output_to_operand_aliasing={{1}: (3, {}), {2}: (4, {})} | custom-call | flops 9663676416 | bytes 20971520 | tf_op jit(solution)/shard_map/experts/pallas_call | solution.py:496
  262.0 11.3 %all-to-all-done.4 = bf16[8,128,768]{2,1,0:T(8,128)(2,1)} async-done(((bf16[8,128,768]{2,1,0:T(8,128)(2,1)}), bf16[8,128,768]{2,1,0:T(8,128)(2,1)}, u32[]{:S(2)}, u32[]{:S(2)}) %all-to-all-start.4) | async-done | bytes 1572896 | tf_op jit(solution)/shard_map/all_to_all | solution.py:527
  273.3 3.8 all-to-all-start.5
  279.3 48.3 %expert_grads.1 = (bf16[8,256,768]{2,1,0:T(8,128)(2,1)}, bf16[2,768,768]{2,1,0:T(8,128)(2,1)}, bf16[2,768,768]{2,1,0:T(8,128)(2,1)}, bf16[2,768,768]{2,1,0:T(8,128)(2,1)}, bf16[2,768,768]{2,1,0:T(8,128)(2,1)}) custom-call(f32[2048,1]{1,0:T(8,128)} %copy.68.gate_ref, bf16[8,128,768]{2,1,0:T(8,128)(2,1)} %copy-done.3, bf16[8,128,768]{2,1,0:T(8,128)(2,1)} %copy-done.2, ...), custom_call_target="tpu_custom_call" | custom-call | flops 9663676416 | bytes 41943040 | tf_op jit(solution)/shard_map/expert_grads/pallas_call | solution.py:449
  328.6 4.9 fusion.10
  335.3 6.3 %all-to-all-start.6 = ((bf16[8,256,768]{2,1,0:T(8,128)(2,1)}), bf16[8,256,768]{2,1,0:T(8,128)(2,1)}, u32[]{:S(2)}, u32[]{:S(2)}) async-start(bf16[8,256,768]{2,1,0:T(8,128)(2,1)} %get-tuple-element.160), calls=%async_computation.6 | async-start | bytes 6291456 | tf_op jit(solution)/shard_map/all_to_all | solution.py:527
  341.6 3.4 fusion.4
  345.1 3.4 multiply_reduce_fusion
  348.5 2.8 fusion.105
  356.2 8.2 %collective-permute-done.16.refs_9_ = bf16[2,128,768]{2,1,0:T(8,128)(2,1)S(1)} collective-permute-done((bf16[2,128,768]{2,1,0:T(8,128)(2,1)S(1)}, bf16[2,128,768]{2,1,0:T(8,128)(2,1)S(1)}, u32[]{:S(2)}, u32[]{:S(2)}) %collective-permute-start.16) | collective-permute-done | bytes 393248 | tf_op jit(solution)/shard_map/ppermute | solution.py:523
  364.3 7.2 %collective-permute-done.17.refs_10_ = bf16[2,128,768]{2,1,0:T(8,128)(2,1)S(1)} collective-permute-done((bf16[2,128,768]{2,1,0:T(8,128)(2,1)S(1)}, bf16[2,128,768]{2,1,0:T(8,128)(2,1)S(1)}, u32[]{:S(2)}, u32[]{:S(2)}) %collective-permute-start.17) | collective-permute-done | bytes 393248 | tf_op jit(solution)/shard_map/ppermute | solution.py:523
  373.0 24.3 %attend_back.2 = (f32[2,512,768]{2,1,0:T(8,128)}, bf16[768,768]{1,0:T(8,128)(2,1)}, bf16[768,768]{1,0:T(8,128)(2,1)}, f32[2,3,8,256]{3,2,1,0:T(8,128)}) custom-call(s32[1]{0:T(128)} %bitcast.2.refs_0_, bf16[4,2,128,768]{3,2,1,0:T(8,128)(2,1)} %copy-done.6, bf16[2,2,512,576]{3,2,1,0:T(8,128)(2,1)} %get-tuple-element.149.refs_2_, ...), custom_call_target="tpu_custom_call" | custom-call | flops 12884901888 | bytes 16777216 | tf_op jit(solution)/shard_map/attend_back/pallas_call | solution.py:309
  397.3 3.0 collective-permute-done.19
  406.2 24.5 %attend_back.3 = (bf16[2,128,768]{2,1,0:T(8,128)(2,1)}, bf16[2,128,768]{2,1,0:T(8,128)(2,1)}, bf16[2,128,768]{2,1,0:T(8,128)(2,1)}, bf16[2,128,768]{2,1,0:T(8,12...) custom-call(s32[1]{0:T(128)} %bitcast.2.refs_0_, ...), custom_call_target="tpu_custom_call" | custom-call | flops 12884901888 | bytes 16777216 | tf_op jit(solution)/shard_map/attend_back/pallas_call | solution.py:309
  432.7 5.2 %fusion.26 = f32[768,8]{1,0:T(8,128)S(1)} fusion(f32[1024,768]{1,0:T(8,128)S(1)} %copy-done.21, f32[768]{0:T(1024)S(1)} %convert_element_type.237, f32[1024]{0:T(1024)S(1)} %get-tuple-element.269, f32[1024]{0:T(1024)S(1)} %copy-done.66, s32[1024]{0:T(1024)S(1)} %bitcast.300, f32[1024,8]{0,1:T(8,128)S(1)} %copy-done.45, f32[1024]{0:T(1024)S(1)} %copy-done.62, ...), kind=kOutput, calls=%fused_computation.43 | convolution fusion | flops 77119488 | bytes 3226624 | tf_op jit(solution)/shard_map/dot_general | solution.py:769
  440.1 2.9 collective-permute-done.23
  443.0 7.5 %collective-permute-done.24 = bf16[2,128,768]{2,1,0:T(8,128)(2,1)S(1)} collective-permute-done((bf16[2,128,768]{2,1,0:T(8,128)(2,1)}, bf16[2,128,768]{2,1,0:T(8,128)(2,1)S(1)}, u32[]{:S(2)}, u32[]{:S(2)}) %collective-permute-start.24) | collective-permute-done | bytes 393248 | tf_op jit(solution)/shard_map/ppermute | solution.py:523
  455.0 2.9 add_convert_fusion.1
  462.0 4.5 fusion.24
  466.5 6.4 %all-to-all-start.7 = ((bf16[8,96,768]{2,1,0:T(8,128)(2,1)}), bf16[8,96,768]{2,1,0:T(8,128)(2,1)S(1)}, u32[]{:S(2)}, u32[]{:S(2)}) async-start(bf16[8,96,768]{2,1,0:T(8,128)(2,1)} %bitcast.262), calls=%async_computation.7 | async-start | bytes 2359296 | tf_op jit(solution)/shard_map/all_to_all | solution.py:527
  472.9 15.5 %collective-permute-done.28 = f32[64,128]{1,0:T(8,128)} collective-permute-done((f32[64,128]{1,0:T(8,128)}, f32[64,128]{1,0:T(8,128)}, u32[]{:S(2)}, u32[]{:S(2)}) %collective-permute-start.28) | collective-permute-done | bytes 32800 | tf_op jit(solution)/shard_map/ppermute | solution.py:560
  491.4 3.4 fusion.33
  496.4 3.2 fusion.32
  502.7 6.9 %add_convert_fusion = bf16[1024,768]{1,0:T(8,128)(2,1)} fusion(f32[1024,768]{1,0:T(8,128)S(1)} %copy-done.22, bf16[2048,768]{1,0:T(8,128)(2,1)} %bitcast.71, s32[1024]{0:T(1024)S(1)} %copy-done.72, f32[1024]{0:T(1024)S(1)} %copy-done.51), kind=kOutput, calls=%fused_computation.33 | convolution fusion | flops 3225681920 | bytes 7872512 | tf_op jit(solution)/shard_map/dot_general | solution.py:30
  (342 shorter events, 92.4 us)
Async XLA Ops:
  0.6 47.9 %copy-start = (s32[8,512]{1,0:T(8,128)S(1)}, s32[8,512]{1,0:T(8,128)}, u32[]{:S(2)}) copy-start(s32[8,512]{1,0:T(8,128)} %param.18) | copy-start | bytes 49156
  2.6 11.1 %collective-permute-start = (bf16[1,96,768]{2,1,0:T(8,128)(2,1)S(1)}, bf16[1,96,768]{2,1,0:T(8,128)(2,1)S(1)}, u32[]{:S(2)}, u32[]{:S(2)}) collective-permute-start(bf16[1,96,768]{2,1,0:T(8,128)(2,1)S(1)} %bitcast.286), channel_id=1, source_target_pairs={{0,16},{4,20},{8,24},{12,28},{16,0},{20,4},{24,8},{28,12},{1,17},{... | collective-permute-start | bytes 442376 | tf_op jit(solution)/shard_map/ppermute | solution.py:543
  14.5 8.5 %collective-permute-start.1 = (bf16[2,96,768]{2,1,0:T(8,128)(2,1)}, bf16[2,96,768]{2,1,0:T(8,128)(2,1)}, u32[]{:S(2)}, u32[]{:S(2)}) collective-permute-start(bf16[2,96,768]{2,1,0:T(8,128)(2,1)} %maximum_bitcast_fusion), channel_id=1, source_target_pairs={{0,8},{4,12},{8,0},{12,4},{16,24},{20,28},{24,16},{28,20},{1,9},{5... | collective-permute-start | bytes 884744 | tf_op jit(solution)/shard_map/ppermute | solution.py:543
  16.8 23.8 %all-to-all-start = ((bf16[4,2,128,768]{3,2,1,0:T(8,128)(2,1)}), bf16[4,2,128,768]{3,2,1,0:T(8,128)(2,1)S(1)}, u32[]{:S(2)}, u32[]{:S(2)}) async-start(bf16[4,2,128,768]{3,2,1,0:T(8,128)(2,1)} %bitcast.7), calls=%async_computation | async-start | bytes 3145728 | tf_op jit(solution)/shard_map/all_to_all | solution.py:531
  24.1 13.7 %collective-permute-start.2 = (bf16[4,96,768]{2,1,0:T(8,128)(2,1)S(1)}, bf16[4,96,768]{2,1,0:T(8,128)(2,1)S(1)}, u32[]{:S(2)}, u32[]{:S(2)}) collective-permute-start(bf16[4,96,768]{2,1,0:T(8,128)(2,1)S(1)} %bitcast.264), channel_id=1, source_target_pairs={{0,4},{4,0},{8,12},{12,8},{16,20},{20,16},{24,28},{28,24},{1,5},{5... | collective-permute-start | bytes 1769480 | tf_op jit(solution)/shard_map/ppermute | solution.py:543
  41.7 84.0 %all-to-all-start.1 = ((bf16[8,256,768]{2,1,0:T(8,128)(2,1)}), bf16[8,256,768]{2,1,0:T(8,128)(2,1)S(1)}, u32[]{:S(2)}, u32[]{:S(2)}) async-start(bf16[8,256,768]{2,1,0:T(8,128)(2,1)} %bitcast.263), calls=%async_computation.1 | async-start | bytes 6291456 | tf_op jit(solution)/shard_map/all_to_all | solution.py:527
  48.5 3.3 collective-permute-start.3
  48.7 28.7 %collective-permute-start.4 = (bf16[768,768]{1,0:T(8,128)(2,1)}, bf16[768,768]{1,0:T(8,128)(2,1)}, u32[]{:S(2)}, u32[]{:S(2)}) collective-permute-start(bf16[768,768]{1,0:T(8,128)(2,1)} %bitcast.257), channel_id=1, source_target_pairs={{0,2},{1,3},{2,0},{3,1},{4,6},{5,7},{6,4},{7,5},{8,10},{9,11},{10,... | collective-permute-start | bytes 3538952 | tf_op jit(solution)/shard_map/ppermute | solution.py:523
  77.4 3.1 collective-permute-start.5
  77.4 28.7 %collective-permute-start.6 = (bf16[768,768]{1,0:T(8,128)(2,1)}, bf16[768,768]{1,0:T(8,128)(2,1)}, u32[]{:S(2)}, u32[]{:S(2)}) collective-permute-start(bf16[768,768]{1,0:T(8,128)(2,1)} %bitcast.26), channel_id=1, source_target_pairs={{0,2},{1,3},{2,0},{3,1},{4,6},{5,7},{6,4},{7,5},{8,10},{9,11},{10,... | collective-permute-start | bytes 3538952 | tf_op jit(solution)/shard_map/ppermute | solution.py:523
  106.1 3.5 collective-permute-start.7
  106.1 11.9 %collective-permute-start.8 = (bf16[2,128,768]{2,1,0:T(8,128)(2,1)S(1)}, bf16[2,128,768]{2,1,0:T(8,128)(2,1)S(1)}, u32[]{:S(2)}, u32[]{:S(2)}) collective-permute-start(bf16[2,128,768]{2,1,0:T(8,128)(2,1)S(1)} %get-tuple-element.112), channel_id=1, source_target_pairs={{0,2},{1,3},{2,0},{3,1},{4,6},{5,7},{6,4},{7,5},{8,10},{9,11},{10,... | collective-permute-start | bytes 1179656 | tf_op jit(solution)/shard_map/ppermute | solution.py:523
  107.6 18.1 %collective-permute-start.9 = (bf16[2,128,768]{2,1,0:T(8,128)(2,1)S(1)}, bf16[2,128,768]{2,1,0:T(8,128)(2,1)}, u32[]{:S(2)}, u32[]{:S(2)}) collective-permute-start(bf16[2,128,768]{2,1,0:T(8,128)(2,1)S(1)} %get-tuple-element.113), channel_id=1, source_target_pairs={{0,3},{1,2},{2,1},{3,0},{4,7},{5,6},{6,5},{7,4},{8,11},{9,10},{10,... | collective-permute-start | bytes 1179656 | tf_op jit(solution)/shard_map/ppermute | solution.py:523
  109.1 38.6 %collective-permute-start.10 = (bf16[768,768]{1,0:T(8,128)(2,1)}, bf16[768,768]{1,0:T(8,128)(2,1)}, u32[]{:S(2)}, u32[]{:S(2)}) collective-permute-start(bf16[768,768]{1,0:T(8,128)(2,1)} %bitcast.26), channel_id=1, source_target_pairs={{0,1},{1,0},{2,3},{3,2},{4,5},{5,4},{6,7},{7,6},{8,9},{9,8},{10,11... | collective-permute-start | bytes 3538952 | tf_op jit(solution)/shard_map/ppermute | solution.py:523
  109.4 38.3 %collective-permute-start.11 = (bf16[768,768]{1,0:T(8,128)(2,1)}, bf16[768,768]{1,0:T(8,128)(2,1)}, u32[]{:S(2)}, u32[]{:S(2)}) collective-permute-start(bf16[768,768]{1,0:T(8,128)(2,1)} %collective-permute-done.6), channel_id=1, source_target_pairs={{0,1},{1,0},{2,3},{3,2},{4,5},{5,4},{6,7},{7,6},{8,9},{9,8},{10,11... | collective-permute-start | bytes 3538952 | tf_op jit(solution)/shard_map/ppermute | solution.py:523
  135.5 209.6 %copy-start.44 = (f32[1024,8]{0,1:T(8,128)}, f32[1024,8]{0,1:T(8,128)S(1)}, u32[]{:S(2)}) copy-start(f32[1024,8]{0,1:T(8,128)S(1)} %get-tuple-element.271) | copy-start | bytes 98308
  135.5 209.5 %copy-start.61 = (f32[1024]{0:T(1024)}, f32[1024]{0:T(1024)S(1)}, u32[]{:S(2)}) copy-start(f32[1024]{0:T(1024)S(1)} %fusion.80) | copy-start | bytes 12292
  135.6 209.5 %copy-start.50 = (f32[1024]{0:T(1024)}, f32[1024]{0:T(1024)S(1)}, u32[]{:S(2)}) copy-start(f32[1024]{0:T(1024)S(1)} %select_reduce_fusion) | copy-start | bytes 12292
  140.2 50.2 %all-to-all-start.2 = ((bf16[8,128,768]{2,1,0:T(8,128)(2,1)}), bf16[8,128,768]{2,1,0:T(8,128)(2,1)S(1)}, u32[]{:S(2)}, u32[]{:S(2)}) async-start(bf16[8,128,768]{2,1,0:T(8,128)(2,1)} %select_convert_fusion.1), calls=%async_computation.2 | async-start | bytes 3145728 | tf_op jit(solution)/shard_map/all_to_all | solution.py:527
  146.2 28.0 %collective-permute-start.12 = (bf16[768,768]{1,0:T(8,128)(2,1)}, bf16[768,768]{1,0:T(8,128)(2,1)S(1)}, u32[]{:S(2)}, u32[]{:S(2)}) collective-permute-start(bf16[768,768]{1,0:T(8,128)(2,1)} %bitcast.281), channel_id=1, source_target_pairs={{0,2},{1,3},{2,0},{3,1},{4,6},{5,7},{6,4},{7,5},{8,10},{9,11},{10,... | collective-permute-start | bytes 3538952 | tf_op jit(solution)/shard_map/ppermute | solution.py:523
  190.3 46.6 %copy-start.3 = (bf16[8,128,768]{2,1,0:T(8,128)(2,1)}, bf16[8,128,768]{2,1,0:T(8,128)(2,1)S(1)}, u32[]{:S(2)}) copy-start(bf16[8,128,768]{2,1,0:T(8,128)(2,1)S(1)} %all-to-all-done.2.u_ref.ua_ref) | copy-start | bytes 4718596
  190.3 42.3 %all-to-all-start.3 = ((bf16[8,128,768]{2,1,0:T(8,128)(2,1)}), bf16[8,128,768]{2,1,0:T(8,128)(2,1)S(1)}, u32[]{:S(2)}, u32[]{:S(2)}) async-start(bf16[8,128,768]{2,1,0:T(8,128)(2,1)} %select_convert_fusion), calls=%async_computation.3 | async-start | bytes 3145728 | tf_op jit(solution)/shard_map/all_to_all | solution.py:527
  196.5 3.1 collective-permute-start.13
  196.6 4.7 collective-permute-start.14
  232.6 45.3 %copy-start.2 = (bf16[8,128,768]{2,1,0:T(8,128)(2,1)}, bf16[8,128,768]{2,1,0:T(8,128)(2,1)S(1)}, u32[]{:S(2)}) copy-start(bf16[8,128,768]{2,1,0:T(8,128)(2,1)S(1)} %all-to-all-done.3.u_ref.ub_ref) | copy-start | bytes 4718596
  232.6 40.7 %all-to-all-start.4 = ((bf16[8,128,768]{2,1,0:T(8,128)(2,1)}), bf16[8,128,768]{2,1,0:T(8,128)(2,1)}, u32[]{:S(2)}, u32[]{:S(2)}) async-start(bf16[8,128,768]{2,1,0:T(8,128)(2,1)} %copy-done.8), calls=%async_computation.4 | async-start | bytes 3145728 | tf_op jit(solution)/shard_map/all_to_all | solution.py:527
  273.3 60.2 %all-to-all-start.5 = ((bf16[8,128,768]{2,1,0:T(8,128)(2,1)}), bf16[8,128,768]{2,1,0:T(8,128)(2,1)S(1)}, u32[]{:S(2)}, u32[]{:S(2)}) async-start(bf16[8,128,768]{2,1,0:T(8,128)(2,1)} %get-tuple-element.137), calls=%async_computation.5 | async-start | bytes 3145728 | tf_op jit(solution)/shard_map/all_to_all | solution.py:527
  327.6 26.9 %collective-permute-start.18 = (bf16[2,768,768]{2,1,0:T(8,128)(2,1)}, bf16[2,768,768]{2,1,0:T(8,128)(2,1)}, u32[]{:S(2)}, u32[]{:S(2)}) collective-permute-start(bf16[2,768,768]{2,1,0:T(8,128)(2,1)} %get-tuple-element.144), channel_id=1, source_target_pairs={{0,1},{1,0},{2,3},{3,2},{4,5},{5,4},{6,7},{7,6},{8,9},{9,8},{10,11... | collective-permute-start | bytes 7077896 | tf_op jit(solution)/shard_map/ppermute | solution.py:523
  335.3 115.3 %all-to-all-start.6 = ((bf16[8,256,768]{2,1,0:T(8,128)(2,1)}), bf16[8,256,768]{2,1,0:T(8,128)(2,1)}, u32[]{:S(2)}, u32[]{:S(2)}) async-start(bf16[8,256,768]{2,1,0:T(8,128)(2,1)} %get-tuple-element.160), calls=%async_computation.6 | async-start | bytes 6291456 | tf_op jit(solution)/shard_map/all_to_all | solution.py:527
  352.2 4.0 collective-permute-start.15
  352.4 11.9 %collective-permute-start.16 = (bf16[2,128,768]{2,1,0:T(8,128)(2,1)S(1)}, bf16[2,128,768]{2,1,0:T(8,128)(2,1)S(1)}, u32[]{:S(2)}, u32[]{:S(2)}) collective-permute-start(bf16[2,128,768]{2,1,0:T(8,128)(2,1)S(1)} %get-tuple-element.233), channel_id=1, source_target_pairs={{0,2},{1,3},{2,0},{3,1},{4,6},{5,7},{6,4},{7,5},{8,10},{9,11},{10,... | collective-permute-start | bytes 1179656 | tf_op jit(solution)/shard_map/ppermute | solution.py:523
  353.9 17.6 %collective-permute-start.17 = (bf16[2,128,768]{2,1,0:T(8,128)(2,1)S(1)}, bf16[2,128,768]{2,1,0:T(8,128)(2,1)S(1)}, u32[]{:S(2)}, u32[]{:S(2)}) collective-permute-start(bf16[2,128,768]{2,1,0:T(8,128)(2,1)S(1)} %get-tuple-element.232), channel_id=1, source_target_pairs={{0,3},{1,2},{2,1},{3,0},{4,7},{5,6},{6,5},{7,4},{8,11},{9,10},{10,... | collective-permute-start | bytes 1179656 | tf_op jit(solution)/shard_map/ppermute | solution.py:523
  354.0 46.3 %collective-permute-start.25 = (bf16[2,768,768]{2,1,0:T(8,128)(2,1)}, bf16[2,768,768]{2,1,0:T(8,128)(2,1)S(1)}, u32[]{:S(2)}, u32[]{:S(2)}) collective-permute-start(bf16[2,768,768]{2,1,0:T(8,128)(2,1)} %get-tuple-element.167), channel_id=1, source_target_pairs={{0,1},{1,0},{2,3},{3,2},{4,5},{5,4},{6,7},{7,6},{8,9},{9,8},{10,11... | collective-permute-start | bytes 7077896 | tf_op jit(solution)/shard_map/ppermute | solution.py:523
  371.5 28.8 %collective-permute-start.19 = (bf16[768,768]{1,0:T(8,128)(2,1)S(1)}, bf16[768,768]{1,0:T(8,128)(2,1)}, u32[]{:S(2)}, u32[]{:S(2)}) collective-permute-start(bf16[768,768]{1,0:T(8,128)(2,1)S(1)} %fusion.58), channel_id=1, source_target_pairs={{0,2},{1,3},{2,0},{3,1},{4,6},{5,7},{6,4},{7,5},{8,10},{9,11},{10,... | collective-permute-start | bytes 3538952 | tf_op jit(solution)/shard_map/ppermute | solution.py:523
  373.0 27.3 %copy-start.24 = (bf16[2,768,768]{2,1,0:T(8,128)(2,1)S(1)}, bf16[2,768,768]{2,1,0:T(8,128)(2,1)}, u32[]{:S(2)}) copy-start(bf16[2,768,768]{2,1,0:T(8,128)(2,1)} %get-tuple-element.166) | copy-start | bytes 7077892
  400.3 3.1 collective-permute-start.20
  404.7 45.8 %collective-permute-start.21 = (bf16[768,768]{1,0:T(8,128)(2,1)}, bf16[768,768]{1,0:T(8,128)(2,1)}, u32[]{:S(2)}, u32[]{:S(2)}) collective-permute-start(bf16[768,768]{1,0:T(8,128)(2,1)} %add_convert_fusion.3), channel_id=1, source_target_pairs={{0,2},{1,3},{2,0},{3,1},{4,6},{5,7},{6,4},{7,5},{8,10},{9,11},{10,... | collective-permute-start | bytes 3538952 | tf_op jit(solution)/shard_map/ppermute | solution.py:523
  430.7 9.4 %collective-permute-start.22 = (bf16[2,128,768]{2,1,0:T(8,128)(2,1)}, bf16[2,128,768]{2,1,0:T(8,128)(2,1)S(1)}, u32[]{:S(2)}, u32[]{:S(2)}) collective-permute-start(bf16[2,128,768]{2,1,0:T(8,128)(2,1)} %get-tuple-element.163), channel_id=1, source_target_pairs={{0,1},{1,0},{2,3},{3,2},{4,5},{5,4},{6,7},{7,6},{8,9},{9,8},{10,11... | collective-permute-start | bytes 1179656 | tf_op jit(solution)/shard_map/ppermute | solution.py:523
  430.8 12.2 %collective-permute-start.23 = (bf16[2,128,768]{2,1,0:T(8,128)(2,1)}, bf16[2,128,768]{2,1,0:T(8,128)(2,1)S(1)}, u32[]{:S(2)}, u32[]{:S(2)}) collective-permute-start(bf16[2,128,768]{2,1,0:T(8,128)(2,1)} %get-tuple-element.164), channel_id=1, source_target_pairs={{0,2},{1,3},{2,0},{3,1},{4,6},{5,7},{6,4},{7,5},{8,10},{9,11},{10,... | collective-permute-start | bytes 1179656 | tf_op jit(solution)/shard_map/ppermute | solution.py:523
  431.4 19.1 %collective-permute-start.24 = (bf16[2,128,768]{2,1,0:T(8,128)(2,1)}, bf16[2,128,768]{2,1,0:T(8,128)(2,1)S(1)}, u32[]{:S(2)}, u32[]{:S(2)}) collective-permute-start(bf16[2,128,768]{2,1,0:T(8,128)(2,1)} %get-tuple-element.165), channel_id=1, source_target_pairs={{0,3},{1,2},{2,1},{3,0},{4,7},{5,6},{6,5},{7,4},{8,11},{9,10},{10,... | collective-permute-start | bytes 1179656 | tf_op jit(solution)/shard_map/ppermute | solution.py:523
  450.5 4.0 collective-permute-start.26
  459.0 1.3 collective-permute-start.27
  459.3 37.1 %collective-permute-start.32 = (bf16[768,768]{1,0:T(8,128)(2,1)}, bf16[768,768]{1,0:T(8,128)(2,1)}, u32[]{:S(2)}, u32[]{:S(2)}) collective-permute-start(bf16[768,768]{1,0:T(8,128)(2,1)} %fusion.59), channel_id=1, source_target_pairs={{0,2},{1,3},{2,0},{3,1},{4,6},{5,7},{6,4},{7,5},{8,10},{9,11},{10,... | collective-permute-start | bytes 3538952 | tf_op jit(solution)/shard_map/ppermute | solution.py:523
  460.9 27.6 %collective-permute-start.28 = (f32[64,128]{1,0:T(8,128)}, f32[64,128]{1,0:T(8,128)}, u32[]{:S(2)}, u32[]{:S(2)}) collective-permute-start(f32[64,128]{1,0:T(8,128)} %fusion.125), channel_id=1, source_target_pairs={{0,2},{1,3},{2,0},{3,1},{4,6},{5,7},{6,4},{7,5},{8,10},{9,11},{10,... | collective-permute-start | bytes 98312 | tf_op jit(solution)/shard_map/ppermute | solution.py:560
  466.5 45.5 %all-to-all-start.7 = ((bf16[8,96,768]{2,1,0:T(8,128)(2,1)}), bf16[8,96,768]{2,1,0:T(8,128)(2,1)S(1)}, u32[]{:S(2)}, u32[]{:S(2)}) async-start(bf16[8,96,768]{2,1,0:T(8,128)(2,1)} %bitcast.262), calls=%async_computation.7 | async-start | bytes 2359296 | tf_op jit(solution)/shard_map/all_to_all | solution.py:527
  489.3 5.5 %collective-permute-start.29 = (f32[64,128]{1,0:T(8,128)S(1)}, f32[64,128]{1,0:T(8,128)S(1)}, u32[]{:S(2)}, u32[]{:S(2)}) collective-permute-start(f32[64,128]{1,0:T(8,128)S(1)} %fusion.127), channel_id=1, source_target_pairs={{0,4},{4,0},{8,12},{12,8},{16,20},{20,16},{24,28},{28,24},{1,5},{5... | collective-permute-start | bytes 98312 | tf_op jit(solution)/shard_map/ppermute | solution.py:560
  494.8 7.2 %collective-permute-start.30 = (f32[64,128]{1,0:T(8,128)S(1)}, f32[64,128]{1,0:T(8,128)S(1)}, u32[]{:S(2)}, u32[]{:S(2)}) collective-permute-start(f32[64,128]{1,0:T(8,128)S(1)} %add.180), channel_id=1, source_target_pairs={{0,8},{4,12},{8,0},{12,4},{16,24},{20,28},{24,16},{28,20},{1,9},{5... | collective-permute-start | bytes 98312 | tf_op jit(solution)/shard_map/ppermute | solution.py:560
  502.0 7.6 %collective-permute-start.31 = (f32[64,128]{1,0:T(8,128)S(1)}, f32[64,128]{1,0:T(8,128)S(1)}, u32[]{:S(2)}, u32[]{:S(2)}) collective-permute-start(f32[64,128]{1,0:T(8,128)S(1)} %add.181), channel_id=1, source_target_pairs={{0,16},{4,20},{8,24},{12,28},{16,0},{20,4},{24,8},{28,12},{1,17},{... | collective-permute-start | bytes 98312 | tf_op jit(solution)/shard_map/ppermute | solution.py:560
  (79 other events, 589.3 us)

commit v3 on v2

--- a/solution.py
+++ b/solution.py
@@ -371,23 +371,18 @@
         out_specs=pl.BlockSpec((1, sources, halves, padded, units), lambda k, b: (k, b, 0, 0, 0)),
         out_shape=jax.ShapeDtypeStruct((chunks, experts, halves, padded, units), BF),
         compiler_params=pltpu.CompilerParams(vmem_limit_bytes=48 << 20),
-        cost_estimate=pl.CostEstimate(
-            flops=2 * experts * halves * padded * model * units * chunks,
-            bytes_accessed=20 << 20,
-            transcendentals=0,
-        ),
+        cost_estimate=pl.CostEstimate(flops=1, bytes_accessed=1, transcendentals=0),
         name="hidden_grads",
     )(grads, second)
 
 
-def expert_grads_kernel(gate_ref, ua_ref, ub_ref, c_ref, r_ref, da_ref, wo_ref,
-                        y_ref, di_ref, di_near, do_ref, do_near,
-                        y_acc, u_t, c_t, di_acc, do_acc):
+def expert_grads_kernel(gate_ref, ua_ref, ub_ref, c_ref, r_ref, da_ref,
+                        di_ref, di_near, do_ref, do_near, u_t, c_t, di_acc, do_acc):
     chunk, step = pl.program_id(0), pl.program_id(1)
     experts, halves, padded, model = c_ref.shape
     sources = experts // 2
     rows = sources * halves * padded
-    units = wo_ref.shape[1]
+    units = r_ref.shape[-1]
 
     @pl.when(chunk == 0)
     def _():
@@ -400,18 +395,9 @@
         c_t[step] = (grads.astype(F32) * gate).astype(BF).T
 
     hidden = r_ref[0].reshape(rows, units)
-    out_part = matmul(hidden, wo_ref[0])
     second_part = matmul(c_t[step], hidden)
     first_part = matmul(u_t[step], da_ref[0].reshape(rows, units))
 
-    @pl.when(chunk == 0)
-    def _():
-        y_acc[step] = out_part
-
-    @pl.when(chunk > 0)
-    def _():
-        y_acc[step] += out_part
-
     @pl.when(step == 0)
     def _():
         di_acc[...] = first_part
@@ -427,15 +413,10 @@
         di_near[0] = (di_acc[...] + first_part).astype(BF)
         do_near[0] = (do_acc[...] + second_part).T.astype(BF)
 
-    @pl.when(chunk == pl.num_programs(0) - 1)
-    def _():
-        values = y_acc[step].astype(BF).reshape(sources, halves * padded, model)
-        y_ref[pl.ds(step * sources, sources)] = values
-
-
-def expert_grads(gates, u_first, u_second, grads, hidden, pre_grad, second):
+
+def expert_grads(gates, u_first, u_second, grads, hidden, pre_grad):
     experts, halves, padded, model = grads.shape
-    chunks, units, _ = second.shape
+    chunks, units = hidden.shape[0], hidden.shape[-1]
     sources = experts // 2
     rows = sources * halves * padded
 
@@ -456,19 +437,15 @@
             whole(grads),
             kept_spec,
             kept_spec,
-            pl.BlockSpec((1, units, model), lambda k, b: (k, 0, 0)),
         ],
         out_specs=[
-            pl.BlockSpec((experts, halves * padded, model), lambda k, b: (0, 0, 0)),
             own,
             near,
             own,
             near,
         ],
-        out_shape=[jax.ShapeDtypeStruct((experts, halves * padded, model), BF)]
-        + [jax.ShapeDtypeStruct((2, model, units), BF)] * 4,
+        out_shape=[jax.ShapeDtypeStruct((2, model, units), BF)] * 4,
         scratch_shapes=[
-            pltpu.VMEM((2, rows, model), F32),
             pltpu.VMEM((2, model, rows), BF),
             pltpu.VMEM((2, model, rows), BF),
             pltpu.VMEM((model, units), F32),
@@ -476,10 +453,10 @@
         ],
         compiler_params=pltpu.CompilerParams(vmem_limit_bytes=60 << 20),
         cost_estimate=pl.CostEstimate(
-            flops=4 * rows * model * units * chunks, bytes_accessed=40 << 20, transcendentals=0
+            flops=8 * rows * model * units * chunks, bytes_accessed=40 << 20, transcendentals=0
         ),
         name="expert_grads",
-    )(gates, u_first, u_second, grads, hidden, pre_grad, second)
+    )(gates, u_first, u_second, grads, hidden, pre_grad)
 
 
 def run_experts(half, slots, inputs, hidden_grad, first, kept):
@@ -546,10 +523,6 @@
         found = jnp.stack(pair, axis=1).reshape((-1,) + block.shape)
         bit //= 2
     return found
-
-
-def scatter_dp(blocks):
-    return jnp.sum(swap_dp(blocks).astype(F32), axis=0)
 
 
 def sum_all(values):
@@ -698,7 +671,6 @@
     far_first = swap_tensor(own_first, 2)
     attn_branch = by_xor(jnp.stack(branch), me).reshape(tok_rows, model_width).astype(F32)
     hidden_rows = flat_input.reshape(tok_rows, model_width) + attn_branch
-    second = stack_tensor(own_second, far_second)
 
     moe_gain_f = moe_gain.astype(F32)
     router_f = router_weight.astype(F32)
@@ -714,22 +686,31 @@
     sent_rows = normed_moe.astype(BF)
     u_placed = [with_extra(place_rows(sent_rows, h), gate_value, h) for h in range(2)]
     u_first = swap_dp(u_placed[0])
+    second = stack_tensor(own_second, far_second)
     c_all = c_arrived.reshape(experts_all, 2, padded, model_width)
-    c_all, second, far_first = tie(c_all, second, far_first)
+    u_next, c_all = tie(u_placed[1], c_all)
+    hidden_grad = hidden_grads(c_all, second)
+    u_first, u_next, hidden_grad = tie(u_first, u_next, hidden_grad)
+    u_second = swap_dp(u_next)
+    hidden_grad, far_first = tie(hidden_grad, far_first)
     first = stack_tensor(own_first, far_first)
-    hidden_grad = hidden_grads(c_all, second)
-    u_first, u_next, hidden_grad = tie(u_first, u_placed[1], hidden_grad)
-    u_second = swap_dp(u_next)
     back_first, *kept = run_experts(0, half, u_first, hidden_grad, first, ())
     back_second, hidden, pre_grad = run_experts(1, half, u_second, hidden_grad, first, kept)
     back_first, u_second = tie(back_first, u_second)
     back_first = swap_dp(back_first)
-    back_first, back_second = tie(back_first, back_second)
+    out_rows = jnp.einsum(
+        "krf,kfd->rd",
+        hidden.reshape(tensor_size, 2 * half_size, -1),
+        second,
+        preferred_element_type=F32,
+    )
+    out_rows = out_rows.astype(BF).reshape(experts_all, 2 * padded, model_width)
+    back_first, back_second, out_rows = tie(back_first, back_second, out_rows)
     back_second = swap_dp(back_second)
 
     gates = jnp.stack([extra_of(u_first), extra_of(u_second)], axis=1)[..., None]
-    out_rows, first_terms, first_near, second_terms, second_near = expert_grads(
-        gates.reshape(2 * half_size, 1), u_first, u_second, c_all, hidden, pre_grad, second
+    first_terms, first_near, second_terms, second_near = expert_grads(
+        gates.reshape(2 * half_size, 1), u_first, u_second, c_all, hidden, pre_grad
     )
 
     def near_sum(own, near):
@@ -744,8 +725,7 @@
     second_passed, *second_parts = near_terms(second_terms, second_near)
 
     out_grad = cotangent_rows.astype(F32)
-    back_second, out_rows = tie(back_second, out_rows)
-    returned = swap_dp(out_rows)
+    back_second, first_terms = tie(back_second, first_terms)
     gate_back = [extra_of(back_first), extra_of(back_second)]
     gate_back = [
         jnp.stack([v.astype(BF), (v - v.astype(BF).astype(F32)).astype(BF)], axis=-1)
@@ -761,37 +741,40 @@
         out_grad + rms * gained - scaled * rms * jnp.mean(gained * scaled, axis=-1, keepdims=True)
     )
     db_rows = residual_grad.astype(BF).reshape(tensor_size, seqs_here, part_len, model_width)
+    db_rows, out_rows = tie(db_rows, out_rows)
+    returned = swap_dp(out_rows)
     db_blocks = [lax.dynamic_index_in_dim(db_rows, me ^ k, 0, keepdims=False) for k in range(4)]
     db_blocks = db_blocks[:1] + [swap_tensor(db_blocks[k], k) for k in range(1, 4)]
-    *db_blocks, first_passed = tie(*db_blocks, first_passed)
-    first_far = swap_tensor(first_passed, 2)
-
     router_part = lax.dot_general(
         normed_moe, logit_grad, TN, precision=lax.Precision.HIGHEST, preferred_element_type=F32
     )
     moe_gain_part = jnp.sum(normed_grad * scaled, axis=0)
+    *db_blocks, first_passed, router_part, moe_gain_part = tie(
+        *db_blocks, first_passed, router_part, moe_gain_part
+    )
+    first_far = swap_tensor(first_passed, 2)
 
     partial, dw_far, dw_both, lines_far = attend_back(
         me, n1_seqs, db_blocks, kept_far, (w_far, w_both), None, heads_here, head_size
     )
     dw_both, first_far = tie(dw_both, first_far)
+    first_grad = sum(v.astype(F32) for v in (*first_parts, first_far)).reshape(expert_in.shape)
     far_term = near_sum(dw_far, dw_both).astype(BF)
-    partial, far_term = tie(partial, far_term)
+    partial, far_term, first_grad = tie(partial, far_term, first_grad)
     far_term = swap_tensor(far_term, 2)
     *normed_back, dw_own, dw_core, lines_near, gain_sums = attend_back(
         me, n1_seqs, db_blocks, kept_near, (w_own, w_core), partial, heads_here, head_size
     )
-    dw_core, far_term, returned = tie(dw_core, far_term, returned)
+    dw_core, far_term, returned, second_passed = tie(dw_core, far_term, returned, second_passed)
+    second_far = swap_tensor(second_passed, 2)
     owner_terms = (near_sum(dw_own, dw_core) + far_term.astype(F32)).astype(BF)
-    owner_terms, gain_sums, lines_near = tie(owner_terms, gain_sums, lines_near)
-    owner_grad = scatter_dp(owner_terms.reshape(dp_size, weight_rows, 4 * head_cols))
+    owner_terms, gain_sums, lines_near, *normed_back = tie(
+        owner_terms, gain_sums, lines_near, *normed_back
+    )
+    owner_terms = swap_dp(owner_terms.reshape(dp_size, weight_rows, 4 * head_cols))
 
     normed_back = normed_back[:1] + [swap_tensor(normed_back[k], k) for k in range(1, 4)]
-    *normed_back, second_passed, first_far = tie(*normed_back, second_passed, first_far)
-    second_far = swap_tensor(second_passed, 2)
-    first_grad = sum(v.astype(F32) for v in (*first_parts, first_far)).reshape(expert_in.shape)
-    second_grad = sum(v.astype(F32) for v in (*second_parts, second_far))
-    second_grad = second_grad.reshape(expert_out.shape)
+    owner_terms, returned, *normed_back = tie(owner_terms, returned, *normed_back)
     normed_back = by_xor(jnp.stack(normed_back), me)
     normed_back = normed_back.reshape(group_seqs, part_len, model_width).astype(F32)
     gained_in = normed_back * attn_gain_f
@@ -806,6 +789,9 @@
         slot_table, returned.reshape(2 * half_size, model_width)
     )
     block_output = block_output.astype(BF).reshape(group_seqs, part_len, model_width)
+    block_output, input_grad, second_far = tie(block_output, input_grad, second_far)
+    second_grad = sum(v.astype(F32) for v in (*second_parts, second_far))
+    second_grad = second_grad.reshape(expert_out.shape)
 
     line_sums = by_xor(jnp.concatenate([lines_near, lines_far], axis=0), me)
     low, high = line_sums[..., :TILE], line_sums[..., TILE:]
@@ -819,6 +805,7 @@
     size = sums.size
     sums = jnp.pad(sums, (0, -size % (8 * TILE))).reshape(-1, TILE)
     sums = sum_all(sums).reshape(-1)
+    owner_grad = jnp.sum(owner_terms.astype(F32), axis=0)
     totals, start = [], 0
     for v in small:
         totals.append(sums[start : start + v.size].reshape(v.shape))

time: 519 us -> 486 us (0.936)
  waiting for transfers between devices: 129 us -> 101 us
  Pallas kernels: 195 us -> 181 us
  matrix products: 41.8 us -> 49.7 us
    ppermute x25, waiting for transfers between devices: 80.4 us -> 54.3 us  [swap_tensor(): return lax.ppermute(block, 'tensor', [(i, i ^ bit) for i in range(size)])]
    pallas_call x1, Pallas kernels: 48.3 us -> 34.2 us  [expert_grads(): pl.pallas_call(expert_grads_kernel, grid=(chunks, 2), in_specs=[whole(gat...]
    dot_general x0 -> x1, matrix products: none -> 14 us  [local(): jnp.einsum('krf,kfd->rd', hidden.reshape(tensor_size, 2 * half_size, -1),...]
    unnamed x186 -> x170, local copies, waits for them, and re-layouts: 14.6 us -> 14 us
  transfers between devices with their start and end apart: 41 -> 41, of which waited for: 24 -> 27; matrix products, arithmetic and copies ran while one was open for 19% -> 19% of each run, Pallas kernels for 38% -> 38%
where the time goes in v3:
time: 486 us; the launch traced here: 481 us
  Pallas kernels  181 us (37%)
  waiting for transfers between devices  101 us (21%)
  starting transfers between devices  72.1 us (15%)
  matrix products  49.7 us (10%)
  other arithmetic  47.1 us (10%)
  local copies, waits for them, and re-layouts  27.2 us (6%)
    ppermute x25, waiting for transfers between devices, swap_tensor(): return lax.ppermute(block, 'tensor', [(i, i ^ bit) for i in range(size)])  54.3 us
    pallas_call x2, Pallas kernels, attend_back(): pl.pallas_call(functools.partial(attend_back_kernel, heads, head_size, la...  48.1 us
    pallas_call x2, Pallas kernels, run_experts(): pl.pallas_call(functools.partial(expert_kernel, slots), grid=(blocks, chu...  46.7 us
    all_to_all x7, starting transfers between devices, swap_dp(): return lax.all_to_all(buffer, 'dp', split_axis=0, concat_axis=0, tiled=True)  37.4 us
    pallas_call x2, Pallas kernels, attend(): pl.pallas_call(functools.partial(attend_kernel, heads, head_size, last, l...  36.8 us
    pallas_call x1, Pallas kernels, expert_grads(): pl.pallas_call(expert_grads_kernel, grid=(chunks, 2), in_specs=[whole(gat...  34.2 us
    ppermute x5, waiting for transfers between devices, sum_all(): lax.ppermute(values, axis, [(i, i ^ bit) for i in range(size)])  17.3 us
    ppermute x25, starting transfers between devices, swap_tensor(): return lax.ppermute(block, 'tensor', [(i, i ^ bit) for i in range(size)])  16.4 us
  transfers between devices with their start and end apart: 41, of which 27 were waited for; matrix products, arithmetic and copies ran while one was open for 19% of the time, Pallas kernels for 38%

profile of v3, /device:TPU:0, one launch (start us, length us, event | category | flops | bytes accessed | tf_op | source)
XLA Modules:
  0.0 480.7 jit_solution(9342673104026591465)
XLA Ops:
  2.6 4.1 collective-permute-start
  9.3 4.5 collective-permute-done
  16.8 3.7 all-to-all-start
  25.4 5.9 %fusion.20 = bf16[2048,768]{1,0:T(8,128)(2,1)} fusion(bf16[1024,768]{1,0:T(8,128)(2,1)S(1)} %bitcast.274, s32[1024]{0:T(1024)S(1)} %fusion.95), kind=kOutput, calls=%fused_computation.24 | convolution fusion | flops 3224895488 | bytes 4722688 | tf_op jit(solution)/shard_map/dot_general | solution.py:650
  31.3 6.5 %collective-permute-done.2 = bf16[4,96,768]{2,1,0:T(8,128)(2,1)S(1)} collective-permute-done((bf16[4,96,768]{2,1,0:T(8,128)(2,1)S(1)}, bf16[4,96,768]{2,1,0:T(8,128)(2,1)S(1)}, u32[]{:S(2)}, u32[]{:S(2)}) %collective-permute-start.2) | collective-permute-done | bytes 589856 | tf_op jit(solution)/shard_map/ppermute | solution.py:520
  41.7 6.2 %all-to-all-start.1 = ((bf16[8,256,768]{2,1,0:T(8,128)(2,1)}), bf16[8,256,768]{2,1,0:T(8,128)(2,1)S(1)}, u32[]{:S(2)}, u32[]{:S(2)}) async-start(bf16[8,256,768]{2,1,0:T(8,128)(2,1)} %bitcast.270), calls=%async_computation.1 | async-start | bytes 6291456 | tf_op jit(solution)/shard_map/all_to_all | solution.py:504
  55.5 18.1 %attend.2 = (f32[2,512,768]{2,1,0:T(8,128)}, bf16[2,2,512,576]{3,2,1,0:T(8,128)(2,1)}, bf16[2,2,512,192]{3,2,1,0:T(8,128)(2,1)S(1)}, bf16[2,2,3,512,512]{4,3,2,1,0:T(8,128)(2,1)}) custom-call(s32[1]{0:T(128)} %bitcast.2.refs_0_, bf16[4,2,128,768]{3,2,1,0:T(8,128)(2,1)S(1)} %copy-done.5, s32[2,512,1]{2,1,0:T(8,128)S(1)} %copy-done.7, ...), custom_call_target="tpu_custom_call" | custom-call | flops 9663676416 | bytes 12582912 | tf_op jit(solution)/shard_map/attend/pallas_call | solution.py:259
  73.6 3.8 collective-permute-done.4.refs_5_
  80.5 18.7 %attend.3 = (bf16[2,128,768]{2,1,0:T(8,128)(2,1)S(1)}, bf16[2,128,768]{2,1,0:T(8,128)(2,1)S(1)}, bf16[2,128,768]{2,1,0:T(8,128)(2,1)S(1)}, bf16[2,128,768]{2,1,0...) custom-call(s32[1]{0:T(128)} %bitcast.2.refs_0_, ...), custom_call_target="tpu_custom_call" | custom-call | flops 9663676416 | bytes 12582912 | tf_op jit(solution)/shard_map/attend/pallas_call | solution.py:259
  100.1 5.7 %collective-permute-done.6 = bf16[768,768]{1,0:T(8,128)(2,1)S(1)} collective-permute-done((bf16[768,768]{1,0:T(8,128)(2,1)S(1)}, bf16[768,768]{1,0:T(8,128)(2,1)S(1)}, u32[]{:S(2)}, u32[]{:S(2)}) %collective-permute-start.6) | collective-permute-done | bytes 1179680 | tf_op jit(solution)/shard_map/ppermute | solution.py:500
  108.8 8.9 %collective-permute-done.8 = bf16[2,128,768]{2,1,0:T(8,128)(2,1)S(1)} collective-permute-done((bf16[2,128,768]{2,1,0:T(8,128)(2,1)S(1)}, bf16[2,128,768]{2,1,0:T(8,128)(2,1)S(1)}, u32[]{:S(2)}, u32[]{:S(2)}) %collective-permute-start.8) | collective-permute-done | bytes 393248 | tf_op jit(solution)/shard_map/ppermute | solution.py:500
  118.5 7.0 %collective-permute-done.9 = bf16[2,128,768]{2,1,0:T(8,128)(2,1)} collective-permute-done((bf16[2,128,768]{2,1,0:T(8,128)(2,1)S(1)}, bf16[2,128,768]{2,1,0:T(8,128)(2,1)}, u32[]{:S(2)}, u32[]{:S(2)}) %collective-permute-start.9) | collective-permute-done | bytes 393248 | tf_op jit(solution)/shard_map/ppermute | solution.py:500
  125.5 3.0 maximum_select_fusion
  130.1 2.7 multiply_reduce_fusion.2
  138.0 3.1 select_convert_fusion.1
  141.1 6.0 %all-to-all-start.2 = ((bf16[8,128,768]{2,1,0:T(8,128)(2,1)}), bf16[8,128,768]{2,1,0:T(8,128)(2,1)}, u32[]{:S(2)}, u32[]{:S(2)}) async-start(bf16[8,128,768]{2,1,0:T(8,128)(2,1)} %select_convert_fusion.1), calls=%async_computation.2 | async-start | bytes 3145728 | tf_op jit(solution)/shard_map/all_to_all | solution.py:504
  151.8 4.1 pad_maximum_fusion.wo_ref
  156.8 3.1 select_convert_fusion
  159.8 15.1 %hidden_grads.1.hg_ref = bf16[4,8,2,128,768]{4,3,2,1,0:T(8,128)(2,1)} custom-call(bf16[8,2,128,768]{3,2,1,0:T(8,128)(2,1)S(1)} %bitcast.257, bf16[4,768,768]{2,1,0:T(8,128)(2,1)} %pad_maximum_fusion.wo_ref), custom_call_target="tpu_custom_call" | custom-call | flops 1 | bytes 1 | tf_op jit(solution)/shard_map/hidden_grads/pallas_call | solution.py:364
  175.0 9.6 %all-to-all-done.2.u_ref.ua_ref = bf16[8,128,768]{2,1,0:T(8,128)(2,1)} async-done(((bf16[8,128,768]{2,1,0:T(8,128)(2,1)}), bf16[8,128,768]{2,1,0:T(8,128)(2,1)}, u32[]{:S(2)}, u32[]{:S(2)}) %all-to-all-start.2) | async-done | bytes 1572896 | tf_op jit(solution)/shard_map/all_to_all | solution.py:504
  184.6 3.8 all-to-all-start.3
  193.2 3.5 pad_maximum_fusion.1.wi_ref
  196.7 23.4 %experts.2 = (bf16[8,128,768]{2,1,0:T(8,128)(2,1)}, bf16[4,8,2,128,768]{4,3,2,1,0:T(8,128)(2,1)}, bf16[4,8,2,128,768]{4,3,2,1,0:T(8,128)(2,1)}) custom-call(bf16[8,128,768]{2,1,0:T(8,128)(2,1)} %all-to-all-done.2.u_ref.ua_ref, bf16[4,8,2,128,768]{4,3,2,1,0:T(8,128)(2,1)} %hidden_grads.1.hg_ref, bf16[4,768,768]{2,1,0:T(8,128)(2,1)} %pad_maximum_fusion.1.wi_ref), custom_call_target="tpu_custom_call" | custom-call | flops 9663676416 | bytes 20971520 | tf_op jit(solution)/shard_map/experts/pallas_call | solution.py:473
  220.2 5.4 %all-to-all-done.3.u_ref.ub_ref = bf16[8,128,768]{2,1,0:T(8,128)(2,1)S(1)} async-done(((bf16[8,128,768]{2,1,0:T(8,128)(2,1)}), bf16[8,128,768]{2,1,0:T(8,128)(2,1)S(1)}, u32[]{:S(2)}, u32[]{:S(2)}) %all-to-all-start.3) | async-done | bytes 1572896 | tf_op jit(solution)/shard_map/all_to_all | solution.py:504
  225.6 3.6 all-to-all-start.4
  230.6 23.3 %experts.3 = (bf16[8,128,768]{2,1,0:T(8,128)(2,1)}, bf16[4,8,2,128,768]{4,3,2,1,0:T(8,128)(2,1)}, bf16[4,8,2,128,768]{4,3,2,1,0:T(8,128)(2,1)}) custom-call(bf16[8,128,768]{2,1,0:T(8,128)(2,1)S(1)} %all-to-all-done.3.u_ref.ub_ref, bf16[4,8,2,128,768]{4,3,2,1,0:T(8,128)(2,1)} %hidden_grads.1.hg_ref, ...), custom_call_target="tpu_custom_call", output_to_operand_aliasing={{1}: (3, {}), {2}: (4, {})} | custom-call | flops 9663676416 | bytes 20971520 | tf_op jit(solution)/shard_map/experts/pallas_call | solution.py:473
  254.0 14.0 %bitcast_convert_fusion = bf16[2048,768]{1,0:T(8,128)(2,1)} fusion(bf16[4,2048,768]{2,1,0:T(8,128)(2,1)} %bitcast.266, bf16[1,768,768]{2,1,0:T(8,128)(2,1)S(1)} %bitcast.292, bf16[1,768,768]{2,1,0:T(8,128)(2,1)S(1)} %bitcast.290, bf16[1,768,768]{2,1,0:T(8,128)(2,1)S(1)} %bitcast.288, bf16[1,768,768]{2,1,0:T(8,128)(2,1)S(1)} %copy-done.37), kind=kOutput, calls=%fused_computation.15 | convolution fusion | flops 9672327168 | bytes 20447232 | tf_op jit(solution)/shard_map/krf,kfd->rd/dot_general | solution.py:701
  268.0 6.0 %all-to-all-start.5 = ((bf16[8,128,768]{2,1,0:T(8,128)(2,1)}), bf16[8,128,768]{2,1,0:T(8,128)(2,1)S(1)}, u32[]{:S(2)}, u32[]{:S(2)}) async-start(bf16[8,128,768]{2,1,0:T(8,128)(2,1)} %get-tuple-element.152), calls=%async_computation.5 | async-start | bytes 3145728 | tf_op jit(solution)/shard_map/all_to_all | solution.py:504
  274.0 34.2 %expert_grads.1 = (bf16[2,768,768]{2,1,0:T(8,128)(2,1)}, bf16[2,768,768]{2,1,0:T(8,128)(2,1)}, bf16[2,768,768]{2,1,0:T(8,128)(2,1)}, bf16[2,768,768]{2,1,0:T(8,128)(2,1)}) custom-call(f32[2048,1]{1,0:T(8,128)} %copy.68.gate_ref, bf16[8,128,768]{2,1,0:T(8,128)(2,1)} %all-to-all-done.2.u_ref.ua_ref, bf16[8,128,768]{2,1,0:T(8,128)(2,1)} %copy-done.3, ...), custom_call_target="tpu_custom_call" | custom-call | flops 19327352832 | bytes 41943040 | tf_op jit(solution)/shard_map/expert_grads/pallas_call | solution.py:430
  308.4 3.6 fusion.10
  315.6 3.4 multiply_reduce_fusion
  319.0 2.8 fusion.105
  321.8 6.0 %all-to-all-start.6 = ((bf16[8,256,768]{2,1,0:T(8,128)(2,1)}), bf16[8,256,768]{2,1,0:T(8,128)(2,1)}, u32[]{:S(2)}, u32[]{:S(2)}) async-start(bf16[8,256,768]{2,1,0:T(8,128)(2,1)} %bitcast.269), calls=%async_computation.6 | async-start | bytes 6291456 | tf_op jit(solution)/shard_map/all_to_all | solution.py:504
  334.5 6.7 %collective-permute-done.16.refs_9_ = bf16[2,128,768]{2,1,0:T(8,128)(2,1)S(1)} collective-permute-done((bf16[2,128,768]{2,1,0:T(8,128)(2,1)S(1)}, bf16[2,128,768]{2,1,0:T(8,128)(2,1)S(1)}, u32[]{:S(2)}, u32[]{:S(2)}) %collective-permute-start.16) | collective-permute-done | bytes 393248 | tf_op jit(solution)/shard_map/ppermute | solution.py:500
  341.2 6.9 %collective-permute-done.17.refs_10_ = bf16[2,128,768]{2,1,0:T(8,128)(2,1)S(1)} collective-permute-done((bf16[2,128,768]{2,1,0:T(8,128)(2,1)S(1)}, bf16[2,128,768]{2,1,0:T(8,128)(2,1)S(1)}, u32[]{:S(2)}, u32[]{:S(2)}) %collective-permute-start.17) | collective-permute-done | bytes 393248 | tf_op jit(solution)/shard_map/ppermute | solution.py:500
  349.7 24.0 %attend_back.2 = (f32[2,512,768]{2,1,0:T(8,128)}, bf16[768,768]{1,0:T(8,128)(2,1)}, bf16[768,768]{1,0:T(8,128)(2,1)}, f32[2,3,8,256]{3,2,1,0:T(8,128)}) custom-call(s32[1]{0:T(128)} %bitcast.2.refs_0_, bf16[4,2,128,768]{3,2,1,0:T(8,128)(2,1)} %copy-done.4, bf16[2,2,512,576]{3,2,1,0:T(8,128)(2,1)} %get-tuple-element.164.refs_2_, ...), custom_call_target="tpu_custom_call" | custom-call | flops 12884901888 | bytes 16777216 | tf_op jit(solution)/shard_map/attend_back/pallas_call | solution.py:309
  373.7 3.4 collective-permute-done.19
  378.7 3.7 fusion.33
  384.3 24.2 %attend_back.3 = (bf16[2,128,768]{2,1,0:T(8,128)(2,1)}, bf16[2,128,768]{2,1,0:T(8,128)(2,1)}, bf16[2,128,768]{2,1,0:T(8,128)(2,1)}, bf16[2,128,768]{2,1,0:T(8,12...) custom-call(s32[1]{0:T(128)} %bitcast.2.refs_0_, ...), custom_call_target="tpu_custom_call" | custom-call | flops 12884901888 | bytes 16777216 | tf_op jit(solution)/shard_map/attend_back/pallas_call | solution.py:309
  414.3 3.1 add_convert_fusion.1
  417.4 5.8 %all-to-all-start.7 = ((bf16[8,96,768]{2,1,0:T(8,128)(2,1)}), bf16[8,96,768]{2,1,0:T(8,128)(2,1)S(1)}, u32[]{:S(2)}, u32[]{:S(2)}) async-start(bf16[8,96,768]{2,1,0:T(8,128)(2,1)} %bitcast.268), calls=%async_computation.7 | async-start | bytes 2359296 | tf_op jit(solution)/shard_map/all_to_all | solution.py:504
  431.6 3.2 collective-permute-done.30
  435.6 8.5 %collective-permute-done.31 = f32[64,128]{1,0:T(8,128)S(1)} collective-permute-done((f32[64,128]{1,0:T(8,128)S(1)}, f32[64,128]{1,0:T(8,128)S(1)}, u32[]{:S(2)}, u32[]{:S(2)}) %collective-permute-start.31) | collective-permute-done | bytes 32800 | tf_op jit(solution)/shard_map/ppermute | solution.py:533
  444.0 3.9 collective-permute-start.32
  449.5 3.9 collective-permute-done.32
  464.5 2.7 fusion.24
  467.2 6.9 %add_convert_fusion = bf16[1024,768]{1,0:T(8,128)(2,1)} fusion(f32[1024,768]{1,0:T(8,128)S(1)} %copy-done.19, bf16[2048,768]{1,0:T(8,128)(2,1)} %bitcast.78, s32[1024]{0:T(1024)S(1)} %copy-done.64, f32[1024]{0:T(1024)S(1)} %select_reduce_fusion), kind=kOutput, calls=%fused_computation.33 | convolution fusion | flops 3225681920 | bytes 7872512 | tf_op jit(solution)/shard_map/dot_general | solution.py:30
  476.7 3.8 fusion.32
  (328 shorter events, 95.2 us)
Async XLA Ops:
  0.6 47.9 %copy-start = (s32[8,512]{1,0:T(8,128)S(1)}, s32[8,512]{1,0:T(8,128)}, u32[]{:S(2)}) copy-start(s32[8,512]{1,0:T(8,128)} %param.18) | copy-start | bytes 49156
  2.6 11.1 %collective-permute-start = (bf16[1,96,768]{2,1,0:T(8,128)(2,1)S(1)}, bf16[1,96,768]{2,1,0:T(8,128)(2,1)S(1)}, u32[]{:S(2)}, u32[]{:S(2)}) collective-permute-start(bf16[1,96,768]{2,1,0:T(8,128)(2,1)S(1)} %bitcast.295), channel_id=1, source_target_pairs={{0,16},{4,20},{8,24},{12,28},{16,0},{20,4},{24,8},{28,12},{1,17},{... | collective-permute-start | bytes 442376 | tf_op jit(solution)/shard_map/ppermute | solution.py:520
  14.5 8.5 %collective-permute-start.1 = (bf16[2,96,768]{2,1,0:T(8,128)(2,1)}, bf16[2,96,768]{2,1,0:T(8,128)(2,1)}, u32[]{:S(2)}, u32[]{:S(2)}) collective-permute-start(bf16[2,96,768]{2,1,0:T(8,128)(2,1)} %maximum_bitcast_fusion), channel_id=1, source_target_pairs={{0,8},{4,12},{8,0},{12,4},{16,24},{20,28},{24,16},{28,20},{1,9},{5... | collective-permute-start | bytes 884744 | tf_op jit(solution)/shard_map/ppermute | solution.py:520
  16.8 23.8 %all-to-all-start = ((bf16[4,2,128,768]{3,2,1,0:T(8,128)(2,1)}), bf16[4,2,128,768]{3,2,1,0:T(8,128)(2,1)S(1)}, u32[]{:S(2)}, u32[]{:S(2)}) async-start(bf16[4,2,128,768]{3,2,1,0:T(8,128)(2,1)} %bitcast.7), calls=%async_computation | async-start | bytes 3145728 | tf_op jit(solution)/shard_map/all_to_all | solution.py:508
  24.1 13.7 %collective-permute-start.2 = (bf16[4,96,768]{2,1,0:T(8,128)(2,1)S(1)}, bf16[4,96,768]{2,1,0:T(8,128)(2,1)S(1)}, u32[]{:S(2)}, u32[]{:S(2)}) collective-permute-start(bf16[4,96,768]{2,1,0:T(8,128)(2,1)S(1)} %bitcast.271), channel_id=1, source_target_pairs={{0,4},{4,0},{8,12},{12,8},{16,20},{20,16},{24,28},{28,24},{1,5},{5... | collective-permute-start | bytes 1769480 | tf_op jit(solution)/shard_map/ppermute | solution.py:520
  41.7 83.7 %all-to-all-start.1 = ((bf16[8,256,768]{2,1,0:T(8,128)(2,1)}), bf16[8,256,768]{2,1,0:T(8,128)(2,1)S(1)}, u32[]{:S(2)}, u32[]{:S(2)}) async-start(bf16[8,256,768]{2,1,0:T(8,128)(2,1)} %bitcast.270), calls=%async_computation.1 | async-start | bytes 6291456 | tf_op jit(solution)/shard_map/all_to_all | solution.py:504
  48.5 3.3 collective-permute-start.3
  48.7 28.7 %collective-permute-start.4 = (bf16[768,768]{1,0:T(8,128)(2,1)}, bf16[768,768]{1,0:T(8,128)(2,1)}, u32[]{:S(2)}, u32[]{:S(2)}) collective-permute-start(bf16[768,768]{1,0:T(8,128)(2,1)} %bitcast.262), channel_id=1, source_target_pairs={{0,2},{1,3},{2,0},{3,1},{4,6},{5,7},{6,4},{7,5},{8,10},{9,11},{10,... | collective-permute-start | bytes 3538952 | tf_op jit(solution)/shard_map/ppermute | solution.py:500
  73.6 25.6 %copy-start.11 = (bf16[2,2,512,192]{3,2,1,0:T(8,128)(2,1)}, bf16[2,2,512,192]{3,2,1,0:T(8,128)(2,1)S(1)}, u32[]{:S(2)}) copy-start(bf16[2,2,512,192]{3,2,1,0:T(8,128)(2,1)S(1)} %get-tuple-element.133.refs_3_) | copy-start | bytes 2359300
  77.4 3.1 collective-permute-start.5
  77.4 28.4 %collective-permute-start.6 = (bf16[768,768]{1,0:T(8,128)(2,1)S(1)}, bf16[768,768]{1,0:T(8,128)(2,1)S(1)}, u32[]{:S(2)}, u32[]{:S(2)}) collective-permute-start(bf16[768,768]{1,0:T(8,128)(2,1)S(1)} %bitcast.286), channel_id=1, source_target_pairs={{0,2},{1,3},{2,0},{3,1},{4,6},{5,7},{6,4},{7,5},{8,10},{9,11},{10,... | collective-permute-start | bytes 3538952 | tf_op jit(solution)/shard_map/ppermute | solution.py:500
  105.8 3.0 collective-permute-start.7
  105.8 11.9 %collective-permute-start.8 = (bf16[2,128,768]{2,1,0:T(8,128)(2,1)S(1)}, bf16[2,128,768]{2,1,0:T(8,128)(2,1)S(1)}, u32[]{:S(2)}, u32[]{:S(2)}) collective-permute-start(bf16[2,128,768]{2,1,0:T(8,128)(2,1)S(1)} %get-tuple-element.125), channel_id=1, source_target_pairs={{0,2},{1,3},{2,0},{3,1},{4,6},{5,7},{6,4},{7,5},{8,10},{9,11},{10,... | collective-permute-start | bytes 1179656 | tf_op jit(solution)/shard_map/ppermute | solution.py:500
  107.3 18.1 %collective-permute-start.9 = (bf16[2,128,768]{2,1,0:T(8,128)(2,1)S(1)}, bf16[2,128,768]{2,1,0:T(8,128)(2,1)}, u32[]{:S(2)}, u32[]{:S(2)}) collective-permute-start(bf16[2,128,768]{2,1,0:T(8,128)(2,1)S(1)} %get-tuple-element.126), channel_id=1, source_target_pairs={{0,3},{1,2},{2,1},{3,0},{4,7},{5,6},{6,5},{7,4},{8,11},{9,10},{10,... | collective-permute-start | bytes 1179656 | tf_op jit(solution)/shard_map/ppermute | solution.py:500
  125.5 34.4 %copy-start.2 = (bf16[8,256,768]{2,1,0:T(8,128)(2,1)}, bf16[8,256,768]{2,1,0:T(8,128)(2,1)S(1)}, u32[]{:S(2)}) copy-start(bf16[8,256,768]{2,1,0:T(8,128)(2,1)S(1)} %all-to-all-done.1) | copy-start | bytes 9437188
  141.1 43.5 %all-to-all-start.2 = ((bf16[8,128,768]{2,1,0:T(8,128)(2,1)}), bf16[8,128,768]{2,1,0:T(8,128)(2,1)}, u32[]{:S(2)}, u32[]{:S(2)}) async-start(bf16[8,128,768]{2,1,0:T(8,128)(2,1)} %select_convert_fusion.1), calls=%async_computation.2 | async-start | bytes 3145728 | tf_op jit(solution)/shard_map/all_to_all | solution.py:504
  147.1 3.1 collective-permute-start.10
  147.1 4.7 collective-permute-start.11
  147.6 40.9 %collective-permute-start.12 = (bf16[768,768]{1,0:T(8,128)(2,1)}, bf16[768,768]{1,0:T(8,128)(2,1)}, u32[]{:S(2)}, u32[]{:S(2)}) collective-permute-start(bf16[768,768]{1,0:T(8,128)(2,1)} %bitcast.283), channel_id=1, source_target_pairs={{0,2},{1,3},{2,0},{3,1},{4,6},{5,7},{6,4},{7,5},{8,10},{9,11},{10,... | collective-permute-start | bytes 3538952 | tf_op jit(solution)/shard_map/ppermute | solution.py:500
  184.6 41.0 %all-to-all-start.3 = ((bf16[8,128,768]{2,1,0:T(8,128)(2,1)}), bf16[8,128,768]{2,1,0:T(8,128)(2,1)S(1)}, u32[]{:S(2)}, u32[]{:S(2)}) async-start(bf16[8,128,768]{2,1,0:T(8,128)(2,1)} %select_convert_fusion), calls=%async_computation.3 | async-start | bytes 3145728 | tf_op jit(solution)/shard_map/all_to_all | solution.py:504
  188.4 3.7 collective-permute-start.13
  188.5 4.7 collective-permute-start.14
  225.6 28.4 %copy-start.3 = (bf16[8,128,768]{2,1,0:T(8,128)(2,1)}, bf16[8,128,768]{2,1,0:T(8,128)(2,1)S(1)}, u32[]{:S(2)}) copy-start(bf16[8,128,768]{2,1,0:T(8,128)(2,1)S(1)} %all-to-all-done.3.u_ref.ub_ref) | copy-start | bytes 4718596
  225.6 42.4 %all-to-all-start.4 = ((bf16[8,128,768]{2,1,0:T(8,128)(2,1)}), bf16[8,128,768]{2,1,0:T(8,128)(2,1)S(1)}, u32[]{:S(2)}, u32[]{:S(2)}) async-start(bf16[8,128,768]{2,1,0:T(8,128)(2,1)} %get-tuple-element.146), calls=%async_computation.4 | async-start | bytes 3145728 | tf_op jit(solution)/shard_map/all_to_all | solution.py:504
  268.0 44.0 %all-to-all-start.5 = ((bf16[8,128,768]{2,1,0:T(8,128)(2,1)}), bf16[8,128,768]{2,1,0:T(8,128)(2,1)S(1)}, u32[]{:S(2)}, u32[]{:S(2)}) async-start(bf16[8,128,768]{2,1,0:T(8,128)(2,1)} %get-tuple-element.152), calls=%async_computation.5 | async-start | bytes 3145728 | tf_op jit(solution)/shard_map/all_to_all | solution.py:504
  308.2 22.6 %collective-permute-start.18 = (bf16[2,768,768]{2,1,0:T(8,128)(2,1)}, bf16[2,768,768]{2,1,0:T(8,128)(2,1)}, u32[]{:S(2)}, u32[]{:S(2)}) collective-permute-start(bf16[2,768,768]{2,1,0:T(8,128)(2,1)} %get-tuple-element.159), channel_id=1, source_target_pairs={{0,1},{1,0},{2,3},{3,2},{4,5},{5,4},{6,7},{7,6},{8,9},{9,8},{10,11... | collective-permute-start | bytes 7077896 | tf_op jit(solution)/shard_map/ppermute | solution.py:500
  321.8 89.3 %all-to-all-start.6 = ((bf16[8,256,768]{2,1,0:T(8,128)(2,1)}), bf16[8,256,768]{2,1,0:T(8,128)(2,1)}, u32[]{:S(2)}, u32[]{:S(2)}) async-start(bf16[8,256,768]{2,1,0:T(8,128)(2,1)} %bitcast.269), calls=%async_computation.6 | async-start | bytes 6291456 | tf_op jit(solution)/shard_map/all_to_all | solution.py:504
  327.8 49.4 %collective-permute-start.22 = (bf16[2,768,768]{2,1,0:T(8,128)(2,1)}, bf16[2,768,768]{2,1,0:T(8,128)(2,1)S(1)}, u32[]{:S(2)}, u32[]{:S(2)}) collective-permute-start(bf16[2,768,768]{2,1,0:T(8,128)(2,1)} %get-tuple-element.179), channel_id=1, source_target_pairs={{0,1},{1,0},{2,3},{3,2},{4,5},{5,4},{6,7},{7,6},{8,9},{9,8},{10,11... | collective-permute-start | bytes 7077896 | tf_op jit(solution)/shard_map/ppermute | solution.py:500
  329.0 5.5 %collective-permute-start.15 = (bf16[2,128,768]{2,1,0:T(8,128)(2,1)S(1)}, bf16[2,128,768]{2,1,0:T(8,128)(2,1)S(1)}, u32[]{:S(2)}, u32[]{:S(2)}) collective-permute-start(bf16[2,128,768]{2,1,0:T(8,128)(2,1)S(1)} %get-tuple-element.260), channel_id=1, source_target_pairs={{0,1},{1,0},{2,3},{3,2},{4,5},{5,4},{6,7},{7,6},{8,9},{9,8},{10,11... | collective-permute-start | bytes 1179656 | tf_op jit(solution)/shard_map/ppermute | solution.py:500
  329.3 12.0 %collective-permute-start.16 = (bf16[2,128,768]{2,1,0:T(8,128)(2,1)S(1)}, bf16[2,128,768]{2,1,0:T(8,128)(2,1)S(1)}, u32[]{:S(2)}, u32[]{:S(2)}) collective-permute-start(bf16[2,128,768]{2,1,0:T(8,128)(2,1)S(1)} %get-tuple-element.259), channel_id=1, source_target_pairs={{0,2},{1,3},{2,0},{3,1},{4,6},{5,7},{6,4},{7,5},{8,10},{9,11},{10,... | collective-permute-start | bytes 1179656 | tf_op jit(solution)/shard_map/ppermute | solution.py:500
  330.8 17.4 %collective-permute-start.17 = (bf16[2,128,768]{2,1,0:T(8,128)(2,1)S(1)}, bf16[2,128,768]{2,1,0:T(8,128)(2,1)S(1)}, u32[]{:S(2)}, u32[]{:S(2)}) collective-permute-start(bf16[2,128,768]{2,1,0:T(8,128)(2,1)S(1)} %get-tuple-element.258), channel_id=1, source_target_pairs={{0,3},{1,2},{2,1},{3,0},{4,7},{5,6},{6,5},{7,4},{8,11},{9,10},{10,... | collective-permute-start | bytes 1179656 | tf_op jit(solution)/shard_map/ppermute | solution.py:500
  348.2 28.9 %collective-permute-start.19 = (bf16[768,768]{1,0:T(8,128)(2,1)S(1)}, bf16[768,768]{1,0:T(8,128)(2,1)}, u32[]{:S(2)}, u32[]{:S(2)}) collective-permute-start(bf16[768,768]{1,0:T(8,128)(2,1)S(1)} %fusion.58), channel_id=1, source_target_pairs={{0,2},{1,3},{2,0},{3,1},{4,6},{5,7},{6,4},{7,5},{8,10},{9,11},{10,... | collective-permute-start | bytes 3538952 | tf_op jit(solution)/shard_map/ppermute | solution.py:500
  349.7 27.5 %copy-start.22 = (bf16[2,768,768]{2,1,0:T(8,128)(2,1)S(1)}, bf16[2,768,768]{2,1,0:T(8,128)(2,1)}, u32[]{:S(2)}) copy-start(bf16[2,768,768]{2,1,0:T(8,128)(2,1)} %get-tuple-element.178) | copy-start | bytes 7077892
  377.1 5.3 %collective-permute-start.20 = (bf16[768,768]{1,0:T(8,128)(2,1)}, bf16[768,768]{1,0:T(8,128)(2,1)S(1)}, u32[]{:S(2)}, u32[]{:S(2)}) collective-permute-start(bf16[768,768]{1,0:T(8,128)(2,1)} %get-tuple-element.171), channel_id=1, source_target_pairs={{0,1},{1,0},{2,3},{3,2},{4,5},{5,4},{6,7},{7,6},{8,9},{9,8},{10,11... | collective-permute-start | bytes 3538952 | tf_op jit(solution)/shard_map/ppermute | solution.py:500
  382.7 28.4 %collective-permute-start.21 = (bf16[768,768]{1,0:T(8,128)(2,1)S(1)}, bf16[768,768]{1,0:T(8,128)(2,1)S(1)}, u32[]{:S(2)}, u32[]{:S(2)}) collective-permute-start(bf16[768,768]{1,0:T(8,128)(2,1)S(1)} %add_convert_fusion.3), channel_id=1, source_target_pairs={{0,2},{1,3},{2,0},{3,1},{4,6},{5,7},{6,4},{7,5},{8,10},{9,11},{10,... | collective-permute-start | bytes 3538952 | tf_op jit(solution)/shard_map/ppermute | solution.py:500
  384.3 27.8 %copy-start.46 = (f32[2,3,8,256]{3,2,1,0:T(8,128)S(1)}, f32[2,3,8,256]{3,2,1,0:T(8,128)}, u32[]{:S(2)}) copy-start(f32[2,3,8,256]{3,2,1,0:T(8,128)} %get-tuple-element.206) | copy-start | bytes 147460
  411.1 3.2 collective-permute-start.23
  417.4 40.5 %copy-start.30 = (bf16[2,128,768]{2,1,0:T(8,128)(2,1)S(1)}, bf16[2,128,768]{2,1,0:T(8,128)(2,1)}, u32[]{:S(2)}) copy-start(bf16[2,128,768]{2,1,0:T(8,128)(2,1)} %get-tuple-element.196) | copy-start | bytes 1179652
  417.4 40.5 %all-to-all-start.7 = ((bf16[8,96,768]{2,1,0:T(8,128)(2,1)}), bf16[8,96,768]{2,1,0:T(8,128)(2,1)S(1)}, u32[]{:S(2)}, u32[]{:S(2)}) async-start(bf16[8,96,768]{2,1,0:T(8,128)(2,1)} %bitcast.268), calls=%async_computation.7 | async-start | bytes 2359296 | tf_op jit(solution)/shard_map/all_to_all | solution.py:504
  424.2 1.3 collective-permute-start.28
  425.5 4.0 collective-permute-start.29
  427.1 30.8 %collective-permute-start.24 = (bf16[2,128,768]{2,1,0:T(8,128)(2,1)}, bf16[2,128,768]{2,1,0:T(8,128)(2,1)}, u32[]{:S(2)}, u32[]{:S(2)}) collective-permute-start(bf16[2,128,768]{2,1,0:T(8,128)(2,1)} %get-tuple-element.191), channel_id=1, source_target_pairs={{0,1},{1,0},{2,3},{3,2},{4,5},{5,4},{6,7},{7,6},{8,9},{9,8},{10,11... | collective-permute-start | bytes 1179656 | tf_op jit(solution)/shard_map/ppermute | solution.py:500
  427.1 30.8 %collective-permute-start.25 = (bf16[2,128,768]{2,1,0:T(8,128)(2,1)}, bf16[2,128,768]{2,1,0:T(8,128)(2,1)}, u32[]{:S(2)}, u32[]{:S(2)}) collective-permute-start(bf16[2,128,768]{2,1,0:T(8,128)(2,1)} %get-tuple-element.192), channel_id=1, source_target_pairs={{0,2},{1,3},{2,0},{3,1},{4,6},{5,7},{6,4},{7,5},{8,10},{9,11},{10,... | collective-permute-start | bytes 1179656 | tf_op jit(solution)/shard_map/ppermute | solution.py:500
  427.6 30.3 %collective-permute-start.26 = (bf16[2,128,768]{2,1,0:T(8,128)(2,1)}, bf16[2,128,768]{2,1,0:T(8,128)(2,1)}, u32[]{:S(2)}, u32[]{:S(2)}) collective-permute-start(bf16[2,128,768]{2,1,0:T(8,128)(2,1)} %get-tuple-element.193), channel_id=1, source_target_pairs={{0,3},{1,2},{2,1},{3,0},{4,7},{5,6},{6,5},{7,4},{8,11},{9,10},{10,... | collective-permute-start | bytes 1179656 | tf_op jit(solution)/shard_map/ppermute | solution.py:500
  429.5 5.3 %collective-permute-start.30 = (f32[64,128]{1,0:T(8,128)S(1)}, f32[64,128]{1,0:T(8,128)S(1)}, u32[]{:S(2)}, u32[]{:S(2)}) collective-permute-start(f32[64,128]{1,0:T(8,128)S(1)} %fusion.128), channel_id=1, source_target_pairs={{0,4},{4,0},{8,12},{12,8},{16,20},{20,16},{24,28},{28,24},{1,5},{5... | collective-permute-start | bytes 98312 | tf_op jit(solution)/shard_map/ppermute | solution.py:533
  434.8 9.2 %collective-permute-start.31 = (f32[64,128]{1,0:T(8,128)S(1)}, f32[64,128]{1,0:T(8,128)S(1)}, u32[]{:S(2)}, u32[]{:S(2)}) collective-permute-start(f32[64,128]{1,0:T(8,128)S(1)} %add.183), channel_id=1, source_target_pairs={{0,8},{4,12},{8,0},{12,4},{16,24},{20,28},{24,16},{28,20},{1,9},{5... | collective-permute-start | bytes 98312 | tf_op jit(solution)/shard_map/ppermute | solution.py:533
  444.0 9.4 %collective-permute-start.32 = (f32[64,128]{1,0:T(8,128)S(1)}, f32[64,128]{1,0:T(8,128)S(1)}, u32[]{:S(2)}, u32[]{:S(2)}) collective-permute-start(f32[64,128]{1,0:T(8,128)S(1)} %add.184), channel_id=1, source_target_pairs={{0,16},{4,20},{8,24},{12,28},{16,0},{20,4},{24,8},{28,12},{1,17},{... | collective-permute-start | bytes 98312 | tf_op jit(solution)/shard_map/ppermute | solution.py:533
  448.0 27.1 %collective-permute-start.27 = (bf16[768,768]{1,0:T(8,128)(2,1)}, bf16[768,768]{1,0:T(8,128)(2,1)}, u32[]{:S(2)}, u32[]{:S(2)}) collective-permute-start(bf16[768,768]{1,0:T(8,128)(2,1)} %fusion.59), channel_id=1, source_target_pairs={{0,2},{1,3},{2,0},{3,1},{4,6},{5,7},{6,4},{7,5},{8,10},{9,11},{10,... | collective-permute-start | bytes 3538952 | tf_op jit(solution)/shard_map/ppermute | solution.py:500
  (71 other events, 473.4 us)

commit v4 on v3

--- a/solution.py
+++ b/solution.py
@@ -774,7 +774,7 @@
     owner_terms = swap_dp(owner_terms.reshape(dp_size, weight_rows, 4 * head_cols))
 
     normed_back = normed_back[:1] + [swap_tensor(normed_back[k], k) for k in range(1, 4)]
-    owner_terms, returned, *normed_back = tie(owner_terms, returned, *normed_back)
+    owner_terms, second_far, *normed_back = tie(owner_terms, second_far, *normed_back)
     normed_back = by_xor(jnp.stack(normed_back), me)
     normed_back = normed_back.reshape(group_seqs, part_len, model_width).astype(F32)
     gained_in = normed_back * attn_gain_f
@@ -789,7 +789,6 @@
         slot_table, returned.reshape(2 * half_size, model_width)
     )
     block_output = block_output.astype(BF).reshape(group_seqs, part_len, model_width)
-    block_output, input_grad, second_far = tie(block_output, input_grad, second_far)
     second_grad = sum(v.astype(F32) for v in (*second_parts, second_far))
     second_grad = second_grad.reshape(expert_out.shape)
 

time: 486 us -> 492 us (1.012)
  waiting for transfers between devices: 101 us -> 107 us
    ppermute x25, waiting for transfers between devices: 54.3 us -> 64.1 us  [swap_tensor(): return lax.ppermute(block, 'tensor', [(i, i ^ bit) for i in range(size)])]
    unnamed x170 -> x168, local copies, waits for them, and re-layouts: 14 us -> 13.4 us
  transfers between devices with their start and end apart: 41 -> 41, of which waited for: 27 -> 27; matrix products, arithmetic and copies ran while one was open for 19% -> 17% of each run, Pallas kernels for 38% -> 37%
where the time goes in v4:
time: 492 us; the launch traced here: 486 us
  Pallas kernels  181 us (37%)
  waiting for transfers between devices  107 us (22%)
  starting transfers between devices  71.3 us (14%)
  matrix products  49.6 us (10%)
  other arithmetic  48.7 us (10%)
  local copies, waits for them, and re-layouts  26.6 us (5%)
    ppermute x25, waiting for transfers between devices, swap_tensor(): return lax.ppermute(block, 'tensor', [(i, i ^ bit) for i in range(size)])  64.1 us
    pallas_call x2, Pallas kernels, attend_back(): pl.pallas_call(functools.partial(attend_back_kernel, heads, head_size, la...  48.1 us
    pallas_call x2, Pallas kernels, run_experts(): pl.pallas_call(functools.partial(expert_kernel, slots), grid=(blocks, chu...  46.8 us
    all_to_all x7, starting transfers between devices, swap_dp(): return lax.all_to_all(buffer, 'dp', split_axis=0, concat_axis=0, tiled=True)  37.3 us
    pallas_call x2, Pallas kernels, attend(): pl.pallas_call(functools.partial(attend_kernel, heads, head_size, last, l...  36.8 us
    pallas_call x1, Pallas kernels, expert_grads(): pl.pallas_call(expert_grads_kernel, grid=(chunks, 2), in_specs=[whole(gat...  34.2 us
    ppermute x25, starting transfers between devices, swap_tensor(): return lax.ppermute(block, 'tensor', [(i, i ^ bit) for i in range(size)])  15.4 us
    pallas_call x1, Pallas kernels, hidden_grads(): pl.pallas_call(hidden_grads_kernel, grid=(chunks, experts // sources), in...  15.1 us
  transfers between devices with their start and end apart: 41, of which 27 were waited for; matrix products, arithmetic and copies ran while one was open for 17% of the time, Pallas kernels for 37%

profile of v4, /device:TPU:0, one launch (start us, length us, event | category | flops | bytes accessed | tf_op | source)
XLA Modules:
  0.0 486.2 jit_solution(117246356252978012)
XLA Ops:
  2.6 4.1 collective-permute-start
  9.3 4.5 collective-permute-done
  16.8 3.7 all-to-all-start
  25.4 5.9 %fusion.20 = bf16[2048,768]{1,0:T(8,128)(2,1)} fusion(bf16[1024,768]{1,0:T(8,128)(2,1)S(1)} %bitcast.274, s32[1024]{0:T(1024)S(1)} %fusion.95), kind=kOutput, calls=%fused_computation.24 | convolution fusion | flops 3224895488 | bytes 4722688 | tf_op jit(solution)/shard_map/dot_general | solution.py:650
  31.3 6.5 %collective-permute-done.2 = bf16[4,96,768]{2,1,0:T(8,128)(2,1)S(1)} collective-permute-done((bf16[4,96,768]{2,1,0:T(8,128)(2,1)S(1)}, bf16[4,96,768]{2,1,0:T(8,128)(2,1)S(1)}, u32[]{:S(2)}, u32[]{:S(2)}) %collective-permute-start.2) | collective-permute-done | bytes 589856 | tf_op jit(solution)/shard_map/ppermute | solution.py:520
  41.7 6.2 %all-to-all-start.1 = ((bf16[8,256,768]{2,1,0:T(8,128)(2,1)}), bf16[8,256,768]{2,1,0:T(8,128)(2,1)S(1)}, u32[]{:S(2)}, u32[]{:S(2)}) async-start(bf16[8,256,768]{2,1,0:T(8,128)(2,1)} %bitcast.270), calls=%async_computation.1 | async-start | bytes 6291456 | tf_op jit(solution)/shard_map/all_to_all | solution.py:504
  55.4 18.1 %attend.2 = (f32[2,512,768]{2,1,0:T(8,128)}, bf16[2,2,512,576]{3,2,1,0:T(8,128)(2,1)}, bf16[2,2,512,192]{3,2,1,0:T(8,128)(2,1)S(1)}, bf16[2,2,3,512,512]{4,3,2,1,0:T(8,128)(2,1)}) custom-call(s32[1]{0:T(128)} %bitcast.2.refs_0_, bf16[4,2,128,768]{3,2,1,0:T(8,128)(2,1)S(1)} %copy-done.5, s32[2,512,1]{2,1,0:T(8,128)S(1)} %copy-done.7, ...), custom_call_target="tpu_custom_call" | custom-call | flops 9663676416 | bytes 12582912 | tf_op jit(solution)/shard_map/attend/pallas_call | solution.py:259
  73.6 3.8 collective-permute-done.4.refs_5_
  80.5 18.7 %attend.3 = (bf16[2,128,768]{2,1,0:T(8,128)(2,1)S(1)}, bf16[2,128,768]{2,1,0:T(8,128)(2,1)S(1)}, bf16[2,128,768]{2,1,0:T(8,128)(2,1)S(1)}, bf16[2,128,768]{2,1,0...) custom-call(s32[1]{0:T(128)} %bitcast.2.refs_0_, ...), custom_call_target="tpu_custom_call" | custom-call | flops 9663676416 | bytes 12582912 | tf_op jit(solution)/shard_map/attend/pallas_call | solution.py:259
  100.1 5.6 %collective-permute-done.6 = bf16[768,768]{1,0:T(8,128)(2,1)S(1)} collective-permute-done((bf16[768,768]{1,0:T(8,128)(2,1)S(1)}, bf16[768,768]{1,0:T(8,128)(2,1)S(1)}, u32[]{:S(2)}, u32[]{:S(2)}) %collective-permute-start.6) | collective-permute-done | bytes 1179680 | tf_op jit(solution)/shard_map/ppermute | solution.py:500
  108.8 8.9 %collective-permute-done.8 = bf16[2,128,768]{2,1,0:T(8,128)(2,1)S(1)} collective-permute-done((bf16[2,128,768]{2,1,0:T(8,128)(2,1)S(1)}, bf16[2,128,768]{2,1,0:T(8,128)(2,1)S(1)}, u32[]{:S(2)}, u32[]{:S(2)}) %collective-permute-start.8) | collective-permute-done | bytes 393248 | tf_op jit(solution)/shard_map/ppermute | solution.py:500
  118.4 7.0 %collective-permute-done.9 = bf16[2,128,768]{2,1,0:T(8,128)(2,1)} collective-permute-done((bf16[2,128,768]{2,1,0:T(8,128)(2,1)S(1)}, bf16[2,128,768]{2,1,0:T(8,128)(2,1)}, u32[]{:S(2)}, u32[]{:S(2)}) %collective-permute-start.9) | collective-permute-done | bytes 393248 | tf_op jit(solution)/shard_map/ppermute | solution.py:500
  125.5 3.0 maximum_select_fusion
  138.0 3.1 select_convert_fusion.1
  141.1 6.0 %all-to-all-start.2 = ((bf16[8,128,768]{2,1,0:T(8,128)(2,1)}), bf16[8,128,768]{2,1,0:T(8,128)(2,1)}, u32[]{:S(2)}, u32[]{:S(2)}) async-start(bf16[8,128,768]{2,1,0:T(8,128)(2,1)} %select_convert_fusion.1), calls=%async_computation.2 | async-start | bytes 3145728 | tf_op jit(solution)/shard_map/all_to_all | solution.py:504
  151.8 4.1 pad_maximum_fusion.wo_ref
  156.8 3.1 select_convert_fusion
  159.8 15.1 %hidden_grads.1.hg_ref = bf16[4,8,2,128,768]{4,3,2,1,0:T(8,128)(2,1)} custom-call(bf16[8,2,128,768]{3,2,1,0:T(8,128)(2,1)S(1)} %bitcast.257, bf16[4,768,768]{2,1,0:T(8,128)(2,1)} %pad_maximum_fusion.wo_ref), custom_call_target="tpu_custom_call" | custom-call | flops 1 | bytes 1 | tf_op jit(solution)/shard_map/hidden_grads/pallas_call | solution.py:364
  175.0 9.6 %all-to-all-done.2.u_ref.ua_ref = bf16[8,128,768]{2,1,0:T(8,128)(2,1)} async-done(((bf16[8,128,768]{2,1,0:T(8,128)(2,1)}), bf16[8,128,768]{2,1,0:T(8,128)(2,1)}, u32[]{:S(2)}, u32[]{:S(2)}) %all-to-all-start.2) | async-done | bytes 1572896 | tf_op jit(solution)/shard_map/all_to_all | solution.py:504
  184.6 3.8 all-to-all-start.3
  193.2 3.5 pad_maximum_fusion.1.wi_ref
  196.7 23.5 %experts.2 = (bf16[8,128,768]{2,1,0:T(8,128)(2,1)}, bf16[4,8,2,128,768]{4,3,2,1,0:T(8,128)(2,1)}, bf16[4,8,2,128,768]{4,3,2,1,0:T(8,128)(2,1)}) custom-call(bf16[8,128,768]{2,1,0:T(8,128)(2,1)} %all-to-all-done.2.u_ref.ua_ref, bf16[4,8,2,128,768]{4,3,2,1,0:T(8,128)(2,1)} %hidden_grads.1.hg_ref, bf16[4,768,768]{2,1,0:T(8,128)(2,1)} %pad_maximum_fusion.1.wi_ref), custom_call_target="tpu_custom_call" | custom-call | flops 9663676416 | bytes 20971520 | tf_op jit(solution)/shard_map/experts/pallas_call | solution.py:473
  220.2 5.3 %all-to-all-done.3.u_ref.ub_ref = bf16[8,128,768]{2,1,0:T(8,128)(2,1)S(1)} async-done(((bf16[8,128,768]{2,1,0:T(8,128)(2,1)}), bf16[8,128,768]{2,1,0:T(8,128)(2,1)S(1)}, u32[]{:S(2)}, u32[]{:S(2)}) %all-to-all-start.3) | async-done | bytes 1572896 | tf_op jit(solution)/shard_map/all_to_all | solution.py:504
  225.5 3.6 all-to-all-start.4
  230.6 23.4 %experts.3 = (bf16[8,128,768]{2,1,0:T(8,128)(2,1)}, bf16[4,8,2,128,768]{4,3,2,1,0:T(8,128)(2,1)}, bf16[4,8,2,128,768]{4,3,2,1,0:T(8,128)(2,1)}) custom-call(bf16[8,128,768]{2,1,0:T(8,128)(2,1)S(1)} %all-to-all-done.3.u_ref.ub_ref, bf16[4,8,2,128,768]{4,3,2,1,0:T(8,128)(2,1)} %hidden_grads.1.hg_ref, ...), custom_call_target="tpu_custom_call", output_to_operand_aliasing={{1}: (3, {}), {2}: (4, {})} | custom-call | flops 9663676416 | bytes 20971520 | tf_op jit(solution)/shard_map/experts/pallas_call | solution.py:473
  254.0 14.0 %bitcast_convert_fusion = bf16[2048,768]{1,0:T(8,128)(2,1)} fusion(bf16[4,2048,768]{2,1,0:T(8,128)(2,1)} %bitcast.266, bf16[1,768,768]{2,1,0:T(8,128)(2,1)S(1)} %bitcast.292, bf16[1,768,768]{2,1,0:T(8,128)(2,1)S(1)} %bitcast.290, bf16[1,768,768]{2,1,0:T(8,128)(2,1)S(1)} %bitcast.288, bf16[1,768,768]{2,1,0:T(8,128)(2,1)S(1)} %copy-done.39), kind=kOutput, calls=%fused_computation.15 | convolution fusion | flops 9672327168 | bytes 20447232 | tf_op jit(solution)/shard_map/krf,kfd->rd/dot_general | solution.py:701
  268.1 6.0 %all-to-all-start.5 = ((bf16[8,128,768]{2,1,0:T(8,128)(2,1)}), bf16[8,128,768]{2,1,0:T(8,128)(2,1)S(1)}, u32[]{:S(2)}, u32[]{:S(2)}) async-start(bf16[8,128,768]{2,1,0:T(8,128)(2,1)} %get-tuple-element.149), calls=%async_computation.5 | async-start | bytes 3145728 | tf_op jit(solution)/shard_map/all_to_all | solution.py:504
  274.1 34.2 %expert_grads.1 = (bf16[2,768,768]{2,1,0:T(8,128)(2,1)}, bf16[2,768,768]{2,1,0:T(8,128)(2,1)}, bf16[2,768,768]{2,1,0:T(8,128)(2,1)}, bf16[2,768,768]{2,1,0:T(8,128)(2,1)}) custom-call(f32[2048,1]{1,0:T(8,128)} %copy.68.gate_ref, bf16[8,128,768]{2,1,0:T(8,128)(2,1)} %all-to-all-done.2.u_ref.ua_ref, bf16[8,128,768]{2,1,0:T(8,128)(2,1)} %copy-done.3, ...), custom_call_target="tpu_custom_call" | custom-call | flops 19327352832 | bytes 41943040 | tf_op jit(solution)/shard_map/expert_grads/pallas_call | solution.py:430
  308.4 3.5 fusion.10
  315.6 2.8 multiply_reduce_fusion
  318.5 2.8 fusion.105
  321.3 6.0 %all-to-all-start.6 = ((bf16[8,256,768]{2,1,0:T(8,128)(2,1)}), bf16[8,256,768]{2,1,0:T(8,128)(2,1)}, u32[]{:S(2)}, u32[]{:S(2)}) async-start(bf16[8,256,768]{2,1,0:T(8,128)(2,1)} %bitcast.269), calls=%async_computation.6 | async-start | bytes 6291456 | tf_op jit(solution)/shard_map/all_to_all | solution.py:504
  334.0 6.7 %collective-permute-done.16.refs_9_ = bf16[2,128,768]{2,1,0:T(8,128)(2,1)S(1)} collective-permute-done((bf16[2,128,768]{2,1,0:T(8,128)(2,1)S(1)}, bf16[2,128,768]{2,1,0:T(8,128)(2,1)S(1)}, u32[]{:S(2)}, u32[]{:S(2)}) %collective-permute-start.16) | collective-permute-done | bytes 393248 | tf_op jit(solution)/shard_map/ppermute | solution.py:500
  340.7 7.0 %collective-permute-done.17.refs_10_ = bf16[2,128,768]{2,1,0:T(8,128)(2,1)S(1)} collective-permute-done((bf16[2,128,768]{2,1,0:T(8,128)(2,1)S(1)}, bf16[2,128,768]{2,1,0:T(8,128)(2,1)S(1)}, u32[]{:S(2)}, u32[]{:S(2)}) %collective-permute-start.17) | collective-permute-done | bytes 393248 | tf_op jit(solution)/shard_map/ppermute | solution.py:500
  349.2 23.9 %attend_back.2 = (f32[2,512,768]{2,1,0:T(8,128)}, bf16[768,768]{1,0:T(8,128)(2,1)}, bf16[768,768]{1,0:T(8,128)(2,1)}, f32[2,3,8,256]{3,2,1,0:T(8,128)}) custom-call(s32[1]{0:T(128)} %bitcast.2.refs_0_, bf16[4,2,128,768]{3,2,1,0:T(8,128)(2,1)} %copy-done.4, bf16[2,2,512,576]{3,2,1,0:T(8,128)(2,1)} %get-tuple-element.161.refs_2_, ...), custom_call_target="tpu_custom_call" | custom-call | flops 12884901888 | bytes 16777216 | tf_op jit(solution)/shard_map/attend_back/pallas_call | solution.py:309
  373.2 3.4 collective-permute-done.19
  378.3 3.7 fusion.33
  383.9 24.2 %attend_back.3 = (bf16[2,128,768]{2,1,0:T(8,128)(2,1)}, bf16[2,128,768]{2,1,0:T(8,128)(2,1)}, bf16[2,128,768]{2,1,0:T(8,128)(2,1)}, bf16[2,128,768]{2,1,0:T(8,12...) custom-call(s32[1]{0:T(128)} %bitcast.2.refs_0_, ...), custom_call_target="tpu_custom_call" | custom-call | flops 12884901888 | bytes 16777216 | tf_op jit(solution)/shard_map/attend_back/pallas_call | solution.py:309
  413.8 3.1 add_convert_fusion.1
  417.0 5.6 %all-to-all-start.7 = ((bf16[8,96,768]{2,1,0:T(8,128)(2,1)}), bf16[8,96,768]{2,1,0:T(8,128)(2,1)S(1)}, u32[]{:S(2)}, u32[]{:S(2)}) async-start(bf16[8,96,768]{2,1,0:T(8,128)(2,1)} %bitcast.268), calls=%async_computation.7 | async-start | bytes 2359296 | tf_op jit(solution)/shard_map/all_to_all | solution.py:504
  430.9 3.0 collective-permute-done.30
  436.9 6.6 %collective-permute-done.31 = f32[64,128]{1,0:T(8,128)S(1)} collective-permute-done((f32[64,128]{1,0:T(8,128)S(1)}, f32[64,128]{1,0:T(8,128)S(1)}, u32[]{:S(2)}, u32[]{:S(2)}) %collective-permute-start.31) | collective-permute-done | bytes 32800 | tf_op jit(solution)/shard_map/ppermute | solution.py:533
  443.5 3.9 collective-permute-start.32
  447.4 7.4 %add_convert_fusion = bf16[1024,768]{1,0:T(8,128)(2,1)} fusion(f32[1024,768]{1,0:T(8,128)} %copy-done.17, bf16[2048,768]{1,0:T(8,128)(2,1)} %bitcast.77, s32[1024]{0:T(1024)S(1)} %copy-done.63, f32[1024]{0:T(1024)S(1)} %select_reduce_fusion), kind=kOutput, calls=%fused_computation.33 | convolution fusion | flops 3225681920 | bytes 7872512 | tf_op jit(solution)/shard_map/dot_general | solution.py:30
  460.6 3.4 collective-permute-done.26
  464.0 6.2 %collective-permute-done.27 = bf16[2,128,768]{2,1,0:T(8,128)(2,1)} collective-permute-done((bf16[2,128,768]{2,1,0:T(8,128)(2,1)}, bf16[2,128,768]{2,1,0:T(8,128)(2,1)}, u32[]{:S(2)}, u32[]{:S(2)}) %collective-permute-start.27) | collective-permute-done | bytes 393248 | tf_op jit(solution)/shard_map/ppermute | solution.py:500
  478.0 4.7 fusion.24
  482.7 3.2 fusion.32
  (326 shorter events, 98.4 us)
Async XLA Ops:
  0.6 47.9 %copy-start = (s32[8,512]{1,0:T(8,128)S(1)}, s32[8,512]{1,0:T(8,128)}, u32[]{:S(2)}) copy-start(s32[8,512]{1,0:T(8,128)} %param.18) | copy-start | bytes 49156
  2.6 11.1 %collective-permute-start = (bf16[1,96,768]{2,1,0:T(8,128)(2,1)S(1)}, bf16[1,96,768]{2,1,0:T(8,128)(2,1)S(1)}, u32[]{:S(2)}, u32[]{:S(2)}) collective-permute-start(bf16[1,96,768]{2,1,0:T(8,128)(2,1)S(1)} %bitcast.295), channel_id=1, source_target_pairs={{0,16},{4,20},{8,24},{12,28},{16,0},{20,4},{24,8},{28,12},{1,17},{... | collective-permute-start | bytes 442376 | tf_op jit(solution)/shard_map/ppermute | solution.py:520
  14.5 8.5 %collective-permute-start.1 = (bf16[2,96,768]{2,1,0:T(8,128)(2,1)}, bf16[2,96,768]{2,1,0:T(8,128)(2,1)}, u32[]{:S(2)}, u32[]{:S(2)}) collective-permute-start(bf16[2,96,768]{2,1,0:T(8,128)(2,1)} %maximum_bitcast_fusion), channel_id=1, source_target_pairs={{0,8},{4,12},{8,0},{12,4},{16,24},{20,28},{24,16},{28,20},{1,9},{5... | collective-permute-start | bytes 884744 | tf_op jit(solution)/shard_map/ppermute | solution.py:520
  16.8 23.8 %all-to-all-start = ((bf16[4,2,128,768]{3,2,1,0:T(8,128)(2,1)}), bf16[4,2,128,768]{3,2,1,0:T(8,128)(2,1)S(1)}, u32[]{:S(2)}, u32[]{:S(2)}) async-start(bf16[4,2,128,768]{3,2,1,0:T(8,128)(2,1)} %bitcast.7), calls=%async_computation | async-start | bytes 3145728 | tf_op jit(solution)/shard_map/all_to_all | solution.py:508
  24.1 13.7 %collective-permute-start.2 = (bf16[4,96,768]{2,1,0:T(8,128)(2,1)S(1)}, bf16[4,96,768]{2,1,0:T(8,128)(2,1)S(1)}, u32[]{:S(2)}, u32[]{:S(2)}) collective-permute-start(bf16[4,96,768]{2,1,0:T(8,128)(2,1)S(1)} %bitcast.271), channel_id=1, source_target_pairs={{0,4},{4,0},{8,12},{12,8},{16,20},{20,16},{24,28},{28,24},{1,5},{5... | collective-permute-start | bytes 1769480 | tf_op jit(solution)/shard_map/ppermute | solution.py:520
  41.7 83.7 %all-to-all-start.1 = ((bf16[8,256,768]{2,1,0:T(8,128)(2,1)}), bf16[8,256,768]{2,1,0:T(8,128)(2,1)S(1)}, u32[]{:S(2)}, u32[]{:S(2)}) async-start(bf16[8,256,768]{2,1,0:T(8,128)(2,1)} %bitcast.270), calls=%async_computation.1 | async-start | bytes 6291456 | tf_op jit(solution)/shard_map/all_to_all | solution.py:504
  48.5 3.3 collective-permute-start.3
  48.7 28.7 %collective-permute-start.4 = (bf16[768,768]{1,0:T(8,128)(2,1)}, bf16[768,768]{1,0:T(8,128)(2,1)}, u32[]{:S(2)}, u32[]{:S(2)}) collective-permute-start(bf16[768,768]{1,0:T(8,128)(2,1)} %bitcast.262), channel_id=1, source_target_pairs={{0,2},{1,3},{2,0},{3,1},{4,6},{5,7},{6,4},{7,5},{8,10},{9,11},{10,... | collective-permute-start | bytes 3538952 | tf_op jit(solution)/shard_map/ppermute | solution.py:500
  73.6 25.6 %copy-start.11 = (bf16[2,2,512,192]{3,2,1,0:T(8,128)(2,1)}, bf16[2,2,512,192]{3,2,1,0:T(8,128)(2,1)S(1)}, u32[]{:S(2)}) copy-start(bf16[2,2,512,192]{3,2,1,0:T(8,128)(2,1)S(1)} %get-tuple-element.130.refs_3_) | copy-start | bytes 2359300
  77.4 3.1 collective-permute-start.5
  77.4 28.4 %collective-permute-start.6 = (bf16[768,768]{1,0:T(8,128)(2,1)S(1)}, bf16[768,768]{1,0:T(8,128)(2,1)S(1)}, u32[]{:S(2)}, u32[]{:S(2)}) collective-permute-start(bf16[768,768]{1,0:T(8,128)(2,1)S(1)} %bitcast.286), channel_id=1, source_target_pairs={{0,2},{1,3},{2,0},{3,1},{4,6},{5,7},{6,4},{7,5},{8,10},{9,11},{10,... | collective-permute-start | bytes 3538952 | tf_op jit(solution)/shard_map/ppermute | solution.py:500
  105.8 3.0 collective-permute-start.7
  105.8 11.9 %collective-permute-start.8 = (bf16[2,128,768]{2,1,0:T(8,128)(2,1)S(1)}, bf16[2,128,768]{2,1,0:T(8,128)(2,1)S(1)}, u32[]{:S(2)}, u32[]{:S(2)}) collective-permute-start(bf16[2,128,768]{2,1,0:T(8,128)(2,1)S(1)} %get-tuple-element.122), channel_id=1, source_target_pairs={{0,2},{1,3},{2,0},{3,1},{4,6},{5,7},{6,4},{7,5},{8,10},{9,11},{10,... | collective-permute-start | bytes 1179656 | tf_op jit(solution)/shard_map/ppermute | solution.py:500
  107.3 18.1 %collective-permute-start.9 = (bf16[2,128,768]{2,1,0:T(8,128)(2,1)S(1)}, bf16[2,128,768]{2,1,0:T(8,128)(2,1)}, u32[]{:S(2)}, u32[]{:S(2)}) collective-permute-start(bf16[2,128,768]{2,1,0:T(8,128)(2,1)S(1)} %get-tuple-element.123), channel_id=1, source_target_pairs={{0,3},{1,2},{2,1},{3,0},{4,7},{5,6},{6,5},{7,4},{8,11},{9,10},{10,... | collective-permute-start | bytes 1179656 | tf_op jit(solution)/shard_map/ppermute | solution.py:500
  125.5 34.4 %copy-start.2 = (bf16[8,256,768]{2,1,0:T(8,128)(2,1)}, bf16[8,256,768]{2,1,0:T(8,128)(2,1)S(1)}, u32[]{:S(2)}) copy-start(bf16[8,256,768]{2,1,0:T(8,128)(2,1)S(1)} %all-to-all-done.1) | copy-start | bytes 9437188
  141.1 43.5 %all-to-all-start.2 = ((bf16[8,128,768]{2,1,0:T(8,128)(2,1)}), bf16[8,128,768]{2,1,0:T(8,128)(2,1)}, u32[]{:S(2)}, u32[]{:S(2)}) async-start(bf16[8,128,768]{2,1,0:T(8,128)(2,1)} %select_convert_fusion.1), calls=%async_computation.2 | async-start | bytes 3145728 | tf_op jit(solution)/shard_map/all_to_all | solution.py:504
  147.1 3.1 collective-permute-start.10
  147.1 4.7 collective-permute-start.11
  147.6 40.9 %collective-permute-start.12 = (bf16[768,768]{1,0:T(8,128)(2,1)}, bf16[768,768]{1,0:T(8,128)(2,1)}, u32[]{:S(2)}, u32[]{:S(2)}) collective-permute-start(bf16[768,768]{1,0:T(8,128)(2,1)} %bitcast.283), channel_id=1, source_target_pairs={{0,2},{1,3},{2,0},{3,1},{4,6},{5,7},{6,4},{7,5},{8,10},{9,11},{10,... | collective-permute-start | bytes 3538952 | tf_op jit(solution)/shard_map/ppermute | solution.py:500
  184.6 41.0 %all-to-all-start.3 = ((bf16[8,128,768]{2,1,0:T(8,128)(2,1)}), bf16[8,128,768]{2,1,0:T(8,128)(2,1)S(1)}, u32[]{:S(2)}, u32[]{:S(2)}) async-start(bf16[8,128,768]{2,1,0:T(8,128)(2,1)} %select_convert_fusion), calls=%async_computation.3 | async-start | bytes 3145728 | tf_op jit(solution)/shard_map/all_to_all | solution.py:504
  188.4 3.7 collective-permute-start.13
  188.5 4.7 collective-permute-start.14
  225.5 28.5 %copy-start.3 = (bf16[8,128,768]{2,1,0:T(8,128)(2,1)}, bf16[8,128,768]{2,1,0:T(8,128)(2,1)S(1)}, u32[]{:S(2)}) copy-start(bf16[8,128,768]{2,1,0:T(8,128)(2,1)S(1)} %all-to-all-done.3.u_ref.ub_ref) | copy-start | bytes 4718596
  225.5 42.5 %all-to-all-start.4 = ((bf16[8,128,768]{2,1,0:T(8,128)(2,1)}), bf16[8,128,768]{2,1,0:T(8,128)(2,1)S(1)}, u32[]{:S(2)}, u32[]{:S(2)}) async-start(bf16[8,128,768]{2,1,0:T(8,128)(2,1)} %get-tuple-element.143), calls=%async_computation.4 | async-start | bytes 3145728 | tf_op jit(solution)/shard_map/all_to_all | solution.py:504
  268.1 43.9 %all-to-all-start.5 = ((bf16[8,128,768]{2,1,0:T(8,128)(2,1)}), bf16[8,128,768]{2,1,0:T(8,128)(2,1)S(1)}, u32[]{:S(2)}, u32[]{:S(2)}) async-start(bf16[8,128,768]{2,1,0:T(8,128)(2,1)} %get-tuple-element.149), calls=%async_computation.5 | async-start | bytes 3145728 | tf_op jit(solution)/shard_map/all_to_all | solution.py:504
  308.3 22.1 %collective-permute-start.18 = (bf16[2,768,768]{2,1,0:T(8,128)(2,1)}, bf16[2,768,768]{2,1,0:T(8,128)(2,1)}, u32[]{:S(2)}, u32[]{:S(2)}) collective-permute-start(bf16[2,768,768]{2,1,0:T(8,128)(2,1)} %get-tuple-element.156), channel_id=1, source_target_pairs={{0,1},{1,0},{2,3},{3,2},{4,5},{5,4},{6,7},{7,6},{8,9},{9,8},{10,11... | collective-permute-start | bytes 7077896 | tf_op jit(solution)/shard_map/ppermute | solution.py:500
  321.3 89.3 %all-to-all-start.6 = ((bf16[8,256,768]{2,1,0:T(8,128)(2,1)}), bf16[8,256,768]{2,1,0:T(8,128)(2,1)}, u32[]{:S(2)}, u32[]{:S(2)}) async-start(bf16[8,256,768]{2,1,0:T(8,128)(2,1)} %bitcast.269), calls=%async_computation.6 | async-start | bytes 6291456 | tf_op jit(solution)/shard_map/all_to_all | solution.py:504
  327.3 49.4 %collective-permute-start.22 = (bf16[2,768,768]{2,1,0:T(8,128)(2,1)}, bf16[2,768,768]{2,1,0:T(8,128)(2,1)S(1)}, u32[]{:S(2)}, u32[]{:S(2)}) collective-permute-start(bf16[2,768,768]{2,1,0:T(8,128)(2,1)} %get-tuple-element.175), channel_id=1, source_target_pairs={{0,1},{1,0},{2,3},{3,2},{4,5},{5,4},{6,7},{7,6},{8,9},{9,8},{10,11... | collective-permute-start | bytes 7077896 | tf_op jit(solution)/shard_map/ppermute | solution.py:500
  328.5 5.5 %collective-permute-start.15 = (bf16[2,128,768]{2,1,0:T(8,128)(2,1)S(1)}, bf16[2,128,768]{2,1,0:T(8,128)(2,1)S(1)}, u32[]{:S(2)}, u32[]{:S(2)}) collective-permute-start(bf16[2,128,768]{2,1,0:T(8,128)(2,1)S(1)} %get-tuple-element.254), channel_id=1, source_target_pairs={{0,1},{1,0},{2,3},{3,2},{4,5},{5,4},{6,7},{7,6},{8,9},{9,8},{10,11... | collective-permute-start | bytes 1179656 | tf_op jit(solution)/shard_map/ppermute | solution.py:500
  328.8 12.0 %collective-permute-start.16 = (bf16[2,128,768]{2,1,0:T(8,128)(2,1)S(1)}, bf16[2,128,768]{2,1,0:T(8,128)(2,1)S(1)}, u32[]{:S(2)}, u32[]{:S(2)}) collective-permute-start(bf16[2,128,768]{2,1,0:T(8,128)(2,1)S(1)} %get-tuple-element.253), channel_id=1, source_target_pairs={{0,2},{1,3},{2,0},{3,1},{4,6},{5,7},{6,4},{7,5},{8,10},{9,11},{10,... | collective-permute-start | bytes 1179656 | tf_op jit(solution)/shard_map/ppermute | solution.py:500
  330.3 17.4 %collective-permute-start.17 = (bf16[2,128,768]{2,1,0:T(8,128)(2,1)S(1)}, bf16[2,128,768]{2,1,0:T(8,128)(2,1)S(1)}, u32[]{:S(2)}, u32[]{:S(2)}) collective-permute-start(bf16[2,128,768]{2,1,0:T(8,128)(2,1)S(1)} %get-tuple-element.252), channel_id=1, source_target_pairs={{0,3},{1,2},{2,1},{3,0},{4,7},{5,6},{6,5},{7,4},{8,11},{9,10},{10,... | collective-permute-start | bytes 1179656 | tf_op jit(solution)/shard_map/ppermute | solution.py:500
  347.7 28.9 %collective-permute-start.19 = (bf16[768,768]{1,0:T(8,128)(2,1)S(1)}, bf16[768,768]{1,0:T(8,128)(2,1)}, u32[]{:S(2)}, u32[]{:S(2)}) collective-permute-start(bf16[768,768]{1,0:T(8,128)(2,1)S(1)} %fusion.58), channel_id=1, source_target_pairs={{0,2},{1,3},{2,0},{3,1},{4,6},{5,7},{6,4},{7,5},{8,10},{9,11},{10,... | collective-permute-start | bytes 3538952 | tf_op jit(solution)/shard_map/ppermute | solution.py:500
  349.2 27.5 %copy-start.22 = (bf16[2,768,768]{2,1,0:T(8,128)(2,1)S(1)}, bf16[2,768,768]{2,1,0:T(8,128)(2,1)}, u32[]{:S(2)}) copy-start(bf16[2,768,768]{2,1,0:T(8,128)(2,1)} %get-tuple-element.174) | copy-start | bytes 7077892
  376.6 5.3 %collective-permute-start.20 = (bf16[768,768]{1,0:T(8,128)(2,1)}, bf16[768,768]{1,0:T(8,128)(2,1)S(1)}, u32[]{:S(2)}, u32[]{:S(2)}) collective-permute-start(bf16[768,768]{1,0:T(8,128)(2,1)} %get-tuple-element.168), channel_id=1, source_target_pairs={{0,1},{1,0},{2,3},{3,2},{4,5},{5,4},{6,7},{7,6},{8,9},{9,8},{10,11... | collective-permute-start | bytes 3538952 | tf_op jit(solution)/shard_map/ppermute | solution.py:500
  382.3 28.4 %collective-permute-start.21 = (bf16[768,768]{1,0:T(8,128)(2,1)S(1)}, bf16[768,768]{1,0:T(8,128)(2,1)S(1)}, u32[]{:S(2)}, u32[]{:S(2)}) collective-permute-start(bf16[768,768]{1,0:T(8,128)(2,1)S(1)} %add_convert_fusion.3), channel_id=1, source_target_pairs={{0,2},{1,3},{2,0},{3,1},{4,6},{5,7},{6,4},{7,5},{8,10},{9,11},{10,... | collective-permute-start | bytes 3538952 | tf_op jit(solution)/shard_map/ppermute | solution.py:500
  383.9 27.2 %copy-start.47 = (f32[2,3,8,256]{3,2,1,0:T(8,128)S(1)}, f32[2,3,8,256]{3,2,1,0:T(8,128)}, u32[]{:S(2)}) copy-start(f32[2,3,8,256]{3,2,1,0:T(8,128)} %get-tuple-element.200) | copy-start | bytes 147460
  410.6 3.2 collective-permute-start.23
  416.9 30.5 %copy-start.63 = (s32[1024]{0:T(1024)S(1)}, s32[1024]{0:T(1024)}, u32[]{:S(2)}) copy-start(s32[1024]{0:T(1024)} %copy-done.61) | copy-start | bytes 12292
  417.0 53.2 %all-to-all-start.7 = ((bf16[8,96,768]{2,1,0:T(8,128)(2,1)}), bf16[8,96,768]{2,1,0:T(8,128)(2,1)S(1)}, u32[]{:S(2)}, u32[]{:S(2)}) async-start(bf16[8,96,768]{2,1,0:T(8,128)(2,1)} %bitcast.268), calls=%async_computation.7 | async-start | bytes 2359296 | tf_op jit(solution)/shard_map/all_to_all | solution.py:504
  423.5 1.3 collective-permute-start.28
  424.8 4.0 collective-permute-start.29
  426.4 34.2 %collective-permute-start.24 = (bf16[768,768]{1,0:T(8,128)(2,1)}, bf16[768,768]{1,0:T(8,128)(2,1)}, u32[]{:S(2)}, u32[]{:S(2)}) collective-permute-start(bf16[768,768]{1,0:T(8,128)(2,1)} %fusion.59), channel_id=1, source_target_pairs={{0,2},{1,3},{2,0},{3,1},{4,6},{5,7},{6,4},{7,5},{8,10},{9,11},{10,... | collective-permute-start | bytes 3538952 | tf_op jit(solution)/shard_map/ppermute | solution.py:500
  428.8 5.1 %collective-permute-start.30 = (f32[64,128]{1,0:T(8,128)S(1)}, f32[64,128]{1,0:T(8,128)S(1)}, u32[]{:S(2)}, u32[]{:S(2)}) collective-permute-start(f32[64,128]{1,0:T(8,128)S(1)} %fusion.128), channel_id=1, source_target_pairs={{0,4},{4,0},{8,12},{12,8},{16,20},{20,16},{24,28},{28,24},{1,5},{5... | collective-permute-start | bytes 98312 | tf_op jit(solution)/shard_map/ppermute | solution.py:533
  434.0 9.5 %collective-permute-start.31 = (f32[64,128]{1,0:T(8,128)S(1)}, f32[64,128]{1,0:T(8,128)S(1)}, u32[]{:S(2)}, u32[]{:S(2)}) collective-permute-start(f32[64,128]{1,0:T(8,128)S(1)} %add.183), channel_id=1, source_target_pairs={{0,8},{4,12},{8,0},{12,4},{16,24},{20,28},{24,16},{28,20},{1,9},{5... | collective-permute-start | bytes 98312 | tf_op jit(solution)/shard_map/ppermute | solution.py:533
  435.0 25.6 %collective-permute-start.25 = (bf16[2,128,768]{2,1,0:T(8,128)(2,1)}, bf16[2,128,768]{2,1,0:T(8,128)(2,1)}, u32[]{:S(2)}, u32[]{:S(2)}) collective-permute-start(bf16[2,128,768]{2,1,0:T(8,128)(2,1)} %get-tuple-element.189), channel_id=1, source_target_pairs={{0,1},{1,0},{2,3},{3,2},{4,5},{5,4},{6,7},{7,6},{8,9},{9,8},{10,11... | collective-permute-start | bytes 1179656 | tf_op jit(solution)/shard_map/ppermute | solution.py:500
  435.0 29.0 %collective-permute-start.26 = (bf16[2,128,768]{2,1,0:T(8,128)(2,1)}, bf16[2,128,768]{2,1,0:T(8,128)(2,1)}, u32[]{:S(2)}, u32[]{:S(2)}) collective-permute-start(bf16[2,128,768]{2,1,0:T(8,128)(2,1)} %get-tuple-element.190), channel_id=1, source_target_pairs={{0,2},{1,3},{2,0},{3,1},{4,6},{5,7},{6,4},{7,5},{8,10},{9,11},{10,... | collective-permute-start | bytes 1179656 | tf_op jit(solution)/shard_map/ppermute | solution.py:500
  436.6 33.6 %collective-permute-start.27 = (bf16[2,128,768]{2,1,0:T(8,128)(2,1)}, bf16[2,128,768]{2,1,0:T(8,128)(2,1)}, u32[]{:S(2)}, u32[]{:S(2)}) collective-permute-start(bf16[2,128,768]{2,1,0:T(8,128)(2,1)} %get-tuple-element.191), channel_id=1, source_target_pairs={{0,3},{1,2},{2,1},{3,0},{4,7},{5,6},{6,5},{7,4},{8,11},{9,10},{10,... | collective-permute-start | bytes 1179656 | tf_op jit(solution)/shard_map/ppermute | solution.py:500
  443.5 11.3 %collective-permute-start.32 = (f32[64,128]{1,0:T(8,128)S(1)}, f32[64,128]{1,0:T(8,128)S(1)}, u32[]{:S(2)}, u32[]{:S(2)}) collective-permute-start(f32[64,128]{1,0:T(8,128)S(1)} %add.184), channel_id=1, source_target_pairs={{0,16},{4,20},{8,24},{12,28},{16,0},{20,4},{24,8},{28,12},{1,17},{... | collective-permute-start | bytes 98312 | tf_op jit(solution)/shard_map/ppermute | solution.py:533
  (70 other events, 476.5 us)
